TPU v7x, 1024 devices: a whole 4x4x32 slice. The times are simulated.
1024 devices in a mesh: dom: 128 (over z, x), sub: 8 (over y, core).
Axes of the slice: x: 4, y: 4, z: 32, core: 2. Of those that a mesh axis runs over, the one named last changes fastest.
Arguments:
- source_term: float32 [125, 524288], P(None, ('dom', 'sub')), may hold values from -20 to 20
- cell_levels: int32 [524288], P(('dom', 'sub')), may hold values from 0 to 2
- coefficient_ids: int32 [524288], P(('dom', 'sub')), may hold values from 0 to 63
- coefficient_values: float32 [64], replicated, may hold values from 0.3 to 3
- conforming_pairs: int32 [2, 983040], P(None, ('dom', 'sub')), may hold values from -1 to 3839, as said below
- hanging_coarse: int32 [524288], P(('dom', 'sub')), may hold values from -1 to 3071, as said below
- hanging_fine: int32 [4, 524288], P(None, ('dom', 'sub')), may hold values from -1 to 3071, as said below
Outputs:
- solution_field: float32 [125, 524288], P(None, ('dom', 'sub'))
- residual: float32 [125, 524288], P(None, ('dom', 'sub'))
Inputs may be any that keep to these rules, and one draw needn't show every extreme that they name: `conforming_pairs`: every used pair lists its face and the opposite face (f + 3 mod 6) of a cell in the same block or within 64 cells of the block boundary in the neighbouring block; each pair appears also from the other side; entries with a -1 have -1 in both rows. `hanging_coarse`: A slot is used exactly when all four children of the matching slot in the block one step further along dom are used; the blocks with the last dom index have no used slots. `hanging_fine`: blocks with dom index 0 have no used slots; a used slot has four used children.
All inputs are finite; a program needn't handle non-finite values.
Results may differ from a plain program's by a relative error of at most 0.0033.
Values sent between devices are 32-bit elements; how exact they have to be, the bound alone decides.
No kernel may reach another device: no remote copies, remote signals or barrier semaphores. Data moves between devices by JAX's collectives and lax.ppermute only.
A program may use at most 32 MiB of HBM per device.

v0:
```python
import jax
import jax.numpy as jnp
import numpy as np
from jax import lax
from jax.sharding import PartitionSpec as P

RIM = 64
ITERS = 2


TAU_PENALTY = 2.0
SIGMA_MASS = 4.0
HIGHEST = lax.Precision.HIGHEST


def extended_2(block, sides, width):
    for axis, dim in sides:
        count = lax.axis_size(axis)
        forward = [(i, i + 1) for i in range(count - 1)]
        backward = [(target, source) for source, target in forward]
        low = lax.ppermute(
            lax.slice_in_dim(block, block.shape[dim] - width, None, axis=dim), axis, forward
        )
        high = lax.ppermute(lax.slice_in_dim(block, 0, width, axis=dim), axis, backward)
        block = jnp.concatenate([low, block, high], axis=dim)
    return block


def passed_along(block, axis, distance):
    devices = range(lax.axis_size(axis))
    route = [(i - distance, i) for i in devices if i - distance in devices]
    return lax.ppermute(block, axis, route)


def element_tables():
    points = np.array([-1.0, -np.sqrt(3.0 / 7.0), 0.0, np.sqrt(3.0 / 7.0), 1.0])
    weights = np.array([0.1, 49.0 / 90.0, 32.0 / 45.0, 49.0 / 90.0, 0.1])

    def lagrange(location):
        values = np.ones((location.shape[0], 5))
        for column in range(5):
            for other in range(5):
                if other != column:
                    values[:, column] *= (location - points[other]) / (
                        points[column] - points[other]
                    )
        return values

    derivative = np.zeros((5, 5))
    for column in range(5):
        for other in range(5):
            if other != column:
                product = np.ones(5) / (points[column] - points[other])
                for remaining in range(5):
                    if remaining != column and remaining != other:
                        product = (
                            product
                            * (points - points[remaining])
                            / (points[column] - points[remaining])
                        )
                derivative[:, column] += product
    stiffness = derivative.T @ (weights[:, None] * derivative)
    halves = [lagrange((points - 1.0) / 2.0), lagrange((points + 1.0) / 2.0)]
    interp = np.stack(
        [
            np.kron(halves[first_half], halves[second_half])
            for first_half in range(2)
            for second_half in range(2)
        ]
    )
    return (
        jnp.asarray(stiffness, jnp.float32),
        jnp.asarray(weights, jnp.float32),
        jnp.asarray(interp, jnp.float32),
    )


def local_apply(nodal_cube, coefficient, cell_scale, stiffness, weights):
    weight_x = weights[:, None, None, None]
    weight_y = weights[None, :, None, None]
    weight_z = weights[None, None, :, None]
    along_x = (
        jnp.einsum("ai,ijkc->ajkc", stiffness, nodal_cube, precision=HIGHEST) * weight_y * weight_z
    )
    along_y = (
        jnp.einsum("bj,ijkc->ibkc", stiffness, nodal_cube, precision=HIGHEST) * weight_x * weight_z
    )
    along_z = (
        jnp.einsum("dk,ijkc->ijdc", stiffness, nodal_cube, precision=HIGHEST) * weight_x * weight_y
    )
    lumped = SIGMA_MASS * weight_x * weight_y * weight_z * (cell_scale * cell_scale * cell_scale)
    return coefficient * cell_scale * (along_x + along_y + along_z) + lumped * nodal_cube


def face_traces(nodal_cube):
    cell_count = nodal_cube.shape[3]
    slabs = [
        nodal_cube[0],
        nodal_cube[:, 0],
        nodal_cube[:, :, 0],
        nodal_cube[4],
        nodal_cube[:, 4],
        nodal_cube[:, :, 4],
    ]
    return jnp.stack([face_slab.reshape(25, cell_count) for face_slab in slabs], axis=1)


def add_faces(nodal_cube, contribution):
    cell_count = nodal_cube.shape[3]
    pieces = contribution.reshape(5, 5, 6, cell_count)
    nodal_cube = nodal_cube.at[0].add(pieces[:, :, 0])
    nodal_cube = nodal_cube.at[:, 0].add(pieces[:, :, 1])
    nodal_cube = nodal_cube.at[:, :, 0].add(pieces[:, :, 2])
    nodal_cube = nodal_cube.at[4].add(pieces[:, :, 3])
    nodal_cube = nodal_cube.at[:, 4].add(pieces[:, :, 4])
    nodal_cube = nodal_cube.at[:, :, 4].add(pieces[:, :, 5])
    return nodal_cube.reshape(125, cell_count)


def operate(
    vector, coefficient, cell_scale, conforming_pairs, hanging_coarse, hanging_fine, tables
):
    stiffness, weights, interp = tables
    cell_count = vector.shape[1]
    nodal_cube = vector.reshape(5, 5, 5, cell_count)
    applied = local_apply(nodal_cube, coefficient, cell_scale, stiffness, weights)
    local_traces = face_traces(nodal_cube)
    extended = extended_2(local_traces, ((("dom", "sub"), 2),), RIM)
    flat_local = local_traces.reshape(25, 6 * cell_count)
    flat_ext = extended.reshape(25, -1)
    pair_live = (conforming_pairs[0] >= 0).astype(jnp.float32)
    first_safe = jnp.maximum(conforming_pairs[0], 0)
    second_safe = jnp.maximum(conforming_pairs[1], 0)
    face_jump = TAU_PENALTY * (flat_local[:, first_safe] - flat_ext[:, second_safe]) * pair_live
    contribution = jnp.zeros_like(flat_local).at[:, first_safe].add(face_jump)
    coarse_live = (hanging_coarse >= 0).astype(jnp.float32)
    coarse_safe = jnp.maximum(hanging_coarse, 0)
    coarse_values = flat_local[:, coarse_safe] * coarse_live
    fine_live = (hanging_fine >= 0).astype(jnp.float32)
    fine_safe = jnp.maximum(hanging_fine, 0)
    fine_values = flat_local[:, fine_safe] * fine_live
    arriving = passed_along(coarse_values, "dom", 1)
    predicted = jnp.einsum("sij,jh->ish", interp, arriving, precision=HIGHEST)
    fine_jump = TAU_PENALTY * (fine_values - predicted) * fine_live
    contribution = contribution.at[:, fine_safe.reshape(-1)].add(fine_jump.reshape(25, -1))
    returned = -jnp.einsum("sji,jsh->ih", interp, fine_jump, precision=HIGHEST)
    going_back = passed_along(returned, "dom", -1)
    contribution = contribution.at[:, coarse_safe].add(going_back * coarse_live)
    return add_faces(applied, contribution.reshape(25, 6, cell_count))


def squares_total(residual):
    return lax.psum(jnp.sum(residual * residual), ("dom", "sub"))


def on_device(
    source_term,
    cell_levels,
    coefficient_ids,
    coefficient_values,
    conforming_pairs,
    hanging_coarse,
    hanging_fine,
):
    tables = element_tables()
    lookup = (
        coefficient_ids[None, :]
        == jnp.arange(coefficient_values.shape[0], dtype=jnp.int32)[:, None]
    ).astype(jnp.float32)
    coefficient = jnp.dot(coefficient_values[None, :], lookup, precision=HIGHEST)[0]
    cell_scale = jnp.exp2(-cell_levels.astype(jnp.float32))
    solution_field = jnp.zeros_like(source_term)
    residual = source_term
    direction = source_term
    norm_now = squares_total(residual)
    for iteration in range(ITERS):
        image = operate(
            direction,
            coefficient,
            cell_scale,
            conforming_pairs,
            hanging_coarse,
            hanging_fine,
            tables,
        )
        alpha = norm_now / lax.psum(jnp.sum(direction * image), ("dom", "sub"))
        solution_field = solution_field + alpha * direction
        residual = residual - alpha * image
        if iteration + 1 < ITERS:
            norm_next = squares_total(residual)
            direction = residual + norm_next / norm_now * direction
            norm_now = norm_next
    return (solution_field, residual)


def solution(mesh):
    placed = (
        P(None, ("dom", "sub")),
        P(("dom", "sub")),
        P(("dom", "sub")),
        P(),
        P(None, ("dom", "sub")),
        P(("dom", "sub")),
        P(None, ("dom", "sub")),
    )
    return jax.shard_map(
        on_device,
        mesh=mesh,
        in_specs=placed,
        out_specs=(P(None, ("dom", "sub")), P(None, ("dom", "sub"))),
        check_vma=False,
    )
```

profile of v0, /device:TPU:1, one launch (start us, length us, event | category | flops | bytes accessed | tf_op | source)
XLA Modules:
  0.0 642.7 jit_solution(3843070077126926662)
XLA Ops:
  4.2 16.2 %collective-permute-start.1 = (f32[25,6,64]{2,1,0:T(8,128)}, f32[25,6,64]{2,1,0:T(8,128)S(1)}, u32[]{:S(2)}, u32[]{:S(2)}) collective-permute-start(f32[25,6,64]{2,1,0:T(8,128)} %get-tuple-element.165), channel_id=1, source_target_pairs={{1,0},{2,1},{3,2},{4,3},{5,4},{6,5},{7,6},{8,7},{9,8},{10,9},{11,1... | collective-permute-start | bytes 115208 | tf_op jit(solution)/shard_map/ppermute | solution.py:24
  20.4 1.9 collective-permute-start
  27.1 1.8 fusion.4
  28.9 7.6 %gather_fusion = f32[2048,25]{1,0:T(8,128)} fusion(f32[25,3072]{0,1:T(8,128)S(1)} %bitcast.156, s32[2048]{0:T(1024)S(1)} %broadcast_clamp_fusion), kind=kCustom, calls=%fused_computation.2 | custom fusion | bytes 417792 | tf_op jit(solution)/shard_map/gather | solution.py:141
  36.4 1.6 copy.57
  42.3 2.0 copy.55
  44.3 17.2 %scatter_custom_fusion = f32[25,3072]{0,1:T(8,128)S(1)} fusion(s32[960]{0:T(1024)} %bitcast.181, f32[]{:T(128)} %constant.303.clone.1, f32[960]{0:T(1024)S(1)} %bitcast.175, f32[25,3840]{0,1:T(8,128)} %bitcast.162, s32[1024]{0:T(1024)S(1)} %get-tuple-element.183, f32[25,3072]{0,1:T(8,128)S(1)} %bitcast.157, s32[1024]{0:T(1024)S(1)} %pad_clamp_fusion.2), kind=kCustom, calls=%fused_computation.40 | custom fusion | flops 72000 | bytes 2593024 | tf_op jit(solution)/shard_map/scatter-add | solution.py:135
  62.1 15.3 %scatter_fusion = f32[25,3072]{0,1:T(8,128)S(1)} fusion(f32[25,3072]{0,1:T(8,128)S(1)} %scatter_custom_fusion, s32[2048]{0:T(1024)S(1)} %bitcast.173, f32[2048,25]{1,0:T(8,128)S(1)} %copy.60), kind=kCustom, calls=%fused_computation.9 | custom fusion | flops 51200 | bytes 622592 | tf_op jit(solution)/shard_map/scatter-add | solution.py:145
  78.4 4.3 scatter_fusion.1
  86.6 166.2 %all-reduce = (f32[]{:T(128)}, f32[]{:T(128)}) all-reduce(f32[]{:T(128)} %get-tuple-element.147, f32[]{:T(128)} %get-tuple-element.146), channel_id=1, replica_groups=mesh['dom'=128,'sub'=8] {'dom','sub'}, use_global_device_ids=true, to_apply=%region_1.0 | all-reduce | flops 2 | bytes 16 | tf_op jit(solution)/shard_map/psum | solution.py:153
  254.7 151.4 %psum.30 = f32[]{:T(128)} all-reduce(f32[]{:T(128)} %multiply_reduce_fusion.1), channel_id=1, replica_groups=mesh['dom'=128,'sub'=8] {'dom','sub'}, use_global_device_ids=true, to_apply=%region_8.0 | all-reduce | flops 1 | bytes 8 | tf_op jit(solution)/shard_map/psum | solution.py:153
  407.5 1.4 convolution_multiply_fusion.2
  410.9 2.5 fusion.7
  413.4 2.6 collective-permute-start.5
  416.0 3.0 collective-permute-start.4
  420.2 3.1 collective-permute-start.6
  423.3 2.2 fusion.24
  425.6 7.6 %gather_fusion.2 = f32[2048,25]{1,0:T(8,128)} fusion(f32[25,3072]{0,1:T(8,128)S(1)} %bitcast.159, s32[2048]{0:T(1024)S(1)} %broadcast_clamp_fusion), kind=kCustom, calls=%fused_computation.6 | custom fusion | bytes 417792 | tf_op jit(solution)/shard_map/gather | solution.py:141
  433.1 1.6 copy.86
  438.5 1.9 copy.84
  440.4 17.0 %scatter_custom_fusion.3 = f32[25,3072]{0,1:T(8,128)S(1)} fusion(s32[960]{0:T(1024)} %bitcast.182, f32[]{:T(128)} %constant.303.clone.1, f32[960]{0:T(1024)S(1)} %bitcast.176, f32[25,3840]{0,1:T(8,128)} %bitcast.161, s32[1024]{0:T(1024)S(1)} %get-tuple-element.183, f32[25,3072]{0,1:T(8,128)S(1)} %bitcast.160, s32[1024]{0:T(1024)S(1)} %pad_clamp_fusion.2), kind=kCustom, calls=%fused_computation.38 | custom fusion | flops 72000 | bytes 2593024 | tf_op jit(solution)/shard_map/scatter-add | solution.py:135
  459.0 15.3 %scatter_fusion.2 = f32[25,3072]{0,1:T(8,128)S(1)} fusion(f32[25,3072]{0,1:T(8,128)S(1)} %scatter_custom_fusion.3, s32[2048]{0:T(1024)S(1)} %bitcast.174, f32[2048,25]{1,0:T(8,128)S(1)} %copy.89), kind=kCustom, calls=%fused_computation.12 | custom fusion | flops 51200 | bytes 622592 | tf_op jit(solution)/shard_map/scatter-add | solution.py:145
  474.5 4.5 scatter_fusion.3
  482.9 157.2 %psum.31 = f32[]{:T(128)} all-reduce(f32[]{:T(128)} %multiply_reduce_fusion), channel_id=1, replica_groups=mesh['dom'=128,'sub'=8] {'dom','sub'}, use_global_device_ids=true, to_apply=%region_13.0 | all-reduce | flops 1 | bytes 8 | tf_op jit(solution)/shard_map/psum | solution.py:186
  (168 shorter events, 31.4 us)
Async XLA Ops:
  0.6 26.2 %copy-start = (f32[64]{0:T(128)S(1)}, f32[64]{0:T(128)}, u32[]{:S(2)}) copy-start(f32[64]{0:T(128)} %param.37) | copy-start | bytes 772
  2.9 20.0 %copy-start.25 = (s32[512]{0:T(512)S(1)}, s32[512]{0:T(512)}, u32[]{:S(2)}) copy-start(s32[512]{0:T(512)} %param.39) | copy-start | bytes 6148
  2.9 20.1 %copy-start.21 = (s32[2,960]{1,0:T(2,128)S(1)}, s32[2,960]{1,0:T(2,128)}, u32[]{:S(2)}) copy-start(s32[2,960]{1,0:T(2,128)} %param.38) | copy-start | bytes 23044
  4.2 21.3 %copy-start.13 = (f32[5,5,1,1]{1,0,3,2:T(8,128)S(1)}, f32[5,5,1,1]{1,0,3,2:T(8,128)}, u32[]{:S(2)}) copy-start(f32[5,5,1,1]{1,0,3,2:T(8,128)} %constant.320) | copy-start | bytes 304
  4.2 37.9 %collective-permute-start.1 = (f32[25,6,64]{2,1,0:T(8,128)}, f32[25,6,64]{2,1,0:T(8,128)S(1)}, u32[]{:S(2)}, u32[]{:S(2)}) collective-permute-start(f32[25,6,64]{2,1,0:T(8,128)} %get-tuple-element.165), channel_id=1, source_target_pairs={{1,0},{2,1},{3,2},{4,3},{5,4},{6,5},{7,6},{8,7},{9,8},{10,9},{11,1... | collective-permute-start | bytes 115208 | tf_op jit(solution)/shard_map/ppermute | solution.py:24
  20.4 21.7 %collective-permute-start = (f32[25,6,64]{2,1,0:T(8,128)S(1)}, f32[25,6,64]{2,1,0:T(8,128)S(1)}, u32[]{:S(2)}, u32[]{:S(2)}) collective-permute-start(f32[25,6,64]{2,1,0:T(8,128)S(1)} %get-tuple-element.164), channel_id=1, source_target_pairs={{0,1},{1,2},{2,3},{3,4},{4,5},{5,6},{6,7},{7,8},{8,9},{9,10},{10,1... | collective-permute-start | bytes 115208 | tf_op jit(solution)/shard_map/ppermute | solution.py:21
  22.9 55.5 %copy-start.14 = (s32[512]{0:T(512)}, s32[512]{0:T(512)S(1)}, u32[]{:S(2)}) copy-start(s32[512]{0:T(512)S(1)} %broadcast_maximum_fusion) | copy-start | bytes 6148
  23.0 5.9 copy-start.24
  24.2 13.8 %collective-permute-start.2 = (f32[25,512]{1,0:T(8,128)S(1)}, f32[25,512]{1,0:T(8,128)S(1)}, u32[]{:S(2)}, u32[]{:S(2)}) collective-permute-start(f32[25,512]{1,0:T(8,128)S(1)} %multiply_bitcast_fusion.1), channel_id=1, source_target_pairs={{0,8},{8,16},{16,24},{24,32},{32,40},{40,48},{48,56},{56,64},{64,7... | collective-permute-start | bytes 153608 | tf_op jit(solution)/shard_map/ppermute | solution.py:32
  27.1 9.4 %copy-start.17 = (f32[512]{0:T(512)}, f32[512]{0:T(512)S(1)}, u32[]{:S(2)}) copy-start(f32[512]{0:T(512)S(1)} %get-tuple-element.180) | copy-start | bytes 6148
  27.1 9.4 %copy-start.19 = (f32[512]{0:T(512)}, f32[512]{0:T(512)S(1)}, u32[]{:S(2)}) copy-start(f32[512]{0:T(512)S(1)} %get-tuple-element.181) | copy-start | bytes 6148
  28.9 9.8 %copy-start.9 = (f32[4,25,25]{2,1,0:T(8,128)S(1)}, f32[4,25,25]{2,1,0:T(8,128)}, u32[]{:S(2)}) copy-start(f32[4,25,25]{2,1,0:T(8,128)} %constant.312.clone) | copy-start | bytes 30004
  40.8 36.6 %collective-permute-start.3 = (f32[25,512]{1,0:T(8,128)}, f32[25,512]{1,0:T(8,128)}, u32[]{:S(2)}, u32[]{:S(2)}) collective-permute-start(f32[25,512]{1,0:T(8,128)} %fusion.15), channel_id=1, source_target_pairs={{8,0},{16,8},{24,16},{32,24},{40,32},{48,40},{56,48},{64,56},{72,6... | collective-permute-start | bytes 153608 | tf_op jit(solution)/shard_map/ppermute | solution.py:32
  85.8 321.8 %copy-start.12 = (f32[5,5,1,1]{1,0,2,3:T(8,128)S(1)}, f32[5,5,1,1]{1,0,2,3:T(8,128)}, u32[]{:S(2)}) copy-start(f32[5,5,1,1]{1,0,2,3:T(8,128)} %constant.321) | copy-start | bytes 304
  85.9 321.5 %copy-start.2 = (f32[125,512]{1,0:T(8,128)}, f32[125,512]{1,0:T(8,128)S(1)}, u32[]{:S(2)}) copy-start(f32[125,512]{1,0:T(8,128)S(1)} %reshape.562) | copy-start | bytes 768004
  410.4 8.6 %copy-start.23 = (s32[1024]{0:T(1024)S(1)}, s32[1024]{0:T(1024)}, u32[]{:S(2)}) copy-start(s32[1024]{0:T(1024)} %copy-done.22) | copy-start | bytes 12292
  410.9 12.4 %copy-start.18 = (f32[512]{0:T(512)S(1)}, f32[512]{0:T(512)}, u32[]{:S(2)}) copy-start(f32[512]{0:T(512)} %copy-done.17) | copy-start | bytes 6148
  410.9 12.4 %copy-start.20 = (f32[512]{0:T(512)S(1)}, f32[512]{0:T(512)}, u32[]{:S(2)}) copy-start(f32[512]{0:T(512)} %copy-done.19) | copy-start | bytes 6148
  413.4 23.9 %collective-permute-start.5 = (f32[25,6,64]{2,0,1:T(8,128)}, f32[25,6,64]{2,0,1:T(8,128)}, u32[]{:S(2)}, u32[]{:S(2)}) collective-permute-start(f32[25,6,64]{2,0,1:T(8,128)} %get-tuple-element.171), channel_id=1, source_target_pairs={{1,0},{2,1},{3,2},{4,3},{5,4},{6,5},{7,6},{8,7},{9,8},{10,9},{11,1... | collective-permute-start | bytes 115208 | tf_op jit(solution)/shard_map/ppermute | solution.py:24
  416.0 21.3 %collective-permute-start.4 = (f32[25,6,64]{2,0,1:T(8,128)}, f32[25,6,64]{2,0,1:T(8,128)}, u32[]{:S(2)}, u32[]{:S(2)}) collective-permute-start(f32[25,6,64]{2,0,1:T(8,128)} %get-tuple-element.170), channel_id=1, source_target_pairs={{0,1},{1,2},{2,3},{3,4},{4,5},{5,6},{6,7},{7,8},{8,9},{9,10},{10,1... | collective-permute-start | bytes 115208 | tf_op jit(solution)/shard_map/ppermute | solution.py:21
  420.2 14.5 %collective-permute-start.6 = (f32[25,512]{1,0:T(8,128)S(1)}, f32[25,512]{1,0:T(8,128)S(1)}, u32[]{:S(2)}, u32[]{:S(2)}) collective-permute-start(f32[25,512]{1,0:T(8,128)S(1)} %multiply_bitcast_fusion), channel_id=1, source_target_pairs={{0,8},{8,16},{16,24},{24,32},{32,40},{40,48},{48,56},{56,64},{64,7... | collective-permute-start | bytes 153608 | tf_op jit(solution)/shard_map/ppermute | solution.py:32
  436.0 38.3 %collective-permute-start.7 = (f32[25,512]{1,0:T(8,128)}, f32[25,512]{1,0:T(8,128)S(1)}, u32[]{:S(2)}, u32[]{:S(2)}) collective-permute-start(f32[25,512]{1,0:T(8,128)} %fusion.13), channel_id=1, source_target_pairs={{8,0},{16,8},{24,16},{32,24},{40,32},{48,40},{56,48},{64,56},{72,6... | collective-permute-start | bytes 153608 | tf_op jit(solution)/shard_map/ppermute | solution.py:32
  459.0 15.5 %copy-start.15 = (s32[512]{0:T(512)S(1)}, s32[512]{0:T(512)}, u32[]{:S(2)}) copy-start(s32[512]{0:T(512)} %copy-done.14) | copy-start | bytes 6148
  480.9 160.5 %copy-start.3 = (f32[125,512]{1,0:T(8,128)S(1)}, f32[125,512]{1,0:T(8,128)}, u32[]{:S(2)}) copy-start(f32[125,512]{1,0:T(8,128)} %copy-done.2) | copy-start | bytes 768004
  (13 other events, 38.3 us)
where the time goes:
time: 651 us; the launch traced here: 643 us
  blocking collectives  475 us (73%)
  other arithmetic  81.8 us (13%)
  local copies, waits for them, and re-layouts  38.6 us (6%)
  starting transfers between devices  30.6 us (5%)
  matrix products  10.8 us (2%)
    psum x2, blocking collectives, squares_total(): return lax.psum(jnp.sum(residual * residual), ('dom', 'sub'))  318 us
    psum x1, blocking collectives, on_device(): alpha = norm_now / lax.psum(jnp.sum(direction * image), ('dom', 'sub'))  157 us
    scatter-add x2, other arithmetic, operate(): contribution = jnp.zeros_like(flat_local).at[:, first_safe].add(face_jump)  34.2 us
    scatter-add x2, other arithmetic, operate(): contribution.at[:, fine_safe.reshape(-1)].add(fine_jump.reshape(25, -1))  30.6 us
    ppermute x2, starting transfers between devices, extended_2(): lax.ppermute(lax.slice_in_dim(block, 0, width, axis=dim), axis, backward)  18.7 us
    gather x4, local copies, waits for them, and re-layouts, operate(): fine_values = flat_local[:, fine_safe] * fine_live  18.2 us
  transfers between devices with their start and end apart: 8, of which 0 were waited for; matrix products, arithmetic and copies ran while one was open for 16% of the time, Pallas kernels for 0%

commit v1 on v0

v1 whole, which is shorter than its diff:
```python
import jax
import jax.numpy as jnp
import numpy as np
import ml_dtypes
from jax import lax
from jax.experimental import pallas as pl
from jax.experimental.pallas import tpu as pltpu
from jax.sharding import Mesh, PartitionSpec as P

CELLS = 512
RIM = 64
EXTENT = CELLS + 2 * RIM
PAIRS = 960
PAIR_SLOTS = 1024
SIDE = 128
FACE = 32
TRACE = 6 * FACE
FINE0 = PAIR_SLOTS
COARSE0 = PAIR_SLOTS + 4 * CELLS
SLOTS = COARSE0 + CELLS
CHUNK = 512
TAU_PENALTY = 2.0
SIGMA_MASS = 4.0
F32 = jnp.float32
BF16 = jnp.bfloat16
ALONG_ROWS = (((1,), (0,)), ((), ()))
ALONG_LANES = (((1,), (1,)), ((), ()))


def element_tables():
    points = np.array([-1.0, -np.sqrt(3.0 / 7.0), 0.0, np.sqrt(3.0 / 7.0), 1.0])
    weights = np.array([0.1, 49.0 / 90.0, 32.0 / 45.0, 49.0 / 90.0, 0.1])

    def lagrange(location):
        values = np.ones((location.shape[0], 5))
        for column in range(5):
            for other in range(5):
                if other != column:
                    values[:, column] *= (location - points[other]) / (
                        points[column] - points[other]
                    )
        return values

    derivative = np.zeros((5, 5))
    for column in range(5):
        for other in range(5):
            if other != column:
                product = np.ones(5) / (points[column] - points[other])
                for remaining in range(5):
                    if remaining != column and remaining != other:
                        product = (
                            product
                            * (points - points[remaining])
                            / (points[column] - points[remaining])
                        )
                derivative[:, column] += product
    stiffness = derivative.T @ (weights[:, None] * derivative)
    halves = [lagrange((points - 1.0) / 2.0), lagrange((points + 1.0) / 2.0)]
    interp = [np.kron(halves[a], halves[b]) for a in range(2) for b in range(2)]
    return stiffness, weights, interp


def two_parts(table):
    high = table.astype(np.float32).astype(ml_dtypes.bfloat16)
    low = (table - high.astype(np.float64)).astype(np.float32).astype(ml_dtypes.bfloat16)
    return high, low


def constant_tables():
    stiffness, weights, interp = element_tables()
    diag = np.diag(weights)

    def kron3(a, b, c):
        return np.kron(np.kron(a, b), c)

    local = np.zeros((128, 128))
    local[:125, :125] = (
        kron3(stiffness, diag, diag) + kron3(diag, stiffness, diag) + kron3(diag, diag, stiffness)
    )
    lumped = np.zeros((128, 1), np.float32)
    lumped[:125, 0] = SIGMA_MASS * np.einsum("i,j,k->ijk", weights, weights, weights).reshape(-1)
    node = np.arange(125).reshape(5, 5, 5)
    slabs = [node[0], node[:, 0], node[:, :, 0], node[4], node[:, 4], node[:, :, 4]]
    trace = np.zeros((TRACE, 128))
    for face, slab in enumerate(slabs):
        trace[face * FACE + np.arange(25), slab.reshape(-1)] = 1.0
    coarse = np.zeros((FACE, FACE))
    down = np.zeros((4 * FACE, FACE))
    for child, matrix in enumerate(interp):
        coarse[:25, :25] += matrix.T @ matrix
        down[child * FACE : child * FACE + 25, :25] = matrix
    return {
        "trace": trace.astype(ml_dtypes.bfloat16),
        "untrace": np.ascontiguousarray(trace.T).astype(ml_dtypes.bfloat16),
        "local": two_parts(local),
        "lumped": lumped,
        "coarse": two_parts(np.kron(np.eye(6), TAU_PENALTY * coarse)),
        "down": two_parts(-TAU_PENALTY * down),
        "up": two_parts(-TAU_PENALTY * np.ascontiguousarray(down.T)),
    }


def dot(a, b, dims=ALONG_ROWS):
    return lax.dot_general(a, b, dims, preferred_element_type=F32)


def split(value):
    high = value.astype(BF16)
    return high, (value - high.astype(F32)).astype(BF16)


def table_dot(high_ref, low_ref, value):
    high, low = split(value)
    table = high_ref[...]
    return dot(table, high) + dot(table, low) + dot(low_ref[...], high)


def face_traces(trace_ref, field):
    high, low = split(field)
    table = trace_ref[...]
    return dot(table, high), dot(table, low)


def one_hot(cell, rows):
    place = lax.broadcasted_iota(jnp.int32, (rows, cell.shape[1]), 0)
    return jnp.where(place == cell, 1.0, 0.0).astype(BF16)


def pick(gathered, face):
    total = None
    for f in range(6):
        both = gathered[f * FACE : (f + 1) * FACE] + gathered[TRACE + f * FACE : TRACE + (f + 1) * FACE]
        term = jnp.where(face == f, both, 0.0)
        total = term if total is None else total + term
    return total


def own_code(code):
    return code >> 9, code & (CELLS - 1)


def extended_code(code):
    face = jnp.where(code < 0, -1, 0)
    for f in range(1, 6):
        face = face + jnp.where(code >= f * EXTENT, 1, 0)
    return face, code - face * EXTENT - RIM


def padded_pairs(pairs_ref, codes):
    codes[...] = jnp.full_like(codes, -1)
    codes[0:2, 0:PAIRS] = pairs_ref[...]


def padded_field(field_ref, field):
    if field_ref.shape[0] == 128:
        return field_ref[...]
    field[...] = jnp.zeros_like(field)
    field[0:125, :] = field_ref[...]
    return field[...]


def gather_hanging(traces, hot, coarse_ref, fine_ref, up):
    rows = []
    for child in range(4):
        face, _ = own_code(fine_ref[child : child + 1, :])
        start = FINE0 + child * CELLS
        rows.append(pick(dot(traces, hot[:, start : start + CELLS]), face))
    face, _ = own_code(coarse_ref[...])
    send_coarse = pick(dot(traces, hot[:, COARSE0:SLOTS]), face)
    send_fine = table_dot(up[0], up[1], jnp.concatenate(rows, axis=0))
    return send_coarse, send_fine


def hot_hanging(hot, coarse_ref, fine_ref):
    for child in range(4):
        _, cell = own_code(fine_ref[child : child + 1, :])
        start = FINE0 + child * CELLS
        hot[:, start : start + CELLS] = one_hot(cell, CELLS)
    _, cell = own_code(coarse_ref[...])
    hot[:, COARSE0:SLOTS] = one_hot(cell, CELLS)


def stacked_traces(trace_ref, field):
    high, low = face_traces(trace_ref, field)
    return jnp.concatenate([high.astype(BF16), low.astype(BF16)], axis=0)


def first_kernel(
    field_ref, coarse_ref, fine_ref, trace_ref, uph_ref, upl_ref, send_coarse_ref, send_fine_ref, field, hot
):
    hot_hanging(hot, coarse_ref, fine_ref)
    traces = stacked_traces(trace_ref, padded_field(field_ref, field))
    send_coarse, send_fine = gather_hanging(traces, hot, coarse_ref, fine_ref, (uph_ref, upl_ref))
    send_coarse_ref[...] = send_coarse
    send_fine_ref[...] = send_fine


def middle_kernel(
    field_ref,
    pairs_ref,
    level_ref,
    id_ref,
    values_ref,
    trace_ref,
    lh_ref,
    ll_ref,
    lumped_ref,
    mh_ref,
    ml_ref,
    applied_ref,
    trace_out_ref,
    coarse_out_ref,
    partner_ref,
    field,
    codes,
):
    vector = padded_field(field_ref, field)
    padded_pairs(pairs_ref, codes)
    high, low = face_traces(trace_ref, vector)
    both = high + low
    trace_out_ref[...] = both
    coarse_out_ref[...] = table_dot(mh_ref, ml_ref, both)
    traces = jnp.concatenate([high.astype(BF16), low.astype(BF16)], axis=0)
    for start in range(0, PAIR_SLOTS, CHUNK):
        face, cell = extended_code(codes[1:2, start : start + CHUNK])
        partner_ref[:, start : start + CHUNK] = pick(dot(traces, one_hot(cell, CELLS)), face)
    place = lax.broadcasted_iota(jnp.int32, (values_ref.shape[1], CELLS), 0)
    lookup = jnp.where(place == id_ref[...], 1.0, 0.0)
    values = jnp.broadcast_to(values_ref[...], (8, values_ref.shape[1]))
    coefficient = lax.dot_general(
        values, lookup, ALONG_ROWS, precision=lax.Precision.HIGHEST, preferred_element_type=F32
    )[0:1]
    level = level_ref[...]
    scale = jnp.where(level == 0, 1.0, jnp.where(level == 1, 0.5, 0.25))
    stiff = table_dot(lh_ref, ll_ref, vector)
    cubed = scale * scale * scale
    applied_ref[...] = (coefficient * scale) * stiff + cubed * (lumped_ref[...] * vector)


def add_faces(
    pairs_ref,
    coarse_ref,
    fine_ref,
    applied_ref,
    trace_in_ref,
    coarse_in_ref,
    partner_ref,
    below_ref,
    above_ref,
    arriving_ref,
    returned_ref,
    trace_ref,
    untrace_ref,
    dh_ref,
    dl_ref,
    codes,
    sides,
    hot,
    spread,
):
    padded_pairs(pairs_ref, codes)
    hot_hanging(hot, coarse_ref, fine_ref)
    if below_ref.shape[0] != 128:
        sides[...] = jnp.zeros_like(sides)
    rows = below_ref.shape[0]
    sides[0:rows, 0:SIDE] = below_ref[...]
    sides[0:rows, SIDE : 2 * SIDE] = above_ref[...]
    side_traces = stacked_traces(trace_ref, sides[...])

    def put(start, value, face, coarse):
        width = value.shape[1]
        high = value.astype(BF16).astype(F32)
        low = value - high
        for f in range(6):
            live = face == f
            spread[f * FACE : (f + 1) * FACE, start : start + width] = jnp.where(live, high, 0.0).astype(BF16)
            spread[TRACE + f * FACE : TRACE + (f + 1) * FACE, start : start + width] = jnp.where(
                live, low, 0.0
            ).astype(BF16)
        row = lax.broadcasted_iota(jnp.int32, (16, width), 0)
        spread[2 * TRACE : 2 * TRACE + 16, start : start + width] = jnp.where(
            row == (face + 8 if coarse else face), 1.0, 0.0
        ).astype(BF16)

    for start in range(0, PAIR_SLOTS, CHUNK):
        face, cell = extended_code(codes[1:2, start : start + CHUNK])
        place = jnp.where(cell < 0, cell + SIDE, jnp.where(cell >= CELLS, cell + (SIDE - CELLS), -1))
        place = jnp.where(face < 0, -1, place)
        partner = partner_ref[:, start : start + CHUNK] + pick(
            dot(side_traces, one_hot(place, 2 * SIDE)), face
        )
        face, cell = own_code(codes[0:1, start : start + CHUNK])
        hot[:, start : start + CHUNK] = one_hot(cell, CELLS)
        put(start, -TAU_PENALTY * partner, face, False)
    predicted = table_dot(dh_ref, dl_ref, arriving_ref[...])
    for child in range(4):
        face, _ = own_code(fine_ref[child : child + 1, :])
        put(FINE0 + child * CELLS, predicted[child * FACE : (child + 1) * FACE], face, False)
    face, _ = own_code(coarse_ref[...])
    put(COARSE0, returned_ref[...], face, True)
    added = dot(spread[...], hot[...], ALONG_LANES)
    pieces = []
    for f in range(6):
        rows = slice(f * FACE, (f + 1) * FACE)
        fine_count = added[2 * TRACE + f : 2 * TRACE + f + 1]
        coarse_count = added[2 * TRACE + 8 + f : 2 * TRACE + 9 + f]
        pieces.append(
            added[f * FACE : (f + 1) * FACE]
            + added[TRACE + f * FACE : TRACE + (f + 1) * FACE]
            + (TAU_PENALTY * fine_count) * trace_in_ref[rows, :]
            + coarse_count * coarse_in_ref[rows, :]
        )
    high, low = split(jnp.concatenate(pieces, axis=0))
    untrace = untrace_ref[...]
    return applied_ref[...] + (dot(untrace, high) + dot(untrace, low))


def image_kernel(*refs):
    (coarse_ref, fine_ref, trace_ref) = (refs[1], refs[2], refs[11])
    uph_ref, upl_ref = refs[15:17]
    out_ref, low_ref, high_ref, send_coarse_ref, send_fine_ref = refs[17:22]
    codes, sides, hot, spread = refs[22:]
    image = add_faces(*refs[:15], codes, sides, hot, spread)
    out_ref[...] = image
    low_ref[...] = image[:, 0:SIDE]
    high_ref[...] = image[:, CELLS - SIDE :]
    traces = stacked_traces(trace_ref, image)
    send_coarse, send_fine = gather_hanging(traces, hot, coarse_ref, fine_ref, (uph_ref, upl_ref))
    send_coarse_ref[...] = send_coarse
    send_fine_ref[...] = send_fine


def total(value):
    return jnp.sum(jnp.sum(value, axis=0, keepdims=True), axis=1, keepdims=True)


def moments_kernel(*refs):
    source_ref, image_ref = refs[15:17]
    out_ref, sums_ref = refs[17:19]
    codes, sides, hot, spread = refs[19:]
    second = add_faces(*refs[:15], codes, sides, hot, spread)
    out_ref[...] = second
    source = source_ref[...]
    image = image_ref[...]
    products = [
        source * source,
        source * image[0:125],
        image * image,
        source * second[0:125],
        image * second,
    ]
    lane = lax.broadcasted_iota(jnp.int32, (1, 128), 1)
    line = jnp.zeros((1, 128), F32)
    for index, product in enumerate(products):
        line = line + jnp.where(lane == index, total(product), 0.0)
    sums_ref[...] = jnp.broadcast_to(line[None], sums_ref.shape)


def last_kernel(sums_ref, source_ref, image_ref, second_ref, solution_ref, residual_ref):
    line = jnp.sum(sums_ref[...], axis=0)
    rr, rw, ww, ru, wu = (line[:, i : i + 1] for i in range(5))
    first_step = rr / rw
    rr_next = rr - 2.0 * first_step * rw + first_step * first_step * ww
    grown = 1.0 + rr_next / rr
    curvature = (
        grown * grown * rw - first_step * grown * (ru + ww) + first_step * first_step * wu
    )
    second_step = rr_next / curvature
    p = first_step + second_step * grown
    q = second_step * first_step
    source = source_ref[...]
    image = image_ref[0:125, :]
    solution_ref[...] = p * source - q * image
    residual_ref[...] = source - p * image + q * second_ref[0:125, :]


def call(kernel, out_shapes, scratch, *operands, name):
    space = pl.BlockSpec(memory_space=pltpu.VMEM)
    return pl.pallas_call(
        kernel,
        out_shape=[jax.ShapeDtypeStruct(shape, F32) for shape in out_shapes],
        in_specs=[space] * len(operands),
        out_specs=[space] * len(out_shapes),
        scratch_shapes=scratch,
        compiler_params=pltpu.CompilerParams(vmem_limit_bytes=48 * 1024 * 1024),
        name=name,
    )(*operands)


FIELD = pltpu.VMEM((128, CELLS), F32)
CODES = pltpu.VMEM((8, PAIR_SLOTS), jnp.int32)
SIDES = pltpu.VMEM((128, 2 * SIDE), F32)
HOT = pltpu.VMEM((CELLS, SLOTS), BF16)
SPREAD = pltpu.VMEM((2 * TRACE + 16, SLOTS), BF16)


def shifted(value, axes, step):
    count = lax.axis_size(axes)
    return lax.ppermute(
        value, axes, [(i, i + step) for i in range(count) if 0 <= i + step < count]
    )


def on_device(source, levels, ids, values, pairs, coarse, fine):
    tables = constant_tables()
    block = ("z", "x", "y", "core")
    dom = ("z", "x")
    plane = ("x", "y", "core")
    levels, ids, values, coarse = (a.reshape(1, -1) for a in (levels, ids, values, coarse))
    trace, untrace = tables["trace"], tables["untrace"]

    def middle(field):
        return call(
            middle_kernel,
            [(128, CELLS), (TRACE, CELLS), (TRACE, CELLS), (FACE, PAIR_SLOTS)],
            [FIELD, CODES],
            field,
            pairs,
            levels,
            ids,
            values,
            trace,
            *tables["local"],
            tables["lumped"],
            *tables["coarse"],
            name="middle",
        )

    below = shifted(source[:, CELLS - SIDE :], block, 1)
    above = shifted(source[:, :SIDE], block, -1)
    send_coarse, send_fine = call(
        first_kernel,
        [(FACE, CELLS)] * 2,
        [FIELD, HOT],
        source,
        coarse,
        fine,
        trace,
        *tables["up"],
        name="first",
    )
    arriving = shifted(send_coarse, dom, 1)
    returned = shifted(send_fine, dom, -1)
    scratch = [CODES, SIDES, HOT, SPREAD]
    image, low, high, send_coarse, send_fine = call(
        image_kernel,
        [(128, CELLS), (128, SIDE), (128, SIDE), (FACE, CELLS), (FACE, CELLS)],
        scratch,
        pairs,
        coarse,
        fine,
        *middle(source),
        below,
        above,
        arriving,
        returned,
        trace,
        untrace,
        *tables["down"],
        *tables["up"],
        name="image",
    )
    below = shifted(high, block, 1)
    above = shifted(low, block, -1)
    arriving = shifted(send_coarse, dom, 1)
    returned = shifted(send_fine, dom, -1)
    in_plane = lax.axis_size(plane)
    along_z = lax.axis_size("z")
    second, sums = call(
        moments_kernel,
        [(128, CELLS), (in_plane, 1, 128)],
        scratch,
        pairs,
        coarse,
        fine,
        *middle(image),
        below,
        above,
        arriving,
        returned,
        trace,
        untrace,
        *tables["down"],
        source,
        image,
        name="moments",
    )
    sums = lax.all_to_all(sums, plane, 0, 0, tiled=True)
    sums = jnp.broadcast_to(jnp.sum(sums, axis=0, keepdims=True), (along_z, 1, 128))
    sums = lax.all_to_all(sums, "z", 0, 0, tiled=True)
    return tuple(call(last_kernel, [source.shape] * 2, [], sums, source, image, second, name="last"))


def solution(mesh):
    dom, sub = mesh.devices.shape
    axes = ("z", "x", "y", "core")
    fine_mesh = Mesh(mesh.devices.reshape(dom // 4, 4, sub // 2, 2), axes)
    return jax.shard_map(
        on_device,
        mesh=fine_mesh,
        in_specs=(
            P(None, axes),
            P(axes),
            P(axes),
            P(),
            P(None, axes),
            P(axes),
            P(None, axes),
        ),
        out_specs=(P(None, axes), P(None, axes)),
        check_vma=False,
    )
```

time: 651 us -> 123 us (0.19); the launches traced: 643 us -> 122 us
  blocking collectives: 475 us -> 69.1 us
  other arithmetic: 81.8 us -> 0.05 us
  local copies, waits for them, and re-layouts: 38.6 us -> 4.48 us
  Pallas kernels: 0 us -> 11.3 us
  matrix products: 10.8 us -> 0 us
    psum x3 -> x0, blocking collectives: 475 us -> none  [the longest x2 318 us: squares_total(): return lax.psum(jnp.sum(residual * residual), ('dom', 'sub'))]
    scatter-add x14 -> x0, other arithmetic: 73.8 us -> none  [the longest x2 34.2 us: operate(): contribution = jnp.zeros_like(flat_local).at[:, first_safe].add(face_jump)]
    all_to_all x0 -> x2, blocking collectives: none -> 69.1 us  [the longest x1 53.1 us: on_device(): sums = lax.all_to_all(sums, 'z', 0, 0, tiled=True)]
    gather x8 -> x0, local copies, waits for them, and re-layouts: 20.5 us -> none  [the longest x4 18.2 us: operate(): fine_values = flat_local[:, fine_safe] * fine_live]
    pallas_call x0 -> x6, Pallas kernels: none -> 11.3 us  [call(): pl.pallas_call(kernel, out_shape=[jax.ShapeDtypeStruct(shape, F32) for sh...]
    dot_general x11 -> x0, matrix products: 10.8 us -> none  [the longest x2 3.18 us: local_apply(): jnp.einsum('ai,ijkc->ajkc', stiffness, nodal_cube, precision=HIGHEST)]
  transfers between devices with their start and end apart: 8 -> 8, of which waited for: 0 -> 1; matrix products, arithmetic and copies ran while one was open for 16% -> 0% of each run, Pallas kernels for 0% -> 2%
where the time goes in v1:
time: 123 us; the launch traced here: 122 us
  blocking collectives  69.1 us (56%)
  starting transfers between devices  34 us (28%)
  Pallas kernels  11.3 us (9%)
  local copies, waits for them, and re-layouts  4.48 us (4%)
  waiting for transfers between devices  2.5 us (2%)
    all_to_all x1, blocking collectives, on_device(): sums = lax.all_to_all(sums, 'z', 0, 0, tiled=True)  53.1 us
    ppermute x8, starting transfers between devices, shifted(): lax.ppermute(value, axes, [(i, i + step) for i in range(count) if 0 <= i...  34 us
    all_to_all x1, blocking collectives, on_device(): sums = lax.all_to_all(sums, plane, 0, 0, tiled=True)  16.1 us
    pallas_call x6, Pallas kernels, call(): pl.pallas_call(kernel, out_shape=[jax.ShapeDtypeStruct(shape, F32) for sh...  11.3 us
    unnamed x42, local copies, waits for them, and re-layouts  4.46 us
    ppermute x8, waiting for transfers between devices, shifted(): lax.ppermute(value, axes, [(i, i + step) for i in range(count) if 0 <= i...  2.5 us
  transfers between devices with their start and end apart: 8, of which 1 were waited for; matrix products, arithmetic and copies ran while one was open for 0% of the time, Pallas kernels for 2%

profile of v1, /device:TPU:1, one launch (start us, length us, event | category | flops | bytes accessed | tf_op | source)
XLA Modules:
  0.0 122.4 jit_solution(8753651987338133596)
XLA Ops:
  0.7 0.7 copy-done.16
  1.3 0.9 copy-done
  2.3 0.8 copy-done.2
  3.1 0.7 copy-done.13
  3.8 0.7 copy-done.17
  4.5 1.5 %first.1 = (f32[32,512]{1,0:T(8,128)S(1)}, f32[32,512]{1,0:T(8,128)S(1)}) custom-call(f32[125,512]{1,0:T(8,128)S(1)} %copy-done, s32[1,512]{1,0:T(1,128)S(1)} %bitcast.4, s32[4,512]{1,0:T(4,128)S(1)} %copy-done.13, bf16[192,128]{1,0:T(8,128)(2,1)S(1)} %copy-done.2, bf16[32,128]{1,0:T(8,128)(2,1)S(1)} %copy-done.16, bf16[32,128]{1,0:T(8,128)(2,1)S(1)} %copy-done.15), custom_call_target="tpu_custom_call" | custom-call | tf_op jit(solution)/shard_map/first/pallas_call | solution.py:379
  6.0 3.9 %collective-permute-start.2 = (f32[32,512]{1,0:T(8,128)S(1)}, f32[32,512]{1,0:T(8,128)S(1)}, u32[]{:S(2)}, u32[]{:S(2)}) collective-permute-start(f32[32,512]{1,0:T(8,128)S(1)} %get-tuple-element.23), channel_id=1, source_target_pairs={{0,8},{8,16},{16,24},{24,32},{32,40},{40,48},{48,56},{56,64},{64,7... | collective-permute-start | bytes 196616 | tf_op jit(solution)/shard_map/ppermute | solution.py:399
  10.0 1.4 %collective-permute-start.3 = (f32[32,512]{1,0:T(8,128)S(1)}, f32[32,512]{1,0:T(8,128)S(1)}, u32[]{:S(2)}, u32[]{:S(2)}) collective-permute-start(f32[32,512]{1,0:T(8,128)S(1)} %get-tuple-element.24), channel_id=1, source_target_pairs={{8,0},{16,8},{24,16},{32,24},{40,32},{48,40},{56,48},{64,56},{72,6... | collective-permute-start | bytes 196616 | tf_op jit(solution)/shard_map/ppermute | solution.py:399
  11.5 13.4 %collective-permute-start.1 = (f32[125,128]{1,0:T(8,128)S(1)}, f32[125,128]{1,0:T(8,128)S(1)}, u32[]{:S(2)}, u32[]{:S(2)}) collective-permute-start(f32[125,128]{1,0:T(8,128)S(1)} %get-tuple-element.36), channel_id=1, source_target_pairs={{1,0},{2,1},{3,2},{4,3},{5,4},{6,5},{7,6},{8,7},{9,8},{10,9},{11,1... | collective-permute-start | bytes 192008 | tf_op jit(solution)/shard_map/ppermute | solution.py:399
  24.9 1.9 %collective-permute-start = (f32[125,128]{1,0:T(8,128)S(1)}, f32[125,128]{1,0:T(8,128)S(1)}, u32[]{:S(2)}, u32[]{:S(2)}) collective-permute-start(f32[125,128]{1,0:T(8,128)S(1)} %get-tuple-element.37), channel_id=1, source_target_pairs={{0,1},{1,2},{2,3},{3,4},{4,5},{5,6},{6,7},{7,8},{8,9},{9,10},{10,1... | collective-permute-start | bytes 192008 | tf_op jit(solution)/shard_map/ppermute | solution.py:399
  26.9 0.6 copy-done.20
  27.5 1.2 middle.2
  28.7 3.8 %image.1 = (f32[128,512]{1,0:T(8,128)S(1)}, f32[128,128]{1,0:T(8,128)S(1)}, f32[128,128]{1,0:T(8,128)S(1)}, f32[32,512]{1,0:T(8,128)S(1)}, f32[32,512]{1,0:T(8,128)S(1)}) custom-call(s32[2,960]{1,0:T(2,128)S(1)} %copy-done.8, s32[1,512]{1,0:T(1,128)S(1)} %bitcast.5, s32[4,512]{1,0:T(4,128)S(1)} %copy-done.13, f32[128,512]{1,0:T(8,128)S(1)} %get-tuple-element.19.refs_3_, ...), custom_call_target="tpu_custom_call" | custom-call | tf_op jit(solution)/shard_map/image/pallas_call | solution.py:379
  32.5 3.7 %collective-permute-start.4 = (f32[128,128]{1,0:T(8,128)S(1)}, f32[128,128]{1,0:T(8,128)S(1)}, u32[]{:S(2)}, u32[]{:S(2)}) collective-permute-start(f32[128,128]{1,0:T(8,128)S(1)} %get-tuple-element.30), channel_id=1, source_target_pairs={{0,1},{1,2},{2,3},{3,4},{4,5},{5,6},{6,7},{7,8},{8,9},{9,10},{10,1... | collective-permute-start | bytes 196616 | tf_op jit(solution)/shard_map/ppermute | solution.py:399
  36.2 1.9 %collective-permute-start.5 = (f32[128,128]{1,0:T(8,128)S(1)}, f32[128,128]{1,0:T(8,128)S(1)}, u32[]{:S(2)}, u32[]{:S(2)}) collective-permute-start(f32[128,128]{1,0:T(8,128)S(1)} %get-tuple-element.31), channel_id=1, source_target_pairs={{1,0},{2,1},{3,2},{4,3},{5,4},{6,5},{7,6},{8,7},{9,8},{10,9},{11,1... | collective-permute-start | bytes 196616 | tf_op jit(solution)/shard_map/ppermute | solution.py:399
  38.2 6.4 %collective-permute-start.6 = (f32[32,512]{1,0:T(8,128)S(1)}, f32[32,512]{1,0:T(8,128)S(1)}, u32[]{:S(2)}, u32[]{:S(2)}) collective-permute-start(f32[32,512]{1,0:T(8,128)S(1)} %get-tuple-element.32), channel_id=1, source_target_pairs={{0,8},{8,16},{16,24},{24,32},{32,40},{40,48},{48,56},{56,64},{64,7... | collective-permute-start | bytes 196616 | tf_op jit(solution)/shard_map/ppermute | solution.py:399
  44.5 1.3 %collective-permute-start.7 = (f32[32,512]{1,0:T(8,128)S(1)}, f32[32,512]{1,0:T(8,128)S(1)}, u32[]{:S(2)}, u32[]{:S(2)}) collective-permute-start(f32[32,512]{1,0:T(8,128)S(1)} %get-tuple-element.33), channel_id=1, source_target_pairs={{8,0},{16,8},{24,16},{32,24},{40,32},{48,40},{56,48},{64,56},{72,6... | collective-permute-start | bytes 196616 | tf_op jit(solution)/shard_map/ppermute | solution.py:399
  45.9 1.2 middle.3
  47.1 2.5 %collective-permute-done.7.refs_10_ = f32[32,512]{1,0:T(8,128)S(1)} collective-permute-done((f32[32,512]{1,0:T(8,128)S(1)}, f32[32,512]{1,0:T(8,128)S(1)}, u32[]{:S(2)}, u32[]{:S(2)}) %collective-permute-start.7) | collective-permute-done | bytes 65568 | tf_op jit(solution)/shard_map/ppermute | solution.py:399
  49.6 2.6 %moments.1 = (f32[128,512]{1,0:T(8,128)S(1)}, f32[32,1,128]{2,1,0:T(1,128)S(1)}) custom-call(s32[2,960]{1,0:T(2,128)S(1)} %copy-done.8, s32[1,512]{1,0:T(1,128)S(1)} %bitcast.6, s32[4,512]{1,0:T(4,128)S(1)} %copy-done.14, f32[128,512]{1,0:T(8,128)S(1)} %get-tuple-element.26.refs_3_, f32[192,512]{1,0:T(8,128)S(1)} %get-tuple-element.27.refs_4_, ...), custom_call_target="tpu_custom_call" | custom-call | tf_op jit(solution)/shard_map/moments/pallas_call | solution.py:379
  52.1 16.1 %all_to_all.10 = f32[32,1,128]{2,1,0:T(1,128)S(1)} all-to-all(f32[32,1,128]{2,1,0:T(1,128)S(1)} %get-tuple-element.34), channel_id=1, replica_groups=mesh['z'=32,'x'=4,'y'=4,'core'=2] {'x','y','core'}, dimensions={0} | all-to-all | bytes 32768 | tf_op jit(solution)/shard_map/all_to_all | solution.py:488
  68.2 0.1 reduce_sum.9
  68.2 53.1 %all_to_all.11.sums_ref = f32[32,1,128]{2,1,0:T(1,128)S(1)} all-to-all(f32[32,1,128]{2,1,0:T(1,128)S(1)} %broadcast_in_dim.2), channel_id=1, replica_groups=mesh['z'=32,'x'=4,'y'=4,'core'=2] {'z'}, dimensions={0} | all-to-all | bytes 32768 | tf_op jit(solution)/shard_map/all_to_all | solution.py:490
  121.3 1.1 last.1
  (45 shorter events, 0.2 us)
Async XLA Ops:
  1.3 0.9 copy-start
  2.3 0.8 copy-start.2
  4.5 22.3 %copy-start.7 = (f32[128,1]{1,0:T(8,128)S(1)}, f32[128,1]{1,0:T(8,128)}, u32[]{:S(2)}) copy-start(f32[128,1]{1,0:T(8,128)} %constant.29.clone.lumped_ref) | copy-start | bytes 1540
  4.5 22.3 %copy-start.11 = (bf16[128,128]{1,0:T(8,128)(2,1)S(1)}, bf16[128,128]{1,0:T(8,128)(2,1)}, u32[]{:S(2)}) copy-start(bf16[128,128]{1,0:T(8,128)(2,1)} %constant.28.clone.ll_ref) | copy-start | bytes 98308
  4.5 22.4 %copy-start.12 = (bf16[128,128]{1,0:T(8,128)(2,1)S(1)}, bf16[128,128]{1,0:T(8,128)(2,1)}, u32[]{:S(2)}) copy-start(bf16[128,128]{1,0:T(8,128)(2,1)} %constant.27.clone.lh_ref) | copy-start | bytes 98308
  6.0 22.7 %collective-permute-start.2 = (f32[32,512]{1,0:T(8,128)S(1)}, f32[32,512]{1,0:T(8,128)S(1)}, u32[]{:S(2)}, u32[]{:S(2)}) collective-permute-start(f32[32,512]{1,0:T(8,128)S(1)} %get-tuple-element.23), channel_id=1, source_target_pairs={{0,8},{8,16},{16,24},{24,32},{32,40},{40,48},{48,56},{56,64},{64,7... | collective-permute-start | bytes 196616 | tf_op jit(solution)/shard_map/ppermute | solution.py:399
  9.9 16.9 %copy-start.3 = (bf16[192,128]{1,0:T(8,128)(2,1)S(1)}, bf16[192,128]{1,0:T(8,128)(2,1)}, u32[]{:S(2)}) copy-start(bf16[192,128]{1,0:T(8,128)(2,1)} %constant.24.clone.trace_ref.refs_11_) | copy-start | bytes 147460
  9.9 16.9 %copy-start.4 = (bf16[192,192]{1,0:T(8,128)(2,1)S(1)}, bf16[192,192]{1,0:T(8,128)(2,1)}, u32[]{:S(2)}) copy-start(bf16[192,192]{1,0:T(8,128)(2,1)} %constant.31.clone.ml_ref) | copy-start | bytes 221188
  10.0 16.9 %copy-start.5 = (bf16[192,192]{1,0:T(8,128)(2,1)S(1)}, bf16[192,192]{1,0:T(8,128)(2,1)}, u32[]{:S(2)}) copy-start(bf16[192,192]{1,0:T(8,128)(2,1)} %constant.30.clone.mh_ref) | copy-start | bytes 221188
  10.0 18.7 %collective-permute-start.3 = (f32[32,512]{1,0:T(8,128)S(1)}, f32[32,512]{1,0:T(8,128)S(1)}, u32[]{:S(2)}, u32[]{:S(2)}) collective-permute-start(f32[32,512]{1,0:T(8,128)S(1)} %get-tuple-element.24), channel_id=1, source_target_pairs={{8,0},{16,8},{24,16},{32,24},{40,32},{48,40},{56,48},{64,56},{72,6... | collective-permute-start | bytes 196616 | tf_op jit(solution)/shard_map/ppermute | solution.py:399
  11.4 15.5 %copy-start.18 = (s32[512]{0:T(512)S(1)}, s32[512]{0:T(512)}, u32[]{:S(2)}) copy-start(s32[512]{0:T(512)} %param.19) | copy-start | bytes 6148
  11.4 15.5 %copy-start.19 = (s32[512]{0:T(512)S(1)}, s32[512]{0:T(512)}, u32[]{:S(2)}) copy-start(s32[512]{0:T(512)} %param.20) | copy-start | bytes 6148
  11.4 15.5 %copy-start.8 = (s32[2,960]{1,0:T(2,128)S(1)}, s32[2,960]{1,0:T(2,128)}, u32[]{:S(2)}) copy-start(s32[2,960]{1,0:T(2,128)} %refs_0_.3) | copy-start | bytes 23044
  11.5 17.2 %collective-permute-start.1 = (f32[125,128]{1,0:T(8,128)S(1)}, f32[125,128]{1,0:T(8,128)S(1)}, u32[]{:S(2)}, u32[]{:S(2)}) collective-permute-start(f32[125,128]{1,0:T(8,128)S(1)} %get-tuple-element.36), channel_id=1, source_target_pairs={{1,0},{2,1},{3,2},{4,3},{5,4},{6,5},{7,6},{8,7},{9,8},{10,9},{11,1... | collective-permute-start | bytes 192008 | tf_op jit(solution)/shard_map/ppermute | solution.py:399
  24.9 3.8 %collective-permute-start = (f32[125,128]{1,0:T(8,128)S(1)}, f32[125,128]{1,0:T(8,128)S(1)}, u32[]{:S(2)}, u32[]{:S(2)}) collective-permute-start(f32[125,128]{1,0:T(8,128)S(1)} %get-tuple-element.37), channel_id=1, source_target_pairs={{0,1},{1,2},{2,3},{3,4},{4,5},{5,6},{6,7},{7,8},{8,9},{9,10},{10,1... | collective-permute-start | bytes 192008 | tf_op jit(solution)/shard_map/ppermute | solution.py:399
  27.5 1.2 %copy-start.6 = (bf16[128,192]{1,0:T(8,128)(2,1)S(1)}, bf16[128,192]{1,0:T(8,128)(2,1)}, u32[]{:S(2)}) copy-start(bf16[128,192]{1,0:T(8,128)(2,1)} %constant.32.clone.refs_12_) | copy-start | bytes 147460
  27.5 1.2 %copy-start.9 = (bf16[128,32]{1,0:T(8,128)(2,1)S(1)}, bf16[128,32]{1,0:T(8,128)(2,1)}, u32[]{:S(2)}) copy-start(bf16[128,32]{1,0:T(8,128)(2,1)} %constant.34.clone.refs_14_) | copy-start | bytes 24580
  27.5 1.3 %copy-start.10 = (bf16[128,32]{1,0:T(8,128)(2,1)S(1)}, bf16[128,32]{1,0:T(8,128)(2,1)}, u32[]{:S(2)}) copy-start(bf16[128,32]{1,0:T(8,128)(2,1)} %constant.33.clone.refs_13_) | copy-start | bytes 24580
  32.5 14.5 %collective-permute-start.4 = (f32[128,128]{1,0:T(8,128)S(1)}, f32[128,128]{1,0:T(8,128)S(1)}, u32[]{:S(2)}, u32[]{:S(2)}) collective-permute-start(f32[128,128]{1,0:T(8,128)S(1)} %get-tuple-element.30), channel_id=1, source_target_pairs={{0,1},{1,2},{2,3},{3,4},{4,5},{5,6},{6,7},{7,8},{8,9},{9,10},{10,1... | collective-permute-start | bytes 196616 | tf_op jit(solution)/shard_map/ppermute | solution.py:399
  36.2 10.8 %collective-permute-start.5 = (f32[128,128]{1,0:T(8,128)S(1)}, f32[128,128]{1,0:T(8,128)S(1)}, u32[]{:S(2)}, u32[]{:S(2)}) collective-permute-start(f32[128,128]{1,0:T(8,128)S(1)} %get-tuple-element.31), channel_id=1, source_target_pairs={{1,0},{2,1},{3,2},{4,3},{5,4},{6,5},{7,6},{8,7},{9,8},{10,9},{11,1... | collective-permute-start | bytes 196616 | tf_op jit(solution)/shard_map/ppermute | solution.py:399
  38.2 8.9 %collective-permute-start.6 = (f32[32,512]{1,0:T(8,128)S(1)}, f32[32,512]{1,0:T(8,128)S(1)}, u32[]{:S(2)}, u32[]{:S(2)}) collective-permute-start(f32[32,512]{1,0:T(8,128)S(1)} %get-tuple-element.32), channel_id=1, source_target_pairs={{0,8},{8,16},{16,24},{24,32},{32,40},{40,48},{48,56},{56,64},{64,7... | collective-permute-start | bytes 196616 | tf_op jit(solution)/shard_map/ppermute | solution.py:399
  44.5 5.0 %collective-permute-start.7 = (f32[32,512]{1,0:T(8,128)S(1)}, f32[32,512]{1,0:T(8,128)S(1)}, u32[]{:S(2)}, u32[]{:S(2)}) collective-permute-start(f32[32,512]{1,0:T(8,128)S(1)} %get-tuple-element.33), channel_id=1, source_target_pairs={{8,0},{16,8},{24,16},{32,24},{40,32},{48,40},{56,48},{64,56},{72,6... | collective-permute-start | bytes 196616 | tf_op jit(solution)/shard_map/ppermute | solution.py:399
  45.8 3.7 %copy-start.1 = (f32[125,512]{1,0:T(8,128)S(1)}, f32[125,512]{1,0:T(8,128)}, u32[]{:S(2)}) copy-start(f32[125,512]{1,0:T(8,128)} %source_ref.1) | copy-start | bytes 768004
  45.9 3.7 %copy-start.14 = (s32[4,512]{1,0:T(4,128)S(1)}, s32[4,512]{1,0:T(4,128)}, u32[]{:S(2)}) copy-start(s32[4,512]{1,0:T(4,128)} %refs_2_.3) | copy-start | bytes 24580
  (5 other events, 3.4 us)

commit v2 on v1

v2 whole, which is shorter than its diff:
```python
import jax
import jax.numpy as jnp
import numpy as np
import ml_dtypes
from jax import lax
from jax.experimental import pallas as pl
from jax.experimental.pallas import tpu as pltpu
from jax.sharding import Mesh, PartitionSpec as P

CELLS = 512
RIM = 64
EXTENT = CELLS + 2 * RIM
PAIRS = 960
PAIR_SLOTS = 1024
SIDE = 128
FACE = 32
TRACE = 6 * FACE
FINE0 = PAIR_SLOTS
COARSE0 = PAIR_SLOTS + 4 * CELLS
SLOTS = COARSE0 + CELLS
CHUNK = 512
FINE_ROW = 2
COARSE_ROW = 6
TAU_PENALTY = 2.0
SIGMA_MASS = 4.0
BLOCK = ("z", "x", "y", "core")
DOM = ("z", "x")
PLANE = ("x", "y", "core")
F32 = jnp.float32
BF16 = jnp.bfloat16
ALONG_ROWS = (((1,), (0,)), ((), ()))
ALONG_LANES = (((1,), (1,)), ((), ()))


def element_tables():
    points = np.array([-1.0, -np.sqrt(3.0 / 7.0), 0.0, np.sqrt(3.0 / 7.0), 1.0])
    weights = np.array([0.1, 49.0 / 90.0, 32.0 / 45.0, 49.0 / 90.0, 0.1])

    def lagrange(location):
        values = np.ones((location.shape[0], 5))
        for column in range(5):
            for other in range(5):
                if other != column:
                    values[:, column] *= (location - points[other]) / (
                        points[column] - points[other]
                    )
        return values

    derivative = np.zeros((5, 5))
    for column in range(5):
        for other in range(5):
            if other != column:
                product = np.ones(5) / (points[column] - points[other])
                for remaining in range(5):
                    if remaining != column and remaining != other:
                        product = (
                            product
                            * (points - points[remaining])
                            / (points[column] - points[remaining])
                        )
                derivative[:, column] += product
    stiffness = derivative.T @ (weights[:, None] * derivative)
    halves = [lagrange((points - 1.0) / 2.0), lagrange((points + 1.0) / 2.0)]
    interp = [np.kron(halves[a], halves[b]) for a in range(2) for b in range(2)]
    return stiffness, weights, interp


def two_parts(table):
    high = table.astype(np.float32).astype(ml_dtypes.bfloat16)
    low = (table - high.astype(np.float64)).astype(np.float32).astype(ml_dtypes.bfloat16)
    return high, low


PLACES = {
    "trace": [(0, 0)],
    "up": [(192, 0), (192, 128)],
    "untrace": [(224, 0)],
    "coarse": [(352, 0), (544, 0)],
    "local": [(736, 0), (736, 128)],
    "down": [(864, 0), (864, 128)],
    "lumped": [(992, 0), (992, 128)],
}
FIRST_ROWS = 224
TABLE_ROWS = 1120


def packed_table():
    stiffness, weights, interp = element_tables()
    diag = np.diag(weights)

    def kron3(a, b, c):
        return np.kron(np.kron(a, b), c)

    local = np.zeros((128, 128))
    local[:125, :125] = (
        kron3(stiffness, diag, diag) + kron3(diag, stiffness, diag) + kron3(diag, diag, stiffness)
    )
    lumped = np.zeros((128, 1))
    lumped[:125, 0] = SIGMA_MASS * np.einsum("i,j,k->ijk", weights, weights, weights).reshape(-1)
    node = np.arange(125).reshape(5, 5, 5)
    slabs = [node[0], node[:, 0], node[:, :, 0], node[4], node[:, 4], node[:, :, 4]]
    trace = np.zeros((TRACE, 128))
    for face, slab in enumerate(slabs):
        trace[face * FACE + np.arange(25), slab.reshape(-1)] = 1.0
    coarse = np.zeros((FACE, FACE))
    down = np.zeros((4 * FACE, FACE))
    for child, matrix in enumerate(interp):
        coarse[:25, :25] += matrix.T @ matrix
        down[child * FACE : child * FACE + 25, :25] = matrix
    table = np.zeros((TABLE_ROWS, 256))
    places = {
        "trace": trace,
        "untrace": trace.T,
        "local": local,
        "coarse": np.kron(np.eye(6), TAU_PENALTY * coarse),
        "down": -TAU_PENALTY * down,
        "up": -TAU_PENALTY * down.T,
        "lumped": lumped,
    }
    for name, value in places.items():
        parts = [value] if name.endswith("trace") else two_parts(value)
        for (row, lane), part in zip(PLACES[name], parts):
            table[row : row + value.shape[0], lane : lane + value.shape[1]] = part
    return table.astype(ml_dtypes.bfloat16)


def views(table):
    def view(name, rows, lanes):
        return [table.at[row : row + rows, lane : lane + lanes] for row, lane in PLACES[name]]

    return {
        "trace": view("trace", TRACE, 128)[0],
        "untrace": view("untrace", 128, TRACE)[0],
        "local": view("local", 128, 128),
        "coarse": view("coarse", TRACE, TRACE),
        "down": view("down", 4 * FACE, FACE),
        "up": view("up", FACE, 128),
        "lumped": view("lumped", 128, 1),
    }


def dot(a, b, dims=ALONG_ROWS):
    return lax.dot_general(a, b, dims, preferred_element_type=F32)


def split(value):
    high = value.astype(BF16)
    return high, (value - high.astype(F32)).astype(BF16)


def table_dot(parts, value):
    high, low = split(value)
    table = parts[0][...]
    return dot(table, high) + dot(table, low) + dot(parts[1][...], high)


def face_traces(trace_ref, field):
    high, low = split(field)
    table = trace_ref[...]
    return dot(table, high), dot(table, low)


def one_hot(cell, rows):
    place = lax.broadcasted_iota(jnp.int32, (rows, cell.shape[1]), 0)
    return jnp.where(place == cell, 1.0, 0.0).astype(BF16)


def pick(gathered, face):
    total = None
    for f in range(6):
        both = gathered[f * FACE : (f + 1) * FACE] + gathered[TRACE + f * FACE : TRACE + (f + 1) * FACE]
        term = jnp.where(face == f, both, 0.0)
        total = term if total is None else total + term
    return total


def own_code(code):
    return code >> 9, code & (CELLS - 1)


def extended_code(code):
    face = jnp.where(code < 0, -1, 0)
    for f in range(1, 6):
        face = face + jnp.where(code >= f * EXTENT, 1, 0)
    return face, code - face * EXTENT - RIM


def padded_field(field_ref, field):
    if field_ref.shape[0] == 128:
        return field_ref[...]
    field[...] = jnp.zeros_like(field)
    field[0:125, :] = field_ref[...]
    return field[...]


def fine_code(codes, child):
    return own_code(codes[FINE_ROW + child : FINE_ROW + child + 1, 0:CELLS])


def coarse_code(codes):
    return own_code(codes[COARSE_ROW : COARSE_ROW + 1, 0:CELLS])


def gather_hanging(traces, hot, codes, up):
    rows = []
    for child in range(4):
        face, _ = fine_code(codes, child)
        start = FINE0 + child * CELLS
        rows.append(pick(dot(traces, hot[:, start : start + CELLS]), face))
    face, _ = coarse_code(codes)
    send_coarse = pick(dot(traces, hot[:, COARSE0:SLOTS]), face)
    send_fine = table_dot(up, jnp.concatenate(rows, axis=0))
    return send_coarse, send_fine


def hot_hanging(hot, codes):
    for child in range(4):
        _, cell = fine_code(codes, child)
        start = FINE0 + child * CELLS
        hot[:, start : start + CELLS] = one_hot(cell, CELLS)
    _, cell = coarse_code(codes)
    hot[:, COARSE0:SLOTS] = one_hot(cell, CELLS)


def stacked_traces(trace_ref, field):
    high, low = face_traces(trace_ref, field)
    return jnp.concatenate([high.astype(BF16), low.astype(BF16)], axis=0)


def swaps(low, high, send_coarse, send_fine, rim_chip_ref, dom_odd_ref, rim_core_ref, dom_even_ref):
    first_core = lax.axis_index("core") == 0
    even_dom = lax.axis_index("x") % 2 == 0
    rim_core_ref[...] = jnp.where(first_core, high, low)
    rim_chip_ref[...] = jnp.where(first_core, low, high)
    dom_even_ref[...] = jnp.where(even_dom, send_coarse, send_fine)
    dom_odd_ref[...] = jnp.where(even_dom, send_fine, send_coarse)


def first_kernel(*refs):
    field_in, level_in, id_in, values_in, pairs_in, coarse_in, fine_in, table_in = refs[:8]
    outs, codes, scales = refs[8:12], refs[12], refs[13]
    source, levels, ids, values, pairs, coarse, fine, table, field, hot, sems = refs[14:]
    moves = [
        (coarse_in, coarse),
        (fine_in, fine),
        (field_in, source),
        (table_in.at[0:FIRST_ROWS], table),
        (level_in, levels),
        (id_in, ids),
        (values_in, values),
        (pairs_in, pairs),
    ]
    copies = [pltpu.make_async_copy(*move, sems.at[i]) for i, move in enumerate(moves)]
    for copy in copies:
        copy.start()
    codes[...] = jnp.full_like(codes, -1)
    copies[0].wait()
    codes[COARSE_ROW : COARSE_ROW + 1, 0:CELLS] = coarse[...]
    copies[1].wait()
    codes[FINE_ROW : FINE_ROW + 4, 0:CELLS] = fine[...]
    hot_hanging(hot, codes)
    copies[2].wait()
    copies[3].wait()
    vector = padded_field(source, field)
    traces = stacked_traces(table.at[0:TRACE, 0:128], vector)
    up = [table.at[row : row + FACE, lane : lane + 128] for row, lane in PLACES["up"]]
    send_coarse, send_fine = gather_hanging(traces, hot, codes, up)
    swaps(vector[:, 0:SIDE], vector[:, CELLS - SIDE :], send_coarse, send_fine, *outs)
    for copy in copies[4:]:
        copy.wait()
    codes[0:2, 0:PAIRS] = pairs[...]
    place = lax.broadcasted_iota(jnp.int32, (values.shape[1], CELLS), 0)
    lookup = jnp.where(place == ids[...], 1.0, 0.0)
    coefficient = lax.dot_general(
        jnp.broadcast_to(values[...], (8, values.shape[1])),
        lookup,
        ALONG_ROWS,
        precision=lax.Precision.HIGHEST,
        preferred_element_type=F32,
    )
    level = levels[...]
    scale = jnp.where(level == 0, 1.0, jnp.where(level == 1, 0.5, 0.25))
    row = lax.broadcasted_iota(jnp.int32, scales.shape, 0)
    scales[...] = jnp.where(row == 0, coefficient * scale, scale * scale * scale)


def middle_kernel(
    field_ref, codes, scales, table_ref, applied_ref, trace_out_ref, coarse_out_ref, partner_ref, field
):
    table = views(table_ref)
    vector = padded_field(field_ref, field)
    high, low = face_traces(table["trace"], vector)
    both = high + low
    trace_out_ref[...] = both
    coarse_out_ref[...] = table_dot(table["coarse"], both)
    traces = jnp.concatenate([high.astype(BF16), low.astype(BF16)], axis=0)
    for start in range(0, PAIR_SLOTS, CHUNK):
        face, cell = extended_code(codes[1:2, start : start + CHUNK])
        partner_ref[:, start : start + CHUNK] = pick(dot(traces, one_hot(cell, CELLS)), face)
    stiff = table_dot(table["local"], vector)
    lumped = table["lumped"][0][...].astype(F32) + table["lumped"][1][...].astype(F32)
    applied_ref[...] = scales[0:1, :] * stiff + scales[1:2, :] * (lumped * vector)


def add_faces(
    codes,
    table_ref,
    applied_ref,
    trace_in_ref,
    coarse_in_ref,
    partner_ref,
    rim_chip_ref,
    dom_odd_ref,
    rim_core_ref,
    dom_even_ref,
    sides,
    hot,
    spread,
):
    table = views(table_ref)
    hot_hanging(hot, codes)
    first_core = lax.axis_index("core") == 0
    even_dom = lax.axis_index("x") % 2 == 0
    sides[:, 0:SIDE] = jnp.where(first_core, rim_chip_ref[...], rim_core_ref[...])
    sides[:, SIDE : 2 * SIDE] = jnp.where(first_core, rim_core_ref[...], rim_chip_ref[...])
    arriving = jnp.where(even_dom, dom_odd_ref[...], dom_even_ref[...])
    returned = jnp.where(even_dom, dom_even_ref[...], dom_odd_ref[...])
    side_traces = stacked_traces(table["trace"], sides[...])

    def put(start, value, face, coarse):
        width = value.shape[1]
        high = value.astype(BF16).astype(F32)
        low = value - high
        for f in range(6):
            live = face == f
            spread[f * FACE : (f + 1) * FACE, start : start + width] = jnp.where(live, high, 0.0).astype(BF16)
            spread[TRACE + f * FACE : TRACE + (f + 1) * FACE, start : start + width] = jnp.where(
                live, low, 0.0
            ).astype(BF16)
        row = lax.broadcasted_iota(jnp.int32, (16, width), 0)
        spread[2 * TRACE : 2 * TRACE + 16, start : start + width] = jnp.where(
            row == (face + 8 if coarse else face), 1.0, 0.0
        ).astype(BF16)

    for start in range(0, PAIR_SLOTS, CHUNK):
        face, cell = extended_code(codes[1:2, start : start + CHUNK])
        place = jnp.where(cell < 0, cell + SIDE, jnp.where(cell >= CELLS, cell + (SIDE - CELLS), -1))
        place = jnp.where(face < 0, -1, place)
        partner = partner_ref[:, start : start + CHUNK] + pick(
            dot(side_traces, one_hot(place, 2 * SIDE)), face
        )
        face, cell = own_code(codes[0:1, start : start + CHUNK])
        hot[:, start : start + CHUNK] = one_hot(cell, CELLS)
        put(start, -TAU_PENALTY * partner, face, False)
    predicted = table_dot(table["down"], arriving)
    for child in range(4):
        face, _ = fine_code(codes, child)
        put(FINE0 + child * CELLS, predicted[child * FACE : (child + 1) * FACE], face, False)
    face, _ = coarse_code(codes)
    put(COARSE0, returned, face, True)
    added = dot(spread[...], hot[...], ALONG_LANES)
    pieces = []
    for f in range(6):
        rows = slice(f * FACE, (f + 1) * FACE)
        fine_count = added[2 * TRACE + f : 2 * TRACE + f + 1]
        coarse_count = added[2 * TRACE + 8 + f : 2 * TRACE + 9 + f]
        pieces.append(
            added[f * FACE : (f + 1) * FACE]
            + added[TRACE + f * FACE : TRACE + (f + 1) * FACE]
            + (TAU_PENALTY * fine_count) * trace_in_ref[rows, :]
            + coarse_count * coarse_in_ref[rows, :]
        )
    high, low = split(jnp.concatenate(pieces, axis=0))
    untrace = table["untrace"][...]
    return applied_ref[...] + (dot(untrace, high) + dot(untrace, low))


def image_kernel(*refs):
    codes, table = refs[0], views(refs[1])
    image = add_faces(*refs[:10], *refs[15:])
    refs[10][...] = image
    traces = stacked_traces(table["trace"], image)
    send_coarse, send_fine = gather_hanging(traces, refs[16], codes, table["up"])
    swaps(image[:, 0:SIDE], image[:, CELLS - SIDE :], send_coarse, send_fine, *refs[11:15])


def total(value):
    return jnp.sum(jnp.sum(value, axis=0, keepdims=True), axis=1, keepdims=True)


def moments_kernel(*refs):
    source_ref, image_ref, out_ref, sums_ref = refs[10:14]
    second = add_faces(*refs[:10], *refs[14:])
    out_ref[...] = second
    source = source_ref[...]
    image = image_ref[...]
    products = [
        source * source,
        source * image[0:125],
        image * image,
        source * second[0:125],
        image * second,
    ]
    lane = lax.broadcasted_iota(jnp.int32, (1, 128), 1)
    line = jnp.zeros((1, 128), F32)
    for index, product in enumerate(products):
        line = line + jnp.where(lane == index, total(product), 0.0)
    sums_ref[...] = jnp.broadcast_to(line[None], sums_ref.shape)


def last_kernel(sums_ref, source_ref, image_ref, second_ref, solution_ref, residual_ref):
    line = jnp.sum(sums_ref[...], axis=0)
    rr, rw, ww, ru, wu = (line[:, i : i + 1] for i in range(5))
    first_step = rr / rw
    rr_next = rr - 2.0 * first_step * rw + first_step * first_step * ww
    grown = 1.0 + rr_next / rr
    curvature = (
        grown * grown * rw - first_step * grown * (ru + ww) + first_step * first_step * wu
    )
    second_step = rr_next / curvature
    p = first_step + second_step * grown
    q = second_step * first_step
    source = source_ref[...]
    image = image_ref[0:125, :]
    solution_ref[...] = p * source - q * image
    residual_ref[...] = source - p * image + q * second_ref[0:125, :]


def call(kernel, out_shapes, scratch, *operands, name, space=pltpu.VMEM, limit=48):
    return pl.pallas_call(
        kernel,
        out_shape=[jax.ShapeDtypeStruct(shape, F32) for shape in out_shapes]
        if isinstance(out_shapes[0], tuple)
        else out_shapes,
        in_specs=[pl.BlockSpec(memory_space=space)] * len(operands),
        out_specs=[pl.BlockSpec(memory_space=pltpu.VMEM)] * len(out_shapes),
        scratch_shapes=scratch,
        compiler_params=pltpu.CompilerParams(vmem_limit_bytes=limit * 1024 * 1024),
        name=name,
    )(*operands)


FIELD = pltpu.VMEM((128, CELLS), F32)
SIDES = pltpu.VMEM((128, 2 * SIDE), F32)
HOT = pltpu.VMEM((CELLS, SLOTS), BF16)
SPREAD = pltpu.VMEM((2 * TRACE + 16, SLOTS), BF16)


def swapped(value, axes, first):
    count = lax.axis_size(axes)
    pairs = [(i, i + 1) for i in range(first, count - 1, 2)]
    return lax.ppermute(value, axes, pairs + [(above, below) for below, above in pairs])


def exchange(rim_chip, dom_odd, rim_core, dom_even):
    rim_chip = swapped(rim_chip, BLOCK, 1)
    dom_odd = swapped(dom_odd, DOM, 1)
    dom_even = swapped(dom_even, DOM, 0)
    rim_core = swapped(rim_core, BLOCK, 0)
    return rim_chip, dom_odd, rim_core, dom_even


def summed_over_blocks(sums):
    in_plane, along_z = lax.axis_size(PLANE), lax.axis_size("z")
    sums = lax.all_to_all(sums, PLANE, 0, 0, tiled=True)
    diagonal = [
        (z * in_plane + place, (z + place) % along_z * in_plane + place)
        for z in range(along_z)
        for place in range(along_z)
    ]
    other = lax.ppermute(jnp.sum(sums, axis=0, keepdims=True), BLOCK, diagonal)
    return lax.all_to_all(jnp.broadcast_to(other, sums.shape), PLANE, 0, 0, tiled=True)


def on_device(source, levels, ids, values, pairs, coarse, fine):
    levels, ids, values, coarse = (a.reshape(1, -1) for a in (levels, ids, values, coarse))
    table = jnp.asarray(packed_table())
    sends = [jax.ShapeDtypeStruct(shape, F32) for shape in [(128, SIDE), (FACE, CELLS)] * 2]
    params = (source, levels, ids, values, pairs, coarse, fine)
    *swapping, codes, scales = call(
        first_kernel,
        [
            *sends,
            jax.ShapeDtypeStruct((8, PAIR_SLOTS), jnp.int32),
            jax.ShapeDtypeStruct((8, CELLS), F32),
        ],
        [
            *(pltpu.VMEM(a.shape, a.dtype) for a in params),
            pltpu.VMEM((FIRST_ROWS, 256), BF16),
            FIELD,
            HOT,
            pltpu.SemaphoreType.DMA((8,)),
        ],
        *params,
        table,
        name="first",
        space=pl.ANY,
        limit=63,
    )

    def middle(field):
        shapes = [(128, CELLS), (TRACE, CELLS), (TRACE, CELLS), (FACE, PAIR_SLOTS)]
        return call(middle_kernel, shapes, [FIELD], field, codes, scales, table, name="middle")

    scratch = [SIDES, HOT, SPREAD]
    arrived = exchange(*swapping)
    image, *swapping = call(
        image_kernel,
        [jax.ShapeDtypeStruct((128, CELLS), F32), *sends],
        scratch,
        codes,
        table,
        *middle(source),
        *arrived,
        name="image",
    )
    arrived = exchange(*swapping)
    second, sums = call(
        moments_kernel,
        [(128, CELLS), (lax.axis_size(PLANE), 1, 128)],
        scratch,
        codes,
        table,
        *middle(image),
        *arrived,
        source,
        image,
        name="moments",
    )
    sums = summed_over_blocks(sums)
    return tuple(call(last_kernel, [source.shape] * 2, [], sums, source, image, second, name="last"))


def solution(mesh):
    dom, sub = mesh.devices.shape
    axes = BLOCK
    fine_mesh = Mesh(mesh.devices.reshape(dom // 4, 4, sub // 2, 2), axes)
    return jax.shard_map(
        on_device,
        mesh=fine_mesh,
        in_specs=(
            P(None, axes),
            P(axes),
            P(axes),
            P(),
            P(None, axes),
            P(axes),
            P(None, axes),
        ),
        out_specs=(P(None, axes), P(None, axes)),
        check_vma=False,
    )
```

time: 123 us -> 99.7 us (0.81)
  blocking collectives: 69.1 us -> 35.1 us
  waiting for transfers between devices: 2.5 us -> 18.4 us
  starting transfers between devices: 34 us -> 30.1 us
  local copies, waits for them, and re-layouts: 4.48 us -> 1.49 us
  Pallas kernels: 11.3 us -> 13.2 us
    all_to_all x2, blocking collectives: 69.1 us -> 35.1 us  [the longest x1 21.5 us: summed_over_blocks(): lax.all_to_all(jnp.broadcast_to(other, sums.shape), PLANE, 0, 0, tiled=True)]
    ppermute x8 -> x9, waiting for transfers between devices: 2.5 us -> 18.4 us  [the longest x1 15.8 us: summed_over_blocks(): other = lax.ppermute(jnp.sum(sums, axis=0, keepdims=True), BLOCK, diagonal)]
    ppermute x8 -> x9, starting transfers between devices: 34 us -> 30.1 us  [the longest x8 27.8 us: swapped(): lax.ppermute(value, axes, pairs + [(above, below) for below, above in pai...]
    unnamed x42 -> x10, local copies, waits for them, and re-layouts: 4.46 us -> 1.48 us
    pallas_call x6, Pallas kernels: 11.3 us -> 13.2 us  [call(): pl.pallas_call(kernel, out_shape=[jax.ShapeDtypeStruct(shape, F32) for sh...]
  transfers between devices with their start and end apart: 8 -> 9, of which waited for: 1 -> 3; matrix products, arithmetic and copies ran while one was open for 0% -> 0% of each run, Pallas kernels for 2% -> 2%
where the time goes in v2:
time: 99.7 us; the launch traced here: 99.1 us
  blocking collectives  35.1 us (35%)
  starting transfers between devices  30.1 us (30%)
  waiting for transfers between devices  18.4 us (18%)
  Pallas kernels  13.2 us (13%)
  local copies, waits for them, and re-layouts  1.49 us (1%)
    ppermute x8, starting transfers between devices, swapped(): lax.ppermute(value, axes, pairs + [(above, below) for below, above in pai...  27.8 us
    all_to_all x1, blocking collectives, summed_over_blocks(): lax.all_to_all(jnp.broadcast_to(other, sums.shape), PLANE, 0, 0, tiled=True)  21.5 us
    ppermute x1, waiting for transfers between devices, summed_over_blocks(): other = lax.ppermute(jnp.sum(sums, axis=0, keepdims=True), BLOCK, diagonal)  15.8 us
    all_to_all x1, blocking collectives, summed_over_blocks(): sums = lax.all_to_all(sums, PLANE, 0, 0, tiled=True)  13.6 us
    pallas_call x6, Pallas kernels, call(): pl.pallas_call(kernel, out_shape=[jax.ShapeDtypeStruct(shape, F32) for sh...  13.2 us
    ppermute x8, waiting for transfers between devices, swapped(): lax.ppermute(value, axes, pairs + [(above, below) for below, above in pai...  2.54 us
    ppermute x1, starting transfers between devices, summed_over_blocks(): other = lax.ppermute(jnp.sum(sums, axis=0, keepdims=True), BLOCK, diagonal)  2.28 us
  transfers between devices with their start and end apart: 9, of which 3 were waited for; matrix products, arithmetic and copies ran while one was open for 0% of the time, Pallas kernels for 2%

profile of v2, /device:TPU:1, one launch (start us, length us, event | category | flops | bytes accessed | tf_op | source)
XLA Modules:
  0.0 99.1 jit_solution(19176157252631654)
XLA Ops:
  0.6 0.0 copy-start
  0.7 3.7 %first.1 = (f32[128,128]{1,0:T(8,128)}, f32[32,512]{1,0:T(8,128)}, f32[128,128]{1,0:T(8,128)}, f32[32,512]{1,0:T(8,128)}, s32[8,1024]{1,0:T(8,128)}, /*index=5*/f32[8,512]{1,0:T(8,128)}) custom-call(f32[125,512]{1,0:T(8,128)} %source_ref.1, s32[1,512]{1,0:T(1,128)} %bitcast.6, s32[1,512]{1,0:T(1,128)} %bitcast.7, f32[1,64]{1,0:T(1,128)} %bitcast.9, ...), custom_call_target="tpu_custom_call" | custom-call | tf_op jit(solution)/shard_map/first/pallas_call | solution.py:430
  4.3 4.6 %collective-permute-start = (f32[128,128]{1,0:T(8,128)}, f32[128,128]{1,0:T(8,128)S(1)}, u32[]{:S(2)}, u32[]{:S(2)}) collective-permute-start(f32[128,128]{1,0:T(8,128)} %get-tuple-element.29), channel_id=1, source_target_pairs={{1,2},{3,4},{5,6},{7,8},{9,10},{11,12},{13,14},{15,16},{17,18},{19... | collective-permute-start | bytes 196616 | tf_op jit(solution)/shard_map/ppermute | solution.py:452
  8.9 0.7 collective-permute-start.1
  9.6 12.1 %collective-permute-start.2 = (f32[128,128]{1,0:T(8,128)}, f32[128,128]{1,0:T(8,128)S(1)}, u32[]{:S(2)}, u32[]{:S(2)}) collective-permute-start(f32[128,128]{1,0:T(8,128)} %get-tuple-element.31), channel_id=1, source_target_pairs={{0,1},{2,3},{4,5},{6,7},{8,9},{10,11},{12,13},{14,15},{16,17},{18,... | collective-permute-start | bytes 196616 | tf_op jit(solution)/shard_map/ppermute | solution.py:452
  21.7 1.9 %collective-permute-start.3 = (f32[32,512]{1,0:T(8,128)}, f32[32,512]{1,0:T(8,128)S(1)}, u32[]{:S(2)}, u32[]{:S(2)}) collective-permute-start(f32[32,512]{1,0:T(8,128)} %get-tuple-element.32), channel_id=1, source_target_pairs={{0,8},{16,24},{32,40},{48,56},{64,72},{80,88},{96,104},{112,120},{... | collective-permute-start | bytes 196616 | tf_op jit(solution)/shard_map/ppermute | solution.py:452
  23.7 0.7 copy-done.2
  24.5 0.7 copy-done.3
  25.2 1.1 %middle.2 = (f32[128,512]{1,0:T(8,128)S(1)}, f32[192,512]{1,0:T(8,128)S(1)}, f32[192,512]{1,0:T(8,128)S(1)}, f32[32,1024]{1,0:T(8,128)S(1)}) custom-call(f32[125,512]{1,0:T(8,128)S(1)} %copy-done.1, s32[8,1024]{1,0:T(8,128)S(1)} %copy-done.2, f32[8,512]{1,0:T(8,128)S(1)} %copy-done.3, bf16[1120,256]{1,0:T(8,128)(2,1)S(1)} %copy-done), custom_call_target="tpu_custom_call" | custom-call | tf_op jit(solution)/shard_map/middle/pallas_call | solution.py:430
  26.3 1.3 %collective-permute-done.3.refs_9_ = f32[32,512]{1,0:T(8,128)S(1)} collective-permute-done((f32[32,512]{1,0:T(8,128)}, f32[32,512]{1,0:T(8,128)S(1)}, u32[]{:S(2)}, u32[]{:S(2)}) %collective-permute-start.3) | collective-permute-done | bytes 65568 | tf_op jit(solution)/shard_map/ppermute | solution.py:452
  27.6 3.8 %image.1 = (f32[128,512]{1,0:T(8,128)S(1)}, f32[128,128]{1,0:T(8,128)S(1)}, f32[32,512]{1,0:T(8,128)S(1)}, f32[128,128]{1,0:T(8,128)S(1)}, f32[32,512]{1,0:T(8,128)S(1)}) custom-call(s32[8,1024]{1,0:T(8,128)S(1)} %copy-done.2, bf16[1120,256]{1,0:T(8,128)(2,1)S(1)} %copy-done, f32[128,512]{1,0:T(8,128)S(1)} %get-tuple-element.25.refs_2_, ...), custom_call_target="tpu_custom_call" | custom-call | tf_op jit(solution)/shard_map/image/pallas_call | solution.py:430
  31.3 1.9 %collective-permute-start.4 = (f32[128,128]{1,0:T(8,128)S(1)}, f32[128,128]{1,0:T(8,128)S(1)}, u32[]{:S(2)}, u32[]{:S(2)}) collective-permute-start(f32[128,128]{1,0:T(8,128)S(1)} %get-tuple-element.38), channel_id=1, source_target_pairs={{1,2},{3,4},{5,6},{7,8},{9,10},{11,12},{13,14},{15,16},{17,18},{19... | collective-permute-start | bytes 196616 | tf_op jit(solution)/shard_map/ppermute | solution.py:452
  33.3 0.7 collective-permute-start.5
  33.9 1.9 %collective-permute-start.6 = (f32[128,128]{1,0:T(8,128)S(1)}, f32[128,128]{1,0:T(8,128)S(1)}, u32[]{:S(2)}, u32[]{:S(2)}) collective-permute-start(f32[128,128]{1,0:T(8,128)S(1)} %get-tuple-element.40), channel_id=1, source_target_pairs={{0,1},{2,3},{4,5},{6,7},{8,9},{10,11},{12,13},{14,15},{16,17},{18,... | collective-permute-start | bytes 196616 | tf_op jit(solution)/shard_map/ppermute | solution.py:452
  35.9 4.0 %collective-permute-start.7 = (f32[32,512]{1,0:T(8,128)S(1)}, f32[32,512]{1,0:T(8,128)S(1)}, u32[]{:S(2)}, u32[]{:S(2)}) collective-permute-start(f32[32,512]{1,0:T(8,128)S(1)} %get-tuple-element.41), channel_id=1, source_target_pairs={{0,8},{16,24},{32,40},{48,56},{64,72},{80,88},{96,104},{112,120},{... | collective-permute-start | bytes 196616 | tf_op jit(solution)/shard_map/ppermute | solution.py:452
  39.9 1.1 %middle.3 = (f32[128,512]{1,0:T(8,128)S(1)}, f32[192,512]{1,0:T(8,128)S(1)}, f32[192,512]{1,0:T(8,128)S(1)}, f32[32,1024]{1,0:T(8,128)S(1)}) custom-call(f32[128,512]{1,0:T(8,128)S(1)} %get-tuple-element.33.field_ref.refs_11_.image_ref, s32[8,1024]{1,0:T(8,128)S(1)} %copy-done.2, f32[8,512]{1,0:T(8,128)S(1)} %copy-done.4, bf16[1120,256]{1,0:T(8,128)(2,1)S(1)} %copy-done), custom_call_target="tpu_custom_call" | custom-call | tf_op jit(solution)/shard_map/middle/pallas_call | solution.py:430
  41.0 1.2 %collective-permute-done.7.refs_9_ = f32[32,512]{1,0:T(8,128)S(1)} collective-permute-done((f32[32,512]{1,0:T(8,128)S(1)}, f32[32,512]{1,0:T(8,128)S(1)}, u32[]{:S(2)}, u32[]{:S(2)}) %collective-permute-start.7) | collective-permute-done | bytes 65568 | tf_op jit(solution)/shard_map/ppermute | solution.py:452
  42.2 2.5 %moments.1 = (f32[128,512]{1,0:T(8,128)S(1)}, f32[32,1,128]{2,1,0:T(1,128)S(1)}) custom-call(s32[8,1024]{1,0:T(8,128)S(1)} %copy-done.2, bf16[1120,256]{1,0:T(8,128)(2,1)S(1)} %copy-done, f32[128,512]{1,0:T(8,128)S(1)} %get-tuple-element.34.refs_2_, f32[192,512]{1,0:T(8,128)S(1)} %get-tuple-element.35.refs_3_, f32[192,512]{1,0:T(8,128)S(1)} %get-tuple-element.36.refs_4_, ...), custom_call_target="tpu_custom_call" | custom-call | tf_op jit(solution)/shard_map/moments/pallas_call | solution.py:430
  44.8 13.6 %all_to_all.10 = f32[32,1,128]{2,1,0:T(1,128)S(1)} all-to-all(f32[32,1,128]{2,1,0:T(1,128)S(1)} %get-tuple-element.42), channel_id=1, replica_groups=mesh['z'=32,'x'=4,'y'=4,'core'=2] {'x','y','core'}, dimensions={0} | all-to-all | bytes 32768 | tf_op jit(solution)/shard_map/all_to_all | solution.py:465
  58.3 0.1 reduce_sum.9
  58.4 2.3 %collective-permute-start.8 = (f32[1,1,128]{2,1,0:T(1,128)S(1)}, f32[1,1,128]{2,1,0:T(1,128)S(1)}, u32[]{:S(2)}, u32[]{:S(2)}) collective-permute-start(f32[1,1,128]{2,1,0:T(1,128)S(1)} %bitcast.10), channel_id=1, source_target_pairs={{0,0},{1,33},{2,66},{3,99},{4,132},{5,165},{6,198},{7,231},{8,264}... | collective-permute-start | bytes 1544 | tf_op jit(solution)/shard_map/ppermute | solution.py:471
  60.7 15.8 %collective-permute-done.8 = f32[1,1,128]{2,1,0:T(1,128)S(1)} collective-permute-done((f32[1,1,128]{2,1,0:T(1,128)S(1)}, f32[1,1,128]{2,1,0:T(1,128)S(1)}, u32[]{:S(2)}, u32[]{:S(2)}) %collective-permute-start.8) | collective-permute-done | bytes 544 | tf_op jit(solution)/shard_map/ppermute | solution.py:471
  76.5 21.5 %all_to_all.11.sums_ref = f32[32,1,128]{2,1,0:T(1,128)S(1)} all-to-all(f32[32,1,128]{2,1,0:T(1,128)S(1)} %broadcast_in_dim.12), channel_id=1, replica_groups=mesh['z'=32,'x'=4,'y'=4,'core'=2] {'x','y','core'}, dimensions={0} | all-to-all | bytes 32768 | tf_op jit(solution)/shard_map/all_to_all | solution.py:472
  98.1 1.1 %last.1 = (f32[125,512]{1,0:T(8,128)}, f32[125,512]{1,0:T(8,128)}) custom-call(f32[32,1,128]{2,1,0:T(1,128)S(1)} %all_to_all.11.sums_ref, f32[125,512]{1,0:T(8,128)S(1)} %copy-done.1, f32[128,512]{1,0:T(8,128)S(1)} %get-tuple-element.33.field_ref.refs_11_.image_ref, f32[128,512]{1,0:T(8,128)S(1)} %get-tuple-element.43.second_ref), custom_call_target="tpu_custom_call" | custom-call | tf_op jit(solution)/shard_map/last/pallas_call | solution.py:430
  (14 shorter events, 0.0 us)
Async XLA Ops:
  0.6 23.0 %copy-start = (bf16[1120,256]{1,0:T(8,128)(2,1)S(1)}, bf16[1120,256]{1,0:T(8,128)(2,1)}, u32[]{:S(2)}) copy-start(bf16[1120,256]{1,0:T(8,128)(2,1)} %constant.4.clone.refs_7_.table_ref.refs_1_) | copy-start | bytes 1720324
  0.6 23.0 %copy-start.1 = (f32[125,512]{1,0:T(8,128)S(1)}, f32[125,512]{1,0:T(8,128)}, u32[]{:S(2)}) copy-start(f32[125,512]{1,0:T(8,128)} %source_ref.1) | copy-start | bytes 768004
  4.3 21.9 %collective-permute-start = (f32[128,128]{1,0:T(8,128)}, f32[128,128]{1,0:T(8,128)S(1)}, u32[]{:S(2)}, u32[]{:S(2)}) collective-permute-start(f32[128,128]{1,0:T(8,128)} %get-tuple-element.29), channel_id=1, source_target_pairs={{1,2},{3,4},{5,6},{7,8},{9,10},{11,12},{13,14},{15,16},{17,18},{19... | collective-permute-start | bytes 196616 | tf_op jit(solution)/shard_map/ppermute | solution.py:452
  8.9 17.3 %collective-permute-start.1 = (f32[32,512]{1,0:T(8,128)}, f32[32,512]{1,0:T(8,128)S(1)}, u32[]{:S(2)}, u32[]{:S(2)}) collective-permute-start(f32[32,512]{1,0:T(8,128)} %get-tuple-element.30), channel_id=1, source_target_pairs={{8,16},{24,32},{40,48},{56,64},{72,80},{88,96},{104,112},{120,128}... | collective-permute-start | bytes 196616 | tf_op jit(solution)/shard_map/ppermute | solution.py:452
  9.6 16.7 %collective-permute-start.2 = (f32[128,128]{1,0:T(8,128)}, f32[128,128]{1,0:T(8,128)S(1)}, u32[]{:S(2)}, u32[]{:S(2)}) collective-permute-start(f32[128,128]{1,0:T(8,128)} %get-tuple-element.31), channel_id=1, source_target_pairs={{0,1},{2,3},{4,5},{6,7},{8,9},{10,11},{12,13},{14,15},{16,17},{18,... | collective-permute-start | bytes 196616 | tf_op jit(solution)/shard_map/ppermute | solution.py:452
  21.7 5.8 %collective-permute-start.3 = (f32[32,512]{1,0:T(8,128)}, f32[32,512]{1,0:T(8,128)S(1)}, u32[]{:S(2)}, u32[]{:S(2)}) collective-permute-start(f32[32,512]{1,0:T(8,128)} %get-tuple-element.32), channel_id=1, source_target_pairs={{0,8},{16,24},{32,40},{48,56},{64,72},{80,88},{96,104},{112,120},{... | collective-permute-start | bytes 196616 | tf_op jit(solution)/shard_map/ppermute | solution.py:452
  23.7 0.8 copy-start.2
  24.4 0.7 copy-start.3
  27.6 12.3 %copy-start.4 = (f32[8,512]{1,0:T(8,128)S(1)}, f32[8,512]{1,0:T(8,128)}, u32[]{:S(2)}) copy-start(f32[8,512]{1,0:T(8,128)} %get-tuple-element.24.scales) | copy-start | bytes 49156
  31.3 9.6 %collective-permute-start.4 = (f32[128,128]{1,0:T(8,128)S(1)}, f32[128,128]{1,0:T(8,128)S(1)}, u32[]{:S(2)}, u32[]{:S(2)}) collective-permute-start(f32[128,128]{1,0:T(8,128)S(1)} %get-tuple-element.38), channel_id=1, source_target_pairs={{1,2},{3,4},{5,6},{7,8},{9,10},{11,12},{13,14},{15,16},{17,18},{19... | collective-permute-start | bytes 196616 | tf_op jit(solution)/shard_map/ppermute | solution.py:452
  33.3 7.7 %collective-permute-start.5 = (f32[32,512]{1,0:T(8,128)S(1)}, f32[32,512]{1,0:T(8,128)S(1)}, u32[]{:S(2)}, u32[]{:S(2)}) collective-permute-start(f32[32,512]{1,0:T(8,128)S(1)} %get-tuple-element.39), channel_id=1, source_target_pairs={{8,16},{24,32},{40,48},{56,64},{72,80},{88,96},{104,112},{120,128}... | collective-permute-start | bytes 196616 | tf_op jit(solution)/shard_map/ppermute | solution.py:452
  33.9 7.0 %collective-permute-start.6 = (f32[128,128]{1,0:T(8,128)S(1)}, f32[128,128]{1,0:T(8,128)S(1)}, u32[]{:S(2)}, u32[]{:S(2)}) collective-permute-start(f32[128,128]{1,0:T(8,128)S(1)} %get-tuple-element.40), channel_id=1, source_target_pairs={{0,1},{2,3},{4,5},{6,7},{8,9},{10,11},{12,13},{14,15},{16,17},{18,... | collective-permute-start | bytes 196616 | tf_op jit(solution)/shard_map/ppermute | solution.py:452
  35.9 6.3 %collective-permute-start.7 = (f32[32,512]{1,0:T(8,128)S(1)}, f32[32,512]{1,0:T(8,128)S(1)}, u32[]{:S(2)}, u32[]{:S(2)}) collective-permute-start(f32[32,512]{1,0:T(8,128)S(1)} %get-tuple-element.41), channel_id=1, source_target_pairs={{0,8},{16,24},{32,40},{48,56},{64,72},{80,88},{96,104},{112,120},{... | collective-permute-start | bytes 196616 | tf_op jit(solution)/shard_map/ppermute | solution.py:452
  58.4 18.1 %collective-permute-start.8 = (f32[1,1,128]{2,1,0:T(1,128)S(1)}, f32[1,1,128]{2,1,0:T(1,128)S(1)}, u32[]{:S(2)}, u32[]{:S(2)}) collective-permute-start(f32[1,1,128]{2,1,0:T(1,128)S(1)} %bitcast.10), channel_id=1, source_target_pairs={{0,0},{1,33},{2,66},{3,99},{4,132},{5,165},{6,198},{7,231},{8,264}... | collective-permute-start | bytes 1544 | tf_op jit(solution)/shard_map/ppermute | solution.py:471

commit v3 on v2

--- a/solution.py
+++ b/solution.py
@@ -21,6 +21,8 @@
 CHUNK = 512
 FINE_ROW = 2
 COARSE_ROW = 6
+SCALE_ROW = 8
+PACKED = (16, PAIR_SLOTS)
 TAU_PENALTY = 2.0
 SIGMA_MASS = 4.0
 BLOCK = ("z", "x", "y", "core")
@@ -175,10 +177,12 @@
 
 
 def own_code(code):
+    code = code.astype(jnp.int32)
     return code >> 9, code & (CELLS - 1)
 
 
 def extended_code(code):
+    code = code.astype(jnp.int32)
     face = jnp.where(code < 0, -1, 0)
     for f in range(1, 6):
         face = face + jnp.where(code >= f * EXTENT, 1, 0)
@@ -213,6 +217,12 @@
     return send_coarse, send_fine
 
 
+def hot_pairs(hot, codes):
+    for start in range(0, PAIR_SLOTS, CHUNK):
+        _, cell = own_code(codes[0:1, start : start + CHUNK])
+        hot[:, start : start + CHUNK] = one_hot(cell, CELLS)
+
+
 def hot_hanging(hot, codes):
     for child in range(4):
         _, cell = fine_code(codes, child)
@@ -227,7 +237,7 @@
     return jnp.concatenate([high.astype(BF16), low.astype(BF16)], axis=0)
 
 
-def swaps(low, high, send_coarse, send_fine, rim_chip_ref, dom_odd_ref, rim_core_ref, dom_even_ref):
+def swaps(low, high, send_coarse, send_fine, rim_chip_ref, dom_odd_ref, dom_even_ref, rim_core_ref):
     first_core = lax.axis_index("core") == 0
     even_dom = lax.axis_index("x") % 2 == 0
     rim_core_ref[...] = jnp.where(first_core, high, low)
@@ -238,8 +248,8 @@
 
 def first_kernel(*refs):
     field_in, level_in, id_in, values_in, pairs_in, coarse_in, fine_in, table_in = refs[:8]
-    outs, codes, scales = refs[8:12], refs[12], refs[13]
-    source, levels, ids, values, pairs, coarse, fine, table, field, hot, sems = refs[14:]
+    outs, codes = refs[8:12], refs[12]
+    source, levels, ids, values, pairs, coarse, fine, table, field, hot, sems = refs[13:]
     moves = [
         (coarse_in, coarse),
         (fine_in, fine),
@@ -253,11 +263,11 @@
     copies = [pltpu.make_async_copy(*move, sems.at[i]) for i, move in enumerate(moves)]
     for copy in copies:
         copy.start()
-    codes[...] = jnp.full_like(codes, -1)
+    codes[...] = jnp.full(codes.shape, -1.0, F32)
     copies[0].wait()
-    codes[COARSE_ROW : COARSE_ROW + 1, 0:CELLS] = coarse[...]
+    codes[COARSE_ROW : COARSE_ROW + 1, 0:CELLS] = coarse[...].astype(F32)
     copies[1].wait()
-    codes[FINE_ROW : FINE_ROW + 4, 0:CELLS] = fine[...]
+    codes[FINE_ROW : FINE_ROW + 4, 0:CELLS] = fine[...].astype(F32)
     hot_hanging(hot, codes)
     copies[2].wait()
     copies[3].wait()
@@ -268,7 +278,7 @@
     swaps(vector[:, 0:SIDE], vector[:, CELLS - SIDE :], send_coarse, send_fine, *outs)
     for copy in copies[4:]:
         copy.wait()
-    codes[0:2, 0:PAIRS] = pairs[...]
+    codes[0:2, 0:PAIRS] = pairs[...].astype(F32)
     place = lax.broadcasted_iota(jnp.int32, (values.shape[1], CELLS), 0)
     lookup = jnp.where(place == ids[...], 1.0, 0.0)
     coefficient = lax.dot_general(
@@ -280,12 +290,12 @@
     )
     level = levels[...]
     scale = jnp.where(level == 0, 1.0, jnp.where(level == 1, 0.5, 0.25))
-    row = lax.broadcasted_iota(jnp.int32, scales.shape, 0)
-    scales[...] = jnp.where(row == 0, coefficient * scale, scale * scale * scale)
+    codes[SCALE_ROW : SCALE_ROW + 1, 0:CELLS] = coefficient[0:1] * scale
+    codes[SCALE_ROW + 1 : SCALE_ROW + 2, 0:CELLS] = scale * scale * scale
 
 
 def middle_kernel(
-    field_ref, codes, scales, table_ref, applied_ref, trace_out_ref, coarse_out_ref, partner_ref, field
+    field_ref, codes, table_ref, applied_ref, trace_out_ref, coarse_out_ref, partner_ref, field
 ):
     table = views(table_ref)
     vector = padded_field(field_ref, field)
@@ -299,7 +309,9 @@
         partner_ref[:, start : start + CHUNK] = pick(dot(traces, one_hot(cell, CELLS)), face)
     stiff = table_dot(table["local"], vector)
     lumped = table["lumped"][0][...].astype(F32) + table["lumped"][1][...].astype(F32)
-    applied_ref[...] = scales[0:1, :] * stiff + scales[1:2, :] * (lumped * vector)
+    factor = codes[SCALE_ROW : SCALE_ROW + 1, 0:CELLS]
+    cubed = codes[SCALE_ROW + 1 : SCALE_ROW + 2, 0:CELLS]
+    applied_ref[...] = factor * stiff + cubed * (lumped * vector)
 
 
 def add_faces(
@@ -311,13 +323,14 @@
     partner_ref,
     rim_chip_ref,
     dom_odd_ref,
+    dom_even_ref,
     rim_core_ref,
-    dom_even_ref,
     sides,
     hot,
     spread,
 ):
     table = views(table_ref)
+    hot_pairs(hot, codes)
     hot_hanging(hot, codes)
     first_core = lax.axis_index("core") == 0
     even_dom = lax.axis_index("x") % 2 == 0
@@ -349,8 +362,7 @@
         partner = partner_ref[:, start : start + CHUNK] + pick(
             dot(side_traces, one_hot(place, 2 * SIDE)), face
         )
-        face, cell = own_code(codes[0:1, start : start + CHUNK])
-        hot[:, start : start + CHUNK] = one_hot(cell, CELLS)
+        face, _ = own_code(codes[0:1, start : start + CHUNK])
         put(start, -TAU_PENALTY * partner, face, False)
     predicted = table_dot(table["down"], arriving)
     for child in range(4):
@@ -429,9 +441,7 @@
 def call(kernel, out_shapes, scratch, *operands, name, space=pltpu.VMEM, limit=48):
     return pl.pallas_call(
         kernel,
-        out_shape=[jax.ShapeDtypeStruct(shape, F32) for shape in out_shapes]
-        if isinstance(out_shapes[0], tuple)
-        else out_shapes,
+        out_shape=[jax.ShapeDtypeStruct(shape, F32) for shape in out_shapes],
         in_specs=[pl.BlockSpec(memory_space=space)] * len(operands),
         out_specs=[pl.BlockSpec(memory_space=pltpu.VMEM)] * len(out_shapes),
         scratch_shapes=scratch,
@@ -452,12 +462,12 @@
     return lax.ppermute(value, axes, pairs + [(above, below) for below, above in pairs])
 
 
-def exchange(rim_chip, dom_odd, rim_core, dom_even):
+def exchange(rim_chip, dom_odd, dom_even, rim_core):
     rim_chip = swapped(rim_chip, BLOCK, 1)
     dom_odd = swapped(dom_odd, DOM, 1)
     dom_even = swapped(dom_even, DOM, 0)
     rim_core = swapped(rim_core, BLOCK, 0)
-    return rim_chip, dom_odd, rim_core, dom_even
+    return rim_chip, dom_odd, dom_even, rim_core
 
 
 def summed_over_blocks(sums):
@@ -475,15 +485,11 @@
 def on_device(source, levels, ids, values, pairs, coarse, fine):
     levels, ids, values, coarse = (a.reshape(1, -1) for a in (levels, ids, values, coarse))
     table = jnp.asarray(packed_table())
-    sends = [jax.ShapeDtypeStruct(shape, F32) for shape in [(128, SIDE), (FACE, CELLS)] * 2]
+    sends = [(128, SIDE), (FACE, CELLS), (FACE, CELLS), (128, SIDE)]
     params = (source, levels, ids, values, pairs, coarse, fine)
-    *swapping, codes, scales = call(
+    *swapping, codes = call(
         first_kernel,
-        [
-            *sends,
-            jax.ShapeDtypeStruct((8, PAIR_SLOTS), jnp.int32),
-            jax.ShapeDtypeStruct((8, CELLS), F32),
-        ],
+        [*sends, PACKED],
         [
             *(pltpu.VMEM(a.shape, a.dtype) for a in params),
             pltpu.VMEM((FIRST_ROWS, 256), BF16),
@@ -498,30 +504,29 @@
         limit=63,
     )
 
-    def middle(field):
-        shapes = [(128, CELLS), (TRACE, CELLS), (TRACE, CELLS), (FACE, PAIR_SLOTS)]
-        return call(middle_kernel, shapes, [FIELD], field, codes, scales, table, name="middle")
-
+    arrays = [(128, CELLS), (TRACE, CELLS), (TRACE, CELLS), (FACE, PAIR_SLOTS)]
     scratch = [SIDES, HOT, SPREAD]
     arrived = exchange(*swapping)
+    own = call(middle_kernel, arrays, [FIELD], source, codes, table, name="middle")
     image, *swapping = call(
         image_kernel,
-        [jax.ShapeDtypeStruct((128, CELLS), F32), *sends],
+        [(128, CELLS), *sends],
         scratch,
         codes,
         table,
-        *middle(source),
+        *own,
         *arrived,
         name="image",
     )
     arrived = exchange(*swapping)
+    own = call(middle_kernel, arrays, [FIELD], image, codes, table, name="middle")
     second, sums = call(
         moments_kernel,
         [(128, CELLS), (lax.axis_size(PLANE), 1, 128)],
         scratch,
         codes,
         table,
-        *middle(image),
+        *own,
         *arrived,
         source,
         image,

time: 99.7 us -> 96.1 us (0.964)
  waiting for transfers between devices: 18.4 us -> 14.7 us
    ppermute x8, waiting for transfers between devices: 2.54 us -> 0.02 us  [swapped(): lax.ppermute(value, axes, pairs + [(above, below) for below, above in pai...]
    ppermute x8, starting transfers between devices: 27.8 us -> 29 us  [swapped(): lax.ppermute(value, axes, pairs + [(above, below) for below, above in pai...]
    ppermute x1, waiting for transfers between devices: 15.8 us -> 14.7 us  [summed_over_blocks(): other = lax.ppermute(jnp.sum(sums, axis=0, keepdims=True), BLOCK, diagonal)]
  transfers between devices with their start and end apart: 9 -> 9, of which waited for: 3 -> 1; matrix products, arithmetic and copies ran while one was open for 0% -> 0% of each run, Pallas kernels for 2% -> 2%
where the time goes in v3:
time: 96.1 us; the launch traced here: 95.7 us
  blocking collectives  35.1 us (37%)
  starting transfers between devices  30.9 us (32%)
  waiting for transfers between devices  14.7 us (15%)
  Pallas kernels  13.2 us (14%)
    ppermute x8, starting transfers between devices, swapped(): lax.ppermute(value, axes, pairs + [(above, below) for below, above in pai...  29 us
    all_to_all x1, blocking collectives, summed_over_blocks(): lax.all_to_all(jnp.broadcast_to(other, sums.shape), PLANE, 0, 0, tiled=True)  22.1 us
    ppermute x1, waiting for transfers between devices, summed_over_blocks(): other = lax.ppermute(jnp.sum(sums, axis=0, keepdims=True), BLOCK, diagonal)  14.7 us
    pallas_call x6, Pallas kernels, call(): pl.pallas_call(kernel, out_shape=[jax.ShapeDtypeStruct(shape, F32) for sh...  13.2 us
    all_to_all x1, blocking collectives, summed_over_blocks(): sums = lax.all_to_all(sums, PLANE, 0, 0, tiled=True)  13 us
  transfers between devices with their start and end apart: 9, of which 1 were waited for; matrix products, arithmetic and copies ran while one was open for 0% of the time, Pallas kernels for 2%

profile of v3, /device:TPU:1, one launch (start us, length us, event | category | flops | bytes accessed | tf_op | source)
XLA Modules:
  0.0 95.7 jit_solution(15422301942723641439)
XLA Ops:
  0.6 0.0 copy-start
  0.7 3.7 %first.1 = (f32[128,128]{1,0:T(8,128)}, f32[32,512]{1,0:T(8,128)}, f32[32,512]{1,0:T(8,128)}, f32[128,128]{1,0:T(8,128)}, f32[16,1024]{1,0:T(8,128)}) custom-call(f32[125,512]{1,0:T(8,128)} %source_ref.1, s32[1,512]{1,0:T(1,128)} %bitcast.6, s32[1,512]{1,0:T(1,128)} %bitcast.7, f32[1,64]{1,0:T(1,128)} %bitcast.9, s32[2,960]{1,0:T(2,128)} %refs_4_.1, ...), custom_call_target="tpu_custom_call" | custom-call | tf_op jit(solution)/shard_map/first/pallas_call | solution.py:442
  4.4 4.6 %collective-permute-start = (f32[128,128]{1,0:T(8,128)}, f32[128,128]{1,0:T(8,128)S(1)}, u32[]{:S(2)}, u32[]{:S(2)}) collective-permute-start(f32[128,128]{1,0:T(8,128)} %get-tuple-element.27), channel_id=1, source_target_pairs={{1,2},{3,4},{5,6},{7,8},{9,10},{11,12},{13,14},{15,16},{17,18},{19... | collective-permute-start | bytes 196616 | tf_op jit(solution)/shard_map/ppermute | solution.py:462
  9.0 0.7 collective-permute-start.1
  9.6 5.6 %collective-permute-start.2 = (f32[32,512]{1,0:T(8,128)}, f32[32,512]{1,0:T(8,128)S(1)}, u32[]{:S(2)}, u32[]{:S(2)}) collective-permute-start(f32[32,512]{1,0:T(8,128)} %get-tuple-element.29), channel_id=1, source_target_pairs={{0,8},{16,24},{32,40},{48,56},{64,72},{80,88},{96,104},{112,120},{... | collective-permute-start | bytes 196616 | tf_op jit(solution)/shard_map/ppermute | solution.py:462
  15.2 8.5 %collective-permute-start.3 = (f32[128,128]{1,0:T(8,128)}, f32[128,128]{1,0:T(8,128)S(1)}, u32[]{:S(2)}, u32[]{:S(2)}) collective-permute-start(f32[128,128]{1,0:T(8,128)} %get-tuple-element.30), channel_id=1, source_target_pairs={{0,1},{2,3},{4,5},{6,7},{8,9},{10,11},{12,13},{14,15},{16,17},{18,... | collective-permute-start | bytes 196616 | tf_op jit(solution)/shard_map/ppermute | solution.py:462
  23.7 0.8 copy-done.2
  24.6 1.1 %middle.2 = (f32[128,512]{1,0:T(8,128)S(1)}, f32[192,512]{1,0:T(8,128)S(1)}, f32[192,512]{1,0:T(8,128)S(1)}, f32[32,1024]{1,0:T(8,128)S(1)}) custom-call(f32[125,512]{1,0:T(8,128)S(1)} %copy-done.1, f32[16,1024]{1,0:T(8,128)S(1)} %copy-done.2, bf16[1120,256]{1,0:T(8,128)(2,1)S(1)} %copy-done), custom_call_target="tpu_custom_call" | custom-call | tf_op jit(solution)/shard_map/middle/pallas_call | solution.py:442
  25.7 0.0 collective-permute-done.1.refs_7_
  25.7 0.0 collective-permute-done.2.refs_8_
  25.7 3.8 %image.1 = (f32[128,512]{1,0:T(8,128)S(1)}, f32[128,128]{1,0:T(8,128)S(1)}, f32[32,512]{1,0:T(8,128)S(1)}, f32[32,512]{1,0:T(8,128)S(1)}, f32[128,128]{1,0:T(8,128)S(1)}) custom-call(f32[16,1024]{1,0:T(8,128)S(1)} %copy-done.2, bf16[1120,256]{1,0:T(8,128)(2,1)S(1)} %copy-done, f32[128,512]{1,0:T(8,128)S(1)} %get-tuple-element.23.refs_2_, ...), custom_call_target="tpu_custom_call" | custom-call | tf_op jit(solution)/shard_map/image/pallas_call | solution.py:442
  29.5 1.9 %collective-permute-start.4 = (f32[128,128]{1,0:T(8,128)S(1)}, f32[128,128]{1,0:T(8,128)S(1)}, u32[]{:S(2)}, u32[]{:S(2)}) collective-permute-start(f32[128,128]{1,0:T(8,128)S(1)} %get-tuple-element.36), channel_id=1, source_target_pairs={{1,2},{3,4},{5,6},{7,8},{9,10},{11,12},{13,14},{15,16},{17,18},{19... | collective-permute-start | bytes 196616 | tf_op jit(solution)/shard_map/ppermute | solution.py:462
  31.4 0.7 collective-permute-start.5
  32.1 4.9 %collective-permute-start.6 = (f32[32,512]{1,0:T(8,128)S(1)}, f32[32,512]{1,0:T(8,128)S(1)}, u32[]{:S(2)}, u32[]{:S(2)}) collective-permute-start(f32[32,512]{1,0:T(8,128)S(1)} %get-tuple-element.38), channel_id=1, source_target_pairs={{0,8},{16,24},{32,40},{48,56},{64,72},{80,88},{96,104},{112,120},{... | collective-permute-start | bytes 196616 | tf_op jit(solution)/shard_map/ppermute | solution.py:462
  37.0 2.2 %collective-permute-start.7 = (f32[128,128]{1,0:T(8,128)S(1)}, f32[128,128]{1,0:T(8,128)S(1)}, u32[]{:S(2)}, u32[]{:S(2)}) collective-permute-start(f32[128,128]{1,0:T(8,128)S(1)} %get-tuple-element.39), channel_id=1, source_target_pairs={{0,1},{2,3},{4,5},{6,7},{8,9},{10,11},{12,13},{14,15},{16,17},{18,... | collective-permute-start | bytes 196616 | tf_op jit(solution)/shard_map/ppermute | solution.py:462
  39.2 1.1 %middle.3 = (f32[128,512]{1,0:T(8,128)S(1)}, f32[192,512]{1,0:T(8,128)S(1)}, f32[192,512]{1,0:T(8,128)S(1)}, f32[32,1024]{1,0:T(8,128)S(1)}) custom-call(f32[128,512]{1,0:T(8,128)S(1)} %get-tuple-element.31.field_ref.refs_11_.image_ref, f32[16,1024]{1,0:T(8,128)S(1)} %copy-done.2, bf16[1120,256]{1,0:T(8,128)(2,1)S(1)} %copy-done), custom_call_target="tpu_custom_call" | custom-call | tf_op jit(solution)/shard_map/middle/pallas_call | solution.py:442
  40.3 0.0 collective-permute-done.4.refs_6_
  40.3 2.5 %moments.1 = (f32[128,512]{1,0:T(8,128)S(1)}, f32[32,1,128]{2,1,0:T(1,128)S(1)}) custom-call(f32[16,1024]{1,0:T(8,128)S(1)} %copy-done.2, bf16[1120,256]{1,0:T(8,128)(2,1)S(1)} %copy-done, f32[128,512]{1,0:T(8,128)S(1)} %get-tuple-element.32.refs_2_, f32[192,512]{1,0:T(8,128)S(1)} %get-tuple-element.33.refs_3_, f32[192,512]{1,0:T(8,128)S(1)} %get-tuple-element.34.refs_4_, ...), custom_call_target="tpu_custom_call" | custom-call | tf_op jit(solution)/shard_map/moments/pallas_call | solution.py:442
  42.9 13.0 %all_to_all.10 = f32[32,1,128]{2,1,0:T(1,128)S(1)} all-to-all(f32[32,1,128]{2,1,0:T(1,128)S(1)} %get-tuple-element.40), channel_id=1, replica_groups=mesh['z'=32,'x'=4,'y'=4,'core'=2] {'x','y','core'}, dimensions={0} | all-to-all | bytes 32768 | tf_op jit(solution)/shard_map/all_to_all | solution.py:475
  55.8 0.1 reduce_sum.9
  55.9 1.9 %collective-permute-start.8 = (f32[1,1,128]{2,1,0:T(1,128)S(1)}, f32[1,1,128]{2,1,0:T(1,128)S(1)}, u32[]{:S(2)}, u32[]{:S(2)}) collective-permute-start(f32[1,1,128]{2,1,0:T(1,128)S(1)} %bitcast.10), channel_id=1, source_target_pairs={{0,0},{1,33},{2,66},{3,99},{4,132},{5,165},{6,198},{7,231},{8,264}... | collective-permute-start | bytes 1544 | tf_op jit(solution)/shard_map/ppermute | solution.py:481
  57.8 14.7 %collective-permute-done.8 = f32[1,1,128]{2,1,0:T(1,128)S(1)} collective-permute-done((f32[1,1,128]{2,1,0:T(1,128)S(1)}, f32[1,1,128]{2,1,0:T(1,128)S(1)}, u32[]{:S(2)}, u32[]{:S(2)}) %collective-permute-start.8) | collective-permute-done | bytes 544 | tf_op jit(solution)/shard_map/ppermute | solution.py:481
  72.5 22.1 %all_to_all.11.sums_ref = f32[32,1,128]{2,1,0:T(1,128)S(1)} all-to-all(f32[32,1,128]{2,1,0:T(1,128)S(1)} %broadcast_in_dim.12), channel_id=1, replica_groups=mesh['z'=32,'x'=4,'y'=4,'core'=2] {'x','y','core'}, dimensions={0} | all-to-all | bytes 32768 | tf_op jit(solution)/shard_map/all_to_all | solution.py:482
  94.6 1.1 %last.1 = (f32[125,512]{1,0:T(8,128)}, f32[125,512]{1,0:T(8,128)}) custom-call(f32[32,1,128]{2,1,0:T(1,128)S(1)} %all_to_all.11.sums_ref, f32[125,512]{1,0:T(8,128)S(1)} %copy-done.1, f32[128,512]{1,0:T(8,128)S(1)} %get-tuple-element.31.field_ref.refs_11_.image_ref, f32[128,512]{1,0:T(8,128)S(1)} %get-tuple-element.41.second_ref), custom_call_target="tpu_custom_call" | custom-call | tf_op jit(solution)/shard_map/last/pallas_call | solution.py:442
  (10 shorter events, 0.0 us)
Async XLA Ops:
  0.6 23.1 %copy-start = (bf16[1120,256]{1,0:T(8,128)(2,1)S(1)}, bf16[1120,256]{1,0:T(8,128)(2,1)}, u32[]{:S(2)}) copy-start(bf16[1120,256]{1,0:T(8,128)(2,1)} %constant.4.clone.refs_7_.table_ref.refs_1_) | copy-start | bytes 1720324
  0.6 23.1 %copy-start.1 = (f32[125,512]{1,0:T(8,128)S(1)}, f32[125,512]{1,0:T(8,128)}, u32[]{:S(2)}) copy-start(f32[125,512]{1,0:T(8,128)} %source_ref.1) | copy-start | bytes 768004
  4.4 21.3 %collective-permute-start = (f32[128,128]{1,0:T(8,128)}, f32[128,128]{1,0:T(8,128)S(1)}, u32[]{:S(2)}, u32[]{:S(2)}) collective-permute-start(f32[128,128]{1,0:T(8,128)} %get-tuple-element.27), channel_id=1, source_target_pairs={{1,2},{3,4},{5,6},{7,8},{9,10},{11,12},{13,14},{15,16},{17,18},{19... | collective-permute-start | bytes 196616 | tf_op jit(solution)/shard_map/ppermute | solution.py:462
  9.0 16.7 %collective-permute-start.1 = (f32[32,512]{1,0:T(8,128)}, f32[32,512]{1,0:T(8,128)S(1)}, u32[]{:S(2)}, u32[]{:S(2)}) collective-permute-start(f32[32,512]{1,0:T(8,128)} %get-tuple-element.28), channel_id=1, source_target_pairs={{8,16},{24,32},{40,48},{56,64},{72,80},{88,96},{104,112},{120,128}... | collective-permute-start | bytes 196616 | tf_op jit(solution)/shard_map/ppermute | solution.py:462
  9.6 16.0 %collective-permute-start.2 = (f32[32,512]{1,0:T(8,128)}, f32[32,512]{1,0:T(8,128)S(1)}, u32[]{:S(2)}, u32[]{:S(2)}) collective-permute-start(f32[32,512]{1,0:T(8,128)} %get-tuple-element.29), channel_id=1, source_target_pairs={{0,8},{16,24},{32,40},{48,56},{64,72},{80,88},{96,104},{112,120},{... | collective-permute-start | bytes 196616 | tf_op jit(solution)/shard_map/ppermute | solution.py:462
  15.2 10.5 %collective-permute-start.3 = (f32[128,128]{1,0:T(8,128)}, f32[128,128]{1,0:T(8,128)S(1)}, u32[]{:S(2)}, u32[]{:S(2)}) collective-permute-start(f32[128,128]{1,0:T(8,128)} %get-tuple-element.30), channel_id=1, source_target_pairs={{0,1},{2,3},{4,5},{6,7},{8,9},{10,11},{12,13},{14,15},{16,17},{18,... | collective-permute-start | bytes 196616 | tf_op jit(solution)/shard_map/ppermute | solution.py:462
  23.7 0.8 copy-start.2
  29.5 10.8 %collective-permute-start.4 = (f32[128,128]{1,0:T(8,128)S(1)}, f32[128,128]{1,0:T(8,128)S(1)}, u32[]{:S(2)}, u32[]{:S(2)}) collective-permute-start(f32[128,128]{1,0:T(8,128)S(1)} %get-tuple-element.36), channel_id=1, source_target_pairs={{1,2},{3,4},{5,6},{7,8},{9,10},{11,12},{13,14},{15,16},{17,18},{19... | collective-permute-start | bytes 196616 | tf_op jit(solution)/shard_map/ppermute | solution.py:462
  31.4 8.9 %collective-permute-start.5 = (f32[32,512]{1,0:T(8,128)S(1)}, f32[32,512]{1,0:T(8,128)S(1)}, u32[]{:S(2)}, u32[]{:S(2)}) collective-permute-start(f32[32,512]{1,0:T(8,128)S(1)} %get-tuple-element.37), channel_id=1, source_target_pairs={{8,16},{24,32},{40,48},{56,64},{72,80},{88,96},{104,112},{120,128}... | collective-permute-start | bytes 196616 | tf_op jit(solution)/shard_map/ppermute | solution.py:462
  32.1 8.2 %collective-permute-start.6 = (f32[32,512]{1,0:T(8,128)S(1)}, f32[32,512]{1,0:T(8,128)S(1)}, u32[]{:S(2)}, u32[]{:S(2)}) collective-permute-start(f32[32,512]{1,0:T(8,128)S(1)} %get-tuple-element.38), channel_id=1, source_target_pairs={{0,8},{16,24},{32,40},{48,56},{64,72},{80,88},{96,104},{112,120},{... | collective-permute-start | bytes 196616 | tf_op jit(solution)/shard_map/ppermute | solution.py:462
  37.0 3.3 %collective-permute-start.7 = (f32[128,128]{1,0:T(8,128)S(1)}, f32[128,128]{1,0:T(8,128)S(1)}, u32[]{:S(2)}, u32[]{:S(2)}) collective-permute-start(f32[128,128]{1,0:T(8,128)S(1)} %get-tuple-element.39), channel_id=1, source_target_pairs={{0,1},{2,3},{4,5},{6,7},{8,9},{10,11},{12,13},{14,15},{16,17},{18,... | collective-permute-start | bytes 196616 | tf_op jit(solution)/shard_map/ppermute | solution.py:462
  55.9 16.6 %collective-permute-start.8 = (f32[1,1,128]{2,1,0:T(1,128)S(1)}, f32[1,1,128]{2,1,0:T(1,128)S(1)}, u32[]{:S(2)}, u32[]{:S(2)}) collective-permute-start(f32[1,1,128]{2,1,0:T(1,128)S(1)} %bitcast.10), channel_id=1, source_target_pairs={{0,0},{1,33},{2,66},{3,99},{4,132},{5,165},{6,198},{7,231},{8,264}... | collective-permute-start | bytes 1544 | tf_op jit(solution)/shard_map/ppermute | solution.py:481

commit v4 on v3

--- a/solution.py
+++ b/solution.py
@@ -14,7 +14,10 @@
 PAIR_SLOTS = 1024
 SIDE = 128
 FACE = 32
-TRACE = 6 * FACE
+MAIN = 24
+TAIL = 6 * MAIN
+STACK = TAIL + 8
+TRACE = 160
 FINE0 = PAIR_SLOTS
 COARSE0 = PAIR_SLOTS + 4 * CELLS
 SLOTS = COARSE0 + CELLS
@@ -75,15 +78,15 @@
 
 PLACES = {
     "trace": [(0, 0)],
-    "up": [(192, 0), (192, 128)],
-    "untrace": [(224, 0)],
-    "coarse": [(352, 0), (544, 0)],
-    "local": [(736, 0), (736, 128)],
-    "down": [(864, 0), (864, 128)],
-    "lumped": [(992, 0), (992, 128)],
+    "up": [(160, 0), (160, 128)],
+    "untrace": [(192, 0)],
+    "coarse": [(320, 0), (480, 0)],
+    "local": [(640, 0), (640, 128)],
+    "down": [(768, 0), (768, 128)],
+    "lumped": [(896, 0), (896, 128)],
 }
-FIRST_ROWS = 224
-TABLE_ROWS = 1120
+FIRST_ROWS = 192
+TABLE_ROWS = 1024
 
 
 def packed_table():
@@ -101,20 +104,24 @@
     lumped[:125, 0] = SIGMA_MASS * np.einsum("i,j,k->ijk", weights, weights, weights).reshape(-1)
     node = np.arange(125).reshape(5, 5, 5)
     slabs = [node[0], node[:, 0], node[:, :, 0], node[4], node[:, 4], node[:, :, 4]]
+    stacked = np.concatenate([np.arange(6)[:, None] * MAIN + np.arange(MAIN), TAIL + np.arange(6)[:, None]], axis=1)
     trace = np.zeros((TRACE, 128))
     for face, slab in enumerate(slabs):
-        trace[face * FACE + np.arange(25), slab.reshape(-1)] = 1.0
-    coarse = np.zeros((FACE, FACE))
+        trace[stacked[face], slab.reshape(-1)] = 1.0
+    coarse = np.zeros((25, 25))
     down = np.zeros((4 * FACE, FACE))
     for child, matrix in enumerate(interp):
-        coarse[:25, :25] += matrix.T @ matrix
+        coarse += matrix.T @ matrix
         down[child * FACE : child * FACE + 25, :25] = matrix
+    coarse_stack = np.zeros((TRACE, TRACE))
+    for rows in stacked:
+        coarse_stack[np.ix_(rows, rows)] = TAU_PENALTY * coarse
     table = np.zeros((TABLE_ROWS, 256))
     places = {
         "trace": trace,
         "untrace": trace.T,
         "local": local,
-        "coarse": np.kron(np.eye(6), TAU_PENALTY * coarse),
+        "coarse": coarse_stack,
         "down": -TAU_PENALTY * down,
         "up": -TAU_PENALTY * down.T,
         "lumped": lumped,
@@ -168,12 +175,20 @@
 
 
 def pick(gathered, face):
-    total = None
+    both = gathered[0:STACK] + gathered[STACK : 2 * STACK]
+    main = None
     for f in range(6):
-        both = gathered[f * FACE : (f + 1) * FACE] + gathered[TRACE + f * FACE : TRACE + (f + 1) * FACE]
-        term = jnp.where(face == f, both, 0.0)
-        total = term if total is None else total + term
-    return total
+        term = jnp.where(face == f, both[f * MAIN : (f + 1) * MAIN], 0.0)
+        main = term if main is None else main + term
+    row = lax.broadcasted_iota(jnp.int32, (8, both.shape[1]), 0)
+    last = jnp.sum(jnp.where(row == face, both[TAIL:STACK], 0.0), axis=0, keepdims=True)
+    return jnp.concatenate([main, jnp.where(row == 0, last, 0.0)], axis=0)
+
+
+def stack(value, face):
+    row = lax.broadcasted_iota(jnp.int32, (8, value.shape[1]), 0)
+    pieces = [jnp.where(face == f, value[0:MAIN], 0.0) for f in range(6)]
+    return pieces + [jnp.where(row == face, value[MAIN : MAIN + 1], 0.0)]
 
 
 def own_code(code):
@@ -232,9 +247,12 @@
     hot[:, COARSE0:SLOTS] = one_hot(cell, CELLS)
 
 
+def joined(high, low):
+    return jnp.concatenate([high[0:STACK], low[0:STACK]], axis=0).astype(BF16)
+
+
 def stacked_traces(trace_ref, field):
-    high, low = face_traces(trace_ref, field)
-    return jnp.concatenate([high.astype(BF16), low.astype(BF16)], axis=0)
+    return joined(*face_traces(trace_ref, field))
 
 
 def swaps(low, high, send_coarse, send_fine, rim_chip_ref, dom_odd_ref, dom_even_ref, rim_core_ref):
@@ -303,7 +321,7 @@
     both = high + low
     trace_out_ref[...] = both
     coarse_out_ref[...] = table_dot(table["coarse"], both)
-    traces = jnp.concatenate([high.astype(BF16), low.astype(BF16)], axis=0)
+    traces = joined(high, low)
     for start in range(0, PAIR_SLOTS, CHUNK):
         face, cell = extended_code(codes[1:2, start : start + CHUNK])
         partner_ref[:, start : start + CHUNK] = pick(dot(traces, one_hot(cell, CELLS)), face)
@@ -343,17 +361,10 @@
     def put(start, value, face, coarse):
         width = value.shape[1]
         high = value.astype(BF16).astype(F32)
-        low = value - high
-        for f in range(6):
-            live = face == f
-            spread[f * FACE : (f + 1) * FACE, start : start + width] = jnp.where(live, high, 0.0).astype(BF16)
-            spread[TRACE + f * FACE : TRACE + (f + 1) * FACE, start : start + width] = jnp.where(
-                live, low, 0.0
-            ).astype(BF16)
         row = lax.broadcasted_iota(jnp.int32, (16, width), 0)
-        spread[2 * TRACE : 2 * TRACE + 16, start : start + width] = jnp.where(
-            row == (face + 8 if coarse else face), 1.0, 0.0
-        ).astype(BF16)
+        count = jnp.where(row == (face + 8 if coarse else face), 1.0, 0.0)
+        pieces = stack(high, face) + stack(value - high, face) + [count]
+        spread[:, start : start + width] = jnp.concatenate(pieces, axis=0).astype(BF16)
 
     for start in range(0, PAIR_SLOTS, CHUNK):
         face, cell = extended_code(codes[1:2, start : start + CHUNK])
@@ -371,17 +382,19 @@
     face, _ = coarse_code(codes)
     put(COARSE0, returned, face, True)
     added = dot(spread[...], hot[...], ALONG_LANES)
+    both = added[0:STACK] + added[STACK : 2 * STACK]
+    fine_count = TAU_PENALTY * added[2 * STACK : 2 * STACK + 8]
+    coarse_count = added[2 * STACK + 8 : 2 * STACK + 16]
     pieces = []
-    for f in range(6):
-        rows = slice(f * FACE, (f + 1) * FACE)
-        fine_count = added[2 * TRACE + f : 2 * TRACE + f + 1]
-        coarse_count = added[2 * TRACE + 8 + f : 2 * TRACE + 9 + f]
+    for f in range(7):
+        rows = slice(f * MAIN, min((f + 1) * MAIN, STACK))
+        counts = slice(f, f + 1) if f < 6 else slice(0, 8)
         pieces.append(
-            added[f * FACE : (f + 1) * FACE]
-            + added[TRACE + f * FACE : TRACE + (f + 1) * FACE]
-            + (TAU_PENALTY * fine_count) * trace_in_ref[rows, :]
-            + coarse_count * coarse_in_ref[rows, :]
+            both[rows]
+            + fine_count[counts] * trace_in_ref[rows, :]
+            + coarse_count[counts] * coarse_in_ref[rows, :]
         )
+    pieces.append(jnp.zeros((TRACE - STACK, CELLS), F32))
     high, low = split(jnp.concatenate(pieces, axis=0))
     untrace = table["untrace"][...]
     return applied_ref[...] + (dot(untrace, high) + dot(untrace, low))
@@ -453,7 +466,7 @@
 FIELD = pltpu.VMEM((128, CELLS), F32)
 SIDES = pltpu.VMEM((128, 2 * SIDE), F32)
 HOT = pltpu.VMEM((CELLS, SLOTS), BF16)
-SPREAD = pltpu.VMEM((2 * TRACE + 16, SLOTS), BF16)
+SPREAD = pltpu.VMEM((2 * STACK + 16, SLOTS), BF16)
 
 
 def swapped(value, axes, first):

time: 96.1 us -> 95.2 us (level)
    pallas_call x6, Pallas kernels: 13.2 us -> 12.3 us  [call(): pl.pallas_call(kernel, out_shape=[jax.ShapeDtypeStruct(shape, F32) for sh...]
where the time goes in v4:
time: 95.2 us; the launch traced here: 94.8 us
  blocking collectives  35.2 us (37%)
  starting transfers between devices  30.9 us (32%)
  waiting for transfers between devices  14.7 us (15%)
  Pallas kernels  12.3 us (13%)
    ppermute x8, starting transfers between devices, swapped(): lax.ppermute(value, axes, pairs + [(above, below) for below, above in pai...  29 us
    all_to_all x1, blocking collectives, summed_over_blocks(): lax.all_to_all(jnp.broadcast_to(other, sums.shape), PLANE, 0, 0, tiled=True)  22.1 us
    ppermute x1, waiting for transfers between devices, summed_over_blocks(): other = lax.ppermute(jnp.sum(sums, axis=0, keepdims=True), BLOCK, diagonal)  14.6 us
    all_to_all x1, blocking collectives, summed_over_blocks(): sums = lax.all_to_all(sums, PLANE, 0, 0, tiled=True)  13.1 us
    pallas_call x6, Pallas kernels, call(): pl.pallas_call(kernel, out_shape=[jax.ShapeDtypeStruct(shape, F32) for sh...  12.3 us
    ppermute x1, starting transfers between devices, summed_over_blocks(): other = lax.ppermute(jnp.sum(sums, axis=0, keepdims=True), BLOCK, diagonal)  1.91 us
  transfers between devices with their start and end apart: 9, of which 1 were waited for; matrix products, arithmetic and copies ran while one was open for 0% of the time, Pallas kernels for 2%

profile of v4, /device:TPU:1, one launch (start us, length us, event | category | flops | bytes accessed | tf_op | source)
XLA Modules:
  0.0 94.8 jit_solution(14735787573535946078)
XLA Ops:
  0.6 0.0 copy-start
  0.7 3.6 %first.1 = (f32[128,128]{1,0:T(8,128)}, f32[32,512]{1,0:T(8,128)}, f32[32,512]{1,0:T(8,128)}, f32[128,128]{1,0:T(8,128)}, f32[16,1024]{1,0:T(8,128)}) custom-call(f32[125,512]{1,0:T(8,128)} %source_ref.1, s32[1,512]{1,0:T(1,128)} %bitcast.6, s32[1,512]{1,0:T(1,128)} %bitcast.7, f32[1,64]{1,0:T(1,128)} %bitcast.11, s32[2,960]{1,0:T(2,128)} %refs_4_.1, ...), custom_call_target="tpu_custom_call" | custom-call | tf_op jit(solution)/shard_map/first/pallas_call | solution.py:455
  4.2 4.6 %collective-permute-start = (f32[128,128]{1,0:T(8,128)}, f32[128,128]{1,0:T(8,128)S(1)}, u32[]{:S(2)}, u32[]{:S(2)}) collective-permute-start(f32[128,128]{1,0:T(8,128)} %get-tuple-element.27), channel_id=1, source_target_pairs={{1,2},{3,4},{5,6},{7,8},{9,10},{11,12},{13,14},{15,16},{17,18},{19... | collective-permute-start | bytes 196616 | tf_op jit(solution)/shard_map/ppermute | solution.py:475
  8.8 0.7 collective-permute-start.1
  9.5 5.6 %collective-permute-start.2 = (f32[32,512]{1,0:T(8,128)}, f32[32,512]{1,0:T(8,128)S(1)}, u32[]{:S(2)}, u32[]{:S(2)}) collective-permute-start(f32[32,512]{1,0:T(8,128)} %get-tuple-element.29), channel_id=1, source_target_pairs={{0,8},{16,24},{32,40},{48,56},{64,72},{80,88},{96,104},{112,120},{... | collective-permute-start | bytes 196616 | tf_op jit(solution)/shard_map/ppermute | solution.py:475
  15.1 8.5 %collective-permute-start.3 = (f32[128,128]{1,0:T(8,128)}, f32[128,128]{1,0:T(8,128)S(1)}, u32[]{:S(2)}, u32[]{:S(2)}) collective-permute-start(f32[128,128]{1,0:T(8,128)} %get-tuple-element.30), channel_id=1, source_target_pairs={{0,1},{2,3},{4,5},{6,7},{8,9},{10,11},{12,13},{14,15},{16,17},{18,... | collective-permute-start | bytes 196616 | tf_op jit(solution)/shard_map/ppermute | solution.py:475
  23.6 0.8 copy-done.2
  24.4 1.0 %middle.2 = (f32[128,512]{1,0:T(8,128)S(1)}, f32[160,512]{1,0:T(8,128)S(1)}, f32[160,512]{1,0:T(8,128)S(1)}, f32[32,1024]{1,0:T(8,128)S(1)}) custom-call(f32[125,512]{1,0:T(8,128)S(1)} %copy-done.1, f32[16,1024]{1,0:T(8,128)S(1)} %copy-done.2, bf16[1024,256]{1,0:T(8,128)(2,1)S(1)} %copy-done), custom_call_target="tpu_custom_call" | custom-call | tf_op jit(solution)/shard_map/middle/pallas_call | solution.py:455
  25.4 0.0 collective-permute-done.refs_6_
  25.4 0.0 collective-permute-done.1.refs_7_
  25.5 3.4 %image.1 = (f32[128,512]{1,0:T(8,128)S(1)}, f32[128,128]{1,0:T(8,128)S(1)}, f32[32,512]{1,0:T(8,128)S(1)}, f32[32,512]{1,0:T(8,128)S(1)}, f32[128,128]{1,0:T(8,128)S(1)}) custom-call(f32[16,1024]{1,0:T(8,128)S(1)} %copy-done.2, bf16[1024,256]{1,0:T(8,128)(2,1)S(1)} %copy-done, f32[128,512]{1,0:T(8,128)S(1)} %get-tuple-element.23.refs_2_, ...), custom_call_target="tpu_custom_call" | custom-call | tf_op jit(solution)/shard_map/image/pallas_call | solution.py:455
  28.9 1.9 %collective-permute-start.4 = (f32[128,128]{1,0:T(8,128)S(1)}, f32[128,128]{1,0:T(8,128)S(1)}, u32[]{:S(2)}, u32[]{:S(2)}) collective-permute-start(f32[128,128]{1,0:T(8,128)S(1)} %get-tuple-element.36), channel_id=1, source_target_pairs={{1,2},{3,4},{5,6},{7,8},{9,10},{11,12},{13,14},{15,16},{17,18},{19... | collective-permute-start | bytes 196616 | tf_op jit(solution)/shard_map/ppermute | solution.py:475
  30.8 0.7 collective-permute-start.5
  31.5 4.9 %collective-permute-start.6 = (f32[32,512]{1,0:T(8,128)S(1)}, f32[32,512]{1,0:T(8,128)S(1)}, u32[]{:S(2)}, u32[]{:S(2)}) collective-permute-start(f32[32,512]{1,0:T(8,128)S(1)} %get-tuple-element.38), channel_id=1, source_target_pairs={{0,8},{16,24},{32,40},{48,56},{64,72},{80,88},{96,104},{112,120},{... | collective-permute-start | bytes 196616 | tf_op jit(solution)/shard_map/ppermute | solution.py:475
  36.4 2.2 %collective-permute-start.7 = (f32[128,128]{1,0:T(8,128)S(1)}, f32[128,128]{1,0:T(8,128)S(1)}, u32[]{:S(2)}, u32[]{:S(2)}) collective-permute-start(f32[128,128]{1,0:T(8,128)S(1)} %get-tuple-element.39), channel_id=1, source_target_pairs={{0,1},{2,3},{4,5},{6,7},{8,9},{10,11},{12,13},{14,15},{16,17},{18,... | collective-permute-start | bytes 196616 | tf_op jit(solution)/shard_map/ppermute | solution.py:475
  38.6 1.0 %middle.3 = (f32[128,512]{1,0:T(8,128)S(1)}, f32[160,512]{1,0:T(8,128)S(1)}, f32[160,512]{1,0:T(8,128)S(1)}, f32[32,1024]{1,0:T(8,128)S(1)}) custom-call(f32[128,512]{1,0:T(8,128)S(1)} %get-tuple-element.31.field_ref.refs_11_.image_ref, f32[16,1024]{1,0:T(8,128)S(1)} %copy-done.2, bf16[1024,256]{1,0:T(8,128)(2,1)S(1)} %copy-done), custom_call_target="tpu_custom_call" | custom-call | tf_op jit(solution)/shard_map/middle/pallas_call | solution.py:455
  39.6 0.0 collective-permute-done.6.refs_8_
  39.6 2.3 %moments.1 = (f32[128,512]{1,0:T(8,128)S(1)}, f32[32,1,128]{2,1,0:T(1,128)S(1)}) custom-call(f32[16,1024]{1,0:T(8,128)S(1)} %copy-done.2, bf16[1024,256]{1,0:T(8,128)(2,1)S(1)} %copy-done, f32[128,512]{1,0:T(8,128)S(1)} %get-tuple-element.32.refs_2_, f32[160,512]{1,0:T(8,128)S(1)} %get-tuple-element.33.refs_3_, f32[160,512]{1,0:T(8,128)S(1)} %get-tuple-element.34.refs_4_, ...), custom_call_target="tpu_custom_call" | custom-call | tf_op jit(solution)/shard_map/moments/pallas_call | solution.py:455
  41.9 13.1 %all_to_all.10 = f32[32,1,128]{2,1,0:T(1,128)S(1)} all-to-all(f32[32,1,128]{2,1,0:T(1,128)S(1)} %get-tuple-element.40), channel_id=1, replica_groups=mesh['z'=32,'x'=4,'y'=4,'core'=2] {'x','y','core'}, dimensions={0} | all-to-all | bytes 32768 | tf_op jit(solution)/shard_map/all_to_all | solution.py:488
  55.0 0.1 reduce_sum.9
  55.0 1.9 %collective-permute-start.8 = (f32[1,1,128]{2,1,0:T(1,128)S(1)}, f32[1,1,128]{2,1,0:T(1,128)S(1)}, u32[]{:S(2)}, u32[]{:S(2)}) collective-permute-start(f32[1,1,128]{2,1,0:T(1,128)S(1)} %bitcast.9), channel_id=1, source_target_pairs={{0,0},{1,33},{2,66},{3,99},{4,132},{5,165},{6,198},{7,231},{8,264}... | collective-permute-start | bytes 1544 | tf_op jit(solution)/shard_map/ppermute | solution.py:494
  57.0 14.6 %collective-permute-done.8 = f32[1,1,128]{2,1,0:T(1,128)S(1)} collective-permute-done((f32[1,1,128]{2,1,0:T(1,128)S(1)}, f32[1,1,128]{2,1,0:T(1,128)S(1)}, u32[]{:S(2)}, u32[]{:S(2)}) %collective-permute-start.8) | collective-permute-done | bytes 544 | tf_op jit(solution)/shard_map/ppermute | solution.py:494
  71.6 22.1 %all_to_all.11.sums_ref = f32[32,1,128]{2,1,0:T(1,128)S(1)} all-to-all(f32[32,1,128]{2,1,0:T(1,128)S(1)} %broadcast_in_dim.12), channel_id=1, replica_groups=mesh['z'=32,'x'=4,'y'=4,'core'=2] {'x','y','core'}, dimensions={0} | all-to-all | bytes 32768 | tf_op jit(solution)/shard_map/all_to_all | solution.py:495
  93.7 1.1 %last.1 = (f32[125,512]{1,0:T(8,128)}, f32[125,512]{1,0:T(8,128)}) custom-call(f32[32,1,128]{2,1,0:T(1,128)S(1)} %all_to_all.11.sums_ref, f32[125,512]{1,0:T(8,128)S(1)} %copy-done.1, f32[128,512]{1,0:T(8,128)S(1)} %get-tuple-element.31.field_ref.refs_11_.image_ref, f32[128,512]{1,0:T(8,128)S(1)} %get-tuple-element.41.second_ref), custom_call_target="tpu_custom_call" | custom-call | tf_op jit(solution)/shard_map/last/pallas_call | solution.py:455
  (10 shorter events, 0.0 us)
Async XLA Ops:
  0.6 22.9 %copy-start = (bf16[1024,256]{1,0:T(8,128)(2,1)S(1)}, bf16[1024,256]{1,0:T(8,128)(2,1)}, u32[]{:S(2)}) copy-start(bf16[1024,256]{1,0:T(8,128)(2,1)} %constant.4.clone.refs_7_.table_ref.refs_1_) | copy-start | bytes 1572868
  0.6 22.9 %copy-start.1 = (f32[125,512]{1,0:T(8,128)S(1)}, f32[125,512]{1,0:T(8,128)}, u32[]{:S(2)}) copy-start(f32[125,512]{1,0:T(8,128)} %source_ref.1) | copy-start | bytes 768004
  4.2 21.2 %collective-permute-start = (f32[128,128]{1,0:T(8,128)}, f32[128,128]{1,0:T(8,128)S(1)}, u32[]{:S(2)}, u32[]{:S(2)}) collective-permute-start(f32[128,128]{1,0:T(8,128)} %get-tuple-element.27), channel_id=1, source_target_pairs={{1,2},{3,4},{5,6},{7,8},{9,10},{11,12},{13,14},{15,16},{17,18},{19... | collective-permute-start | bytes 196616 | tf_op jit(solution)/shard_map/ppermute | solution.py:475
  8.8 16.6 %collective-permute-start.1 = (f32[32,512]{1,0:T(8,128)}, f32[32,512]{1,0:T(8,128)S(1)}, u32[]{:S(2)}, u32[]{:S(2)}) collective-permute-start(f32[32,512]{1,0:T(8,128)} %get-tuple-element.28), channel_id=1, source_target_pairs={{8,16},{24,32},{40,48},{56,64},{72,80},{88,96},{104,112},{120,128}... | collective-permute-start | bytes 196616 | tf_op jit(solution)/shard_map/ppermute | solution.py:475
  9.5 15.9 %collective-permute-start.2 = (f32[32,512]{1,0:T(8,128)}, f32[32,512]{1,0:T(8,128)S(1)}, u32[]{:S(2)}, u32[]{:S(2)}) collective-permute-start(f32[32,512]{1,0:T(8,128)} %get-tuple-element.29), channel_id=1, source_target_pairs={{0,8},{16,24},{32,40},{48,56},{64,72},{80,88},{96,104},{112,120},{... | collective-permute-start | bytes 196616 | tf_op jit(solution)/shard_map/ppermute | solution.py:475
  15.1 10.4 %collective-permute-start.3 = (f32[128,128]{1,0:T(8,128)}, f32[128,128]{1,0:T(8,128)S(1)}, u32[]{:S(2)}, u32[]{:S(2)}) collective-permute-start(f32[128,128]{1,0:T(8,128)} %get-tuple-element.30), channel_id=1, source_target_pairs={{0,1},{2,3},{4,5},{6,7},{8,9},{10,11},{12,13},{14,15},{16,17},{18,... | collective-permute-start | bytes 196616 | tf_op jit(solution)/shard_map/ppermute | solution.py:475
  23.6 0.8 copy-start.2
  28.9 10.7 %collective-permute-start.4 = (f32[128,128]{1,0:T(8,128)S(1)}, f32[128,128]{1,0:T(8,128)S(1)}, u32[]{:S(2)}, u32[]{:S(2)}) collective-permute-start(f32[128,128]{1,0:T(8,128)S(1)} %get-tuple-element.36), channel_id=1, source_target_pairs={{1,2},{3,4},{5,6},{7,8},{9,10},{11,12},{13,14},{15,16},{17,18},{19... | collective-permute-start | bytes 196616 | tf_op jit(solution)/shard_map/ppermute | solution.py:475
  30.8 8.8 %collective-permute-start.5 = (f32[32,512]{1,0:T(8,128)S(1)}, f32[32,512]{1,0:T(8,128)S(1)}, u32[]{:S(2)}, u32[]{:S(2)}) collective-permute-start(f32[32,512]{1,0:T(8,128)S(1)} %get-tuple-element.37), channel_id=1, source_target_pairs={{8,16},{24,32},{40,48},{56,64},{72,80},{88,96},{104,112},{120,128}... | collective-permute-start | bytes 196616 | tf_op jit(solution)/shard_map/ppermute | solution.py:475
  31.5 8.1 %collective-permute-start.6 = (f32[32,512]{1,0:T(8,128)S(1)}, f32[32,512]{1,0:T(8,128)S(1)}, u32[]{:S(2)}, u32[]{:S(2)}) collective-permute-start(f32[32,512]{1,0:T(8,128)S(1)} %get-tuple-element.38), channel_id=1, source_target_pairs={{0,8},{16,24},{32,40},{48,56},{64,72},{80,88},{96,104},{112,120},{... | collective-permute-start | bytes 196616 | tf_op jit(solution)/shard_map/ppermute | solution.py:475
  36.4 3.2 %collective-permute-start.7 = (f32[128,128]{1,0:T(8,128)S(1)}, f32[128,128]{1,0:T(8,128)S(1)}, u32[]{:S(2)}, u32[]{:S(2)}) collective-permute-start(f32[128,128]{1,0:T(8,128)S(1)} %get-tuple-element.39), channel_id=1, source_target_pairs={{0,1},{2,3},{4,5},{6,7},{8,9},{10,11},{12,13},{14,15},{16,17},{18,... | collective-permute-start | bytes 196616 | tf_op jit(solution)/shard_map/ppermute | solution.py:475
  55.0 16.6 %collective-permute-start.8 = (f32[1,1,128]{2,1,0:T(1,128)S(1)}, f32[1,1,128]{2,1,0:T(1,128)S(1)}, u32[]{:S(2)}, u32[]{:S(2)}) collective-permute-start(f32[1,1,128]{2,1,0:T(1,128)S(1)} %bitcast.9), channel_id=1, source_target_pairs={{0,0},{1,33},{2,66},{3,99},{4,132},{5,165},{6,198},{7,231},{8,264}... | collective-permute-start | bytes 1544 | tf_op jit(solution)/shard_map/ppermute | solution.py:494

commit v5 on v4

--- a/solution.py
+++ b/solution.py
@@ -313,8 +313,11 @@
 
 
 def middle_kernel(
-    field_ref, codes, table_ref, applied_ref, trace_out_ref, coarse_out_ref, partner_ref, field
+    field_ref, pairs_ref, table_ref, stiff_ref, trace_out_ref, coarse_out_ref, partner_ref, *refs
 ):
+    *first_ref, field, pairs = refs
+    pairs[...] = jnp.full(pairs.shape, -1, jnp.int32)
+    pairs[0:2, 0:PAIRS] = pairs_ref[...]
     table = views(table_ref)
     vector = padded_field(field_ref, field)
     high, low = face_traces(table["trace"], vector)
@@ -323,19 +326,41 @@
     coarse_out_ref[...] = table_dot(table["coarse"], both)
     traces = joined(high, low)
     for start in range(0, PAIR_SLOTS, CHUNK):
-        face, cell = extended_code(codes[1:2, start : start + CHUNK])
+        face, cell = extended_code(pairs[1:2, start : start + CHUNK])
         partner_ref[:, start : start + CHUNK] = pick(dot(traces, one_hot(cell, CELLS)), face)
-    stiff = table_dot(table["local"], vector)
-    lumped = table["lumped"][0][...].astype(F32) + table["lumped"][1][...].astype(F32)
+        for ref in first_ref:
+            face, cell = own_code(pairs[0:1, start : start + CHUNK])
+            ref[:, start : start + CHUNK] = pick(dot(traces, one_hot(cell, CELLS)), face)
+    stiff_ref[...] = table_dot(table["local"], vector)
+
+
+def applied(codes, table, stiff, field):
+    rows = field.shape[0]
+    lumped = [part[...][0:rows].astype(F32) for part in table["lumped"]]
     factor = codes[SCALE_ROW : SCALE_ROW + 1, 0:CELLS]
     cubed = codes[SCALE_ROW + 1 : SCALE_ROW + 2, 0:CELLS]
-    applied_ref[...] = factor * stiff + cubed * (lumped * vector)
+    return factor * stiff[0:rows] + cubed * ((lumped[0] + lumped[1]) * field)
+
+
+def traces_beside(trace_ref, rim_chip_ref, rim_core_ref):
+    is_below = lax.broadcasted_iota(jnp.int32, rim_chip_ref.shape, 1) >= SIDE - RIM
+    from_chip = is_below == (lax.axis_index("core") == 0)
+    return stacked_traces(trace_ref, jnp.where(from_chip, rim_chip_ref[...], rim_core_ref[...]))
+
+
+def partner_values(codes, partner_ref, side_traces, start):
+    face, cell = extended_code(codes[1:2, start : start + CHUNK])
+    place = jnp.where(cell < 0, cell + SIDE, jnp.where(cell >= CELLS, cell - CELLS, -1))
+    place = jnp.where(face < 0, -1, place)
+    beside = pick(dot(side_traces, one_hot(place, SIDE)), face)
+    return partner_ref[:, start : start + CHUNK] + beside
 
 
 def add_faces(
     codes,
     table_ref,
-    applied_ref,
+    field_ref,
+    stiff_ref,
     trace_in_ref,
     coarse_in_ref,
     partner_ref,
@@ -343,20 +368,17 @@
     dom_odd_ref,
     dom_even_ref,
     rim_core_ref,
-    sides,
     hot,
     spread,
+    local,
 ):
     table = views(table_ref)
     hot_pairs(hot, codes)
     hot_hanging(hot, codes)
-    first_core = lax.axis_index("core") == 0
     even_dom = lax.axis_index("x") % 2 == 0
-    sides[:, 0:SIDE] = jnp.where(first_core, rim_chip_ref[...], rim_core_ref[...])
-    sides[:, SIDE : 2 * SIDE] = jnp.where(first_core, rim_core_ref[...], rim_chip_ref[...])
     arriving = jnp.where(even_dom, dom_odd_ref[...], dom_even_ref[...])
     returned = jnp.where(even_dom, dom_even_ref[...], dom_odd_ref[...])
-    side_traces = stacked_traces(table["trace"], sides[...])
+    side_traces = traces_beside(table["trace"], rim_chip_ref, rim_core_ref)
 
     def put(start, value, face, coarse):
         width = value.shape[1]
@@ -367,12 +389,7 @@
         spread[:, start : start + width] = jnp.concatenate(pieces, axis=0).astype(BF16)
 
     for start in range(0, PAIR_SLOTS, CHUNK):
-        face, cell = extended_code(codes[1:2, start : start + CHUNK])
-        place = jnp.where(cell < 0, cell + SIDE, jnp.where(cell >= CELLS, cell + (SIDE - CELLS), -1))
-        place = jnp.where(face < 0, -1, place)
-        partner = partner_ref[:, start : start + CHUNK] + pick(
-            dot(side_traces, one_hot(place, 2 * SIDE)), face
-        )
+        partner = partner_values(codes, partner_ref, side_traces, start)
         face, _ = own_code(codes[0:1, start : start + CHUNK])
         put(start, -TAU_PENALTY * partner, face, False)
     predicted = table_dot(table["down"], arriving)
@@ -383,64 +400,92 @@
     put(COARSE0, returned, face, True)
     added = dot(spread[...], hot[...], ALONG_LANES)
     both = added[0:STACK] + added[STACK : 2 * STACK]
-    fine_count = TAU_PENALTY * added[2 * STACK : 2 * STACK + 8]
-    coarse_count = added[2 * STACK + 8 : 2 * STACK + 16]
-    pieces = []
-    for f in range(7):
-        rows = slice(f * MAIN, min((f + 1) * MAIN, STACK))
-        counts = slice(f, f + 1) if f < 6 else slice(0, 8)
-        pieces.append(
-            both[rows]
-            + fine_count[counts] * trace_in_ref[rows, :]
-            + coarse_count[counts] * coarse_in_ref[rows, :]
-        )
+    counts = added[2 * STACK : 2 * STACK + 16]
+    pieces = [both[rows] + own for rows, own in own_faces(counts, trace_in_ref, coarse_in_ref)]
     pieces.append(jnp.zeros((TRACE - STACK, CELLS), F32))
     high, low = split(jnp.concatenate(pieces, axis=0))
     untrace = table["untrace"][...]
-    return applied_ref[...] + (dot(untrace, high) + dot(untrace, low))
+    rows = field_ref.shape[0]
+    local[...] = dot(untrace, high) + dot(untrace, low)
+    local[0:rows, :] += applied(codes, table, stiff_ref[...], field_ref[...])
+    return local[...], counts
+
+
+def own_faces(counts, trace_ref, coarse_ref):
+    for f in range(7):
+        rows = slice(f * MAIN, min((f + 1) * MAIN, STACK))
+        fine = counts[f : f + 1] if f < 6 else counts[0:8]
+        coarse = counts[f + 8 : f + 9] if f < 6 else counts[8:16]
+        yield rows, (TAU_PENALTY * fine) * trace_ref[rows, :] + coarse * coarse_ref[rows, :]
 
 
 def image_kernel(*refs):
     codes, table = refs[0], views(refs[1])
-    image = add_faces(*refs[:10], *refs[15:])
-    refs[10][...] = image
+    image, counts = add_faces(*refs[:11], *refs[17:])
+    refs[11][...] = image
     traces = stacked_traces(table["trace"], image)
-    send_coarse, send_fine = gather_hanging(traces, refs[16], codes, table["up"])
-    swaps(image[:, 0:SIDE], image[:, CELLS - SIDE :], send_coarse, send_fine, *refs[11:15])
+    send_coarse, send_fine = gather_hanging(traces, refs[17], codes, table["up"])
+    swaps(image[:, 0:SIDE], image[:, CELLS - SIDE :], send_coarse, send_fine, *refs[12:16])
+    refs[16][...] = counts
+
+
+def second_kernel(*refs):
+    refs[11][...], _ = add_faces(*refs[:11], *refs[12:])
 
 
 def total(value):
     return jnp.sum(jnp.sum(value, axis=0, keepdims=True), axis=1, keepdims=True)
 
 
-def moments_kernel(*refs):
-    source_ref, image_ref, out_ref, sums_ref = refs[10:14]
-    second = add_faces(*refs[:10], *refs[14:])
-    out_ref[...] = second
+def moments_kernel(
+    codes,
+    table_ref,
+    image_ref,
+    stiff_ref,
+    trace_ref,
+    coarse_ref,
+    partner_ref,
+    rim_chip_ref,
+    dom_odd_ref,
+    dom_even_ref,
+    rim_core_ref,
+    _sent_chip_ref,
+    sent_odd_ref,
+    sent_even_ref,
+    _sent_core_ref,
+    first_ref,
+    counts_ref,
+    source_ref,
+    sums_ref,
+):
+    table = views(table_ref)
     source = source_ref[...]
     image = image_ref[...]
-    products = [
-        source * source,
-        source * image[0:125],
-        image * image,
-        source * second[0:125],
-        image * second,
-    ]
+    side_traces = traces_beside(table["trace"], rim_chip_ref, rim_core_ref)
+    curved = total(image * applied(codes, table, stiff_ref[...], image))
+    hanging = sent_odd_ref[...] * dom_odd_ref[...] + sent_even_ref[...] * dom_even_ref[...]
+    for start in range(0, PAIR_SLOTS, CHUNK):
+        partner = partner_values(codes, partner_ref, side_traces, start)
+        hanging = hanging - TAU_PENALTY * (partner * first_ref[:, start : start + CHUNK])
+    curved = curved + total(hanging)
+    own = [trace_ref[rows, :] * value for rows, value in own_faces(counts_ref[...], trace_ref, coarse_ref)]
+    curved = curved + total(jnp.concatenate(own, axis=0))
+    sums = [total(source * source), total(source * image[0:125]), total(image * image), curved]
     lane = lax.broadcasted_iota(jnp.int32, (1, 128), 1)
     line = jnp.zeros((1, 128), F32)
-    for index, product in enumerate(products):
-        line = line + jnp.where(lane == index, total(product), 0.0)
+    for index, value in enumerate(sums):
+        line = line + jnp.where(lane == index, value, 0.0)
     sums_ref[...] = jnp.broadcast_to(line[None], sums_ref.shape)
 
 
 def last_kernel(sums_ref, source_ref, image_ref, second_ref, solution_ref, residual_ref):
     line = jnp.sum(sums_ref[...], axis=0)
-    rr, rw, ww, ru, wu = (line[:, i : i + 1] for i in range(5))
+    rr, rw, ww, wu = (line[:, i : i + 1] for i in range(4))
     first_step = rr / rw
     rr_next = rr - 2.0 * first_step * rw + first_step * first_step * ww
     grown = 1.0 + rr_next / rr
     curvature = (
-        grown * grown * rw - first_step * grown * (ru + ww) + first_step * first_step * wu
+        grown * grown * rw - 2.0 * first_step * grown * ww + first_step * first_step * wu
     )
     second_step = rr_next / curvature
     p = first_step + second_step * grown
@@ -463,8 +508,8 @@
     )(*operands)
 
 
+PAIR_CODES = pltpu.VMEM((8, PAIR_SLOTS), jnp.int32)
 FIELD = pltpu.VMEM((128, CELLS), F32)
-SIDES = pltpu.VMEM((128, 2 * SIDE), F32)
 HOT = pltpu.VMEM((CELLS, SLOTS), BF16)
 SPREAD = pltpu.VMEM((2 * STACK + 16, SLOTS), BF16)
 
@@ -518,33 +563,40 @@
     )
 
     arrays = [(128, CELLS), (TRACE, CELLS), (TRACE, CELLS), (FACE, PAIR_SLOTS)]
-    scratch = [SIDES, HOT, SPREAD]
+    scratch = [HOT, SPREAD, FIELD]
     arrived = exchange(*swapping)
-    own = call(middle_kernel, arrays, [FIELD], source, codes, table, name="middle")
-    image, *swapping = call(
+    own = call(middle_kernel, arrays, [FIELD, PAIR_CODES], source, pairs, table, name="middle")
+    image, *swapping, counts = call(
         image_kernel,
-        [(128, CELLS), *sends],
+        [(128, CELLS), *sends, (16, CELLS)],
         scratch,
         codes,
         table,
+        source,
         *own,
         *arrived,
         name="image",
     )
     arrived = exchange(*swapping)
-    own = call(middle_kernel, arrays, [FIELD], image, codes, table, name="middle")
-    second, sums = call(
+    *own, first = call(
+        middle_kernel, [*arrays, (FACE, PAIR_SLOTS)], [FIELD, PAIR_CODES], image, pairs, table, name="middle"
+    )
+    sums = call(
         moments_kernel,
-        [(128, CELLS), (lax.axis_size(PLANE), 1, 128)],
-        scratch,
+        [(lax.axis_size(PLANE), 1, 128)],
+        [],
         codes,
         table,
+        image,
         *own,
         *arrived,
+        *swapping,
+        first,
+        counts,
         source,
-        image,
         name="moments",
-    )
+    )[0]
+    second = call(second_kernel, [(128, CELLS)], scratch, codes, table, image, *own, *arrived, name="second")[0]
     sums = summed_over_blocks(sums)
     return tuple(call(last_kernel, [source.shape] * 2, [], sums, source, image, second, name="last"))
 

time: 95.2 us -> 94.9 us (level)
  blocking collectives: 35.2 us -> 12.3 us
  starting transfers between devices: 30.9 us -> 46.8 us
  waiting for transfers between devices: 14.7 us -> 20.5 us
  Pallas kernels: 12.3 us -> 13.3 us
    all_to_all x1 -> x0, blocking collectives: 22.1 us -> none  [summed_over_blocks(): lax.all_to_all(jnp.broadcast_to(other, sums.shape), PLANE, 0, 0, tiled=True)]
    all_to_all x0 -> x1, starting transfers between devices: none -> 15.4 us  [summed_over_blocks(): lax.all_to_all(jnp.broadcast_to(other, sums.shape), PLANE, 0, 0, tiled=True)]
    all_to_all x0 -> x1, waiting for transfers between devices: none -> 4.7 us  [summed_over_blocks(): lax.all_to_all(jnp.broadcast_to(other, sums.shape), PLANE, 0, 0, tiled=True)]
    pallas_call x6 -> x7, Pallas kernels: 12.3 us -> 13.3 us  [call(): pl.pallas_call(kernel, out_shape=[jax.ShapeDtypeStruct(shape, F32) for sh...]
    ppermute x1, waiting for transfers between devices: 14.6 us -> 15.7 us  [summed_over_blocks(): other = lax.ppermute(jnp.sum(sums, axis=0, keepdims=True), BLOCK, diagonal)]
  transfers between devices with their start and end apart: 9 -> 10, of which waited for: 1 -> 3; matrix products, arithmetic and copies ran while one was open for 0% -> 0% of each run, Pallas kernels for 2% -> 5%
where the time goes in v5:
time: 94.9 us; the launch traced here: 94.5 us
  starting transfers between devices  46.8 us (49%)
  waiting for transfers between devices  20.5 us (22%)
  Pallas kernels  13.3 us (14%)
  blocking collectives  12.3 us (13%)
    ppermute x8, starting transfers between devices, swapped(): lax.ppermute(value, axes, pairs + [(above, below) for below, above in pai...  29.4 us
    ppermute x1, waiting for transfers between devices, summed_over_blocks(): other = lax.ppermute(jnp.sum(sums, axis=0, keepdims=True), BLOCK, diagonal)  15.7 us
    all_to_all x1, starting transfers between devices, summed_over_blocks(): lax.all_to_all(jnp.broadcast_to(other, sums.shape), PLANE, 0, 0, tiled=True)  15.4 us
    pallas_call x7, Pallas kernels, call(): pl.pallas_call(kernel, out_shape=[jax.ShapeDtypeStruct(shape, F32) for sh...  13.3 us
    all_to_all x1, blocking collectives, summed_over_blocks(): sums = lax.all_to_all(sums, PLANE, 0, 0, tiled=True)  12.3 us
    all_to_all x1, waiting for transfers between devices, summed_over_blocks(): lax.all_to_all(jnp.broadcast_to(other, sums.shape), PLANE, 0, 0, tiled=True)  4.7 us
    ppermute x1, starting transfers between devices, summed_over_blocks(): other = lax.ppermute(jnp.sum(sums, axis=0, keepdims=True), BLOCK, diagonal)  1.98 us
  transfers between devices with their start and end apart: 10, of which 3 were waited for; matrix products, arithmetic and copies ran while one was open for 0% of the time, Pallas kernels for 5%

profile of v5, /device:TPU:1, one launch (start us, length us, event | category | flops | bytes accessed | tf_op | source)
XLA Modules:
  0.0 94.5 jit_solution(8136126113431708736)
XLA Ops:
  0.6 0.0 copy-start
  0.7 3.6 %first.1 = (f32[128,128]{1,0:T(8,128)}, f32[32,512]{1,0:T(8,128)}, f32[32,512]{1,0:T(8,128)}, f32[128,128]{1,0:T(8,128)}, f32[16,1024]{1,0:T(8,128)}) custom-call(f32[125,512]{1,0:T(8,128)} %source_ref.3, s32[1,512]{1,0:T(1,128)} %bitcast.6, s32[1,512]{1,0:T(1,128)} %bitcast.7, f32[1,64]{1,0:T(1,128)} %bitcast.11, s32[2,960]{1,0:T(2,128)} %pairs_ref.3, ...), custom_call_target="tpu_custom_call" | custom-call | tf_op jit(solution)/shard_map/first/pallas_call | solution.py:500
  4.2 4.6 %collective-permute-start = (f32[128,128]{1,0:T(8,128)}, f32[128,128]{1,0:T(8,128)S(1)}, u32[]{:S(2)}, u32[]{:S(2)}) collective-permute-start(f32[128,128]{1,0:T(8,128)} %get-tuple-element.27), channel_id=1, source_target_pairs={{1,2},{3,4},{5,6},{7,8},{9,10},{11,12},{13,14},{15,16},{17,18},{19... | collective-permute-start | bytes 196616 | tf_op jit(solution)/shard_map/ppermute | solution.py:520
  8.8 0.7 collective-permute-start.1
  9.5 5.6 %collective-permute-start.2 = (f32[32,512]{1,0:T(8,128)}, f32[32,512]{1,0:T(8,128)S(1)}, u32[]{:S(2)}, u32[]{:S(2)}) collective-permute-start(f32[32,512]{1,0:T(8,128)} %get-tuple-element.29), channel_id=1, source_target_pairs={{0,8},{16,24},{32,40},{48,56},{64,72},{80,88},{96,104},{112,120},{... | collective-permute-start | bytes 196616 | tf_op jit(solution)/shard_map/ppermute | solution.py:520
  15.1 8.6 %collective-permute-start.3 = (f32[128,128]{1,0:T(8,128)}, f32[128,128]{1,0:T(8,128)S(1)}, u32[]{:S(2)}, u32[]{:S(2)}) collective-permute-start(f32[128,128]{1,0:T(8,128)} %get-tuple-element.30), channel_id=1, source_target_pairs={{0,1},{2,3},{4,5},{6,7},{8,9},{10,11},{12,13},{14,15},{16,17},{18,... | collective-permute-start | bytes 196616 | tf_op jit(solution)/shard_map/ppermute | solution.py:520
  23.8 1.0 %middle.2 = (f32[128,512]{1,0:T(8,128)S(1)}, f32[160,512]{1,0:T(8,128)S(1)}, f32[160,512]{1,0:T(8,128)S(1)}, f32[32,1024]{1,0:T(8,128)S(1)}) custom-call(f32[125,512]{1,0:T(8,128)S(1)} %copy-done.1, s32[2,960]{1,0:T(2,128)S(1)} %copy-done.3, bf16[1024,256]{1,0:T(8,128)(2,1)S(1)} %copy-done), custom_call_target="tpu_custom_call" | custom-call | tf_op jit(solution)/shard_map/middle/pallas_call | solution.py:500
  24.7 0.1 collective-permute-done.3.refs_10_
  24.8 3.5 %image.1 = (f32[128,512]{1,0:T(8,128)S(1)}, f32[128,128]{1,0:T(8,128)S(1)}, f32[32,512]{1,0:T(8,128)S(1)}, f32[32,512]{1,0:T(8,128)S(1)}, f32[128,128]{1,0:T(8,128)S(1)}, /*index=5*/f32[16,512]{1,0:T(8,128)S(1)}) custom-call(f32[16,1024]{1,0:T(8,128)S(1)} %copy-done.2, bf16[1024,256]{1,0:T(8,128)(2,1)S(1)} %copy-done, f32[125,512]{1,0:T(8,128)S(1)} %copy-done.1, ...), custom_call_target="tpu_custom_call" | custom-call | tf_op jit(solution)/shard_map/image/pallas_call | solution.py:500
  28.3 1.9 %collective-permute-start.4 = (f32[128,128]{1,0:T(8,128)S(1)}, f32[128,128]{1,0:T(8,128)S(1)}, u32[]{:S(2)}, u32[]{:S(2)}) collective-permute-start(f32[128,128]{1,0:T(8,128)S(1)} %get-tuple-element.36._sent_chip_ref), channel_id=1, source_target_pairs={{1,2},{3,4},{5,6},{7,8},{9,10},{11,12},{13,14},{15,16},{17,18},{19... | collective-permute-start | bytes 196616 | tf_op jit(solution)/shard_map/ppermute | solution.py:520
  30.2 0.7 collective-permute-start.5
  30.9 4.9 %collective-permute-start.6 = (f32[32,512]{1,0:T(8,128)S(1)}, f32[32,512]{1,0:T(8,128)S(1)}, u32[]{:S(2)}, u32[]{:S(2)}) collective-permute-start(f32[32,512]{1,0:T(8,128)S(1)} %get-tuple-element.38.sent_even_ref), channel_id=1, source_target_pairs={{0,8},{16,24},{32,40},{48,56},{64,72},{80,88},{96,104},{112,120},{... | collective-permute-start | bytes 196616 | tf_op jit(solution)/shard_map/ppermute | solution.py:520
  35.8 2.5 %collective-permute-start.7 = (f32[128,128]{1,0:T(8,128)S(1)}, f32[128,128]{1,0:T(8,128)S(1)}, u32[]{:S(2)}, u32[]{:S(2)}) collective-permute-start(f32[128,128]{1,0:T(8,128)S(1)} %get-tuple-element.39._sent_core_ref), channel_id=1, source_target_pairs={{0,1},{2,3},{4,5},{6,7},{8,9},{10,11},{12,13},{14,15},{16,17},{18,... | collective-permute-start | bytes 196616 | tf_op jit(solution)/shard_map/ppermute | solution.py:520
  38.3 1.4 %middle.3 = (f32[128,512]{1,0:T(8,128)S(1)}, f32[160,512]{1,0:T(8,128)S(1)}, f32[160,512]{1,0:T(8,128)S(1)}, f32[32,1024]{1,0:T(8,128)S(1)}, f32[32,1024]{1,0:T(8,128)S(1)}) custom-call(f32[128,512]{1,0:T(8,128)S(1)} %get-tuple-element.31.field_ref.image_ref.refs_2_, s32[2,960]{1,0:T(2,128)S(1)} %copy-done.3, bf16[1024,256]{1,0:T(8,128)(2,1)S(1)} %copy-done), custom_call_target="tpu_custom_call" | custom-call | tf_op jit(solution)/shard_map/middle/pallas_call | solution.py:500
  39.8 0.7 moments.1
  40.5 12.3 %all_to_all.10 = f32[32,1,128]{2,1,0:T(1,128)S(1)} all-to-all(f32[32,1,128]{2,1,0:T(1,128)S(1)} %moments.1), channel_id=1, replica_groups=mesh['z'=32,'x'=4,'y'=4,'core'=2] {'x','y','core'}, dimensions={0} | all-to-all | bytes 32768 | tf_op jit(solution)/shard_map/all_to_all | solution.py:533
  52.8 0.1 reduce_sum.9
  52.9 2.0 %collective-permute-start.8 = (f32[1,1,128]{2,1,0:T(1,128)S(1)}, f32[1,1,128]{2,1,0:T(1,128)S(1)}, u32[]{:S(2)}, u32[]{:S(2)}) collective-permute-start(f32[1,1,128]{2,1,0:T(1,128)S(1)} %bitcast.9), channel_id=1, source_target_pairs={{0,0},{1,33},{2,66},{3,99},{4,132},{5,165},{6,198},{7,231},{8,264}... | collective-permute-start | bytes 1544 | tf_op jit(solution)/shard_map/ppermute | solution.py:539
  54.9 15.7 %collective-permute-done.8 = f32[1,1,128]{2,1,0:T(1,128)S(1)} collective-permute-done((f32[1,1,128]{2,1,0:T(1,128)S(1)}, f32[1,1,128]{2,1,0:T(1,128)S(1)}, u32[]{:S(2)}, u32[]{:S(2)}) %collective-permute-start.8) | collective-permute-done | bytes 544 | tf_op jit(solution)/shard_map/ppermute | solution.py:539
  70.6 0.6 broadcast_in_dim.12
  71.2 15.4 %all-to-all-start.1 = ((f32[32,1,128]{2,1,0:T(1,128)}), f32[32,1,128]{2,1,0:T(1,128)S(1)}, u32[]{:S(2)}, u32[]{:S(2)}) async-start(f32[32,1,128]{2,1,0:T(1,128)} %broadcast_in_dim.12), calls=%async_computation.1 | async-start | bytes 32768 | tf_op jit(solution)/shard_map/all_to_all | solution.py:540
  86.6 2.2 %second.1.second_ref = f32[128,512]{1,0:T(8,128)S(1)} custom-call(f32[16,1024]{1,0:T(8,128)S(1)} %copy-done.2, bf16[1024,256]{1,0:T(8,128)(2,1)S(1)} %copy-done, f32[128,512]{1,0:T(8,128)S(1)} %get-tuple-element.31.field_ref.image_ref.refs_2_, f32[128,512]{1,0:T(8,128)S(1)} %get-tuple-element.32.stiff_ref.refs_3_, ...), custom_call_target="tpu_custom_call" | custom-call | tf_op jit(solution)/shard_map/second/pallas_call | solution.py:500
  88.7 4.7 %all-to-all-done.1.sums_ref = f32[32,1,128]{2,1,0:T(1,128)S(1)} async-done(((f32[32,1,128]{2,1,0:T(1,128)}), f32[32,1,128]{2,1,0:T(1,128)S(1)}, u32[]{:S(2)}, u32[]{:S(2)}) %all-to-all-start.1) | async-done | bytes 16416 | tf_op jit(solution)/shard_map/all_to_all | solution.py:540
  93.4 1.0 %last.1 = (f32[125,512]{1,0:T(8,128)}, f32[125,512]{1,0:T(8,128)}) custom-call(f32[32,1,128]{2,1,0:T(1,128)S(1)} %all-to-all-done.1.sums_ref, f32[125,512]{1,0:T(8,128)S(1)} %copy-done.1, f32[128,512]{1,0:T(8,128)S(1)} %get-tuple-element.31.field_ref.image_ref.refs_2_, f32[128,512]{1,0:T(8,128)S(1)} %second.1.second_ref), custom_call_target="tpu_custom_call" | custom-call | tf_op jit(solution)/shard_map/last/pallas_call | solution.py:500
  (14 shorter events, 0.0 us)
Async XLA Ops:
  0.6 23.1 %copy-start = (bf16[1024,256]{1,0:T(8,128)(2,1)S(1)}, bf16[1024,256]{1,0:T(8,128)(2,1)}, u32[]{:S(2)}) copy-start(bf16[1024,256]{1,0:T(8,128)(2,1)} %constant.4.clone.refs_7_.table_ref.refs_1_) | copy-start | bytes 1572868
  0.6 23.1 %copy-start.1 = (f32[125,512]{1,0:T(8,128)S(1)}, f32[125,512]{1,0:T(8,128)}, u32[]{:S(2)}) copy-start(f32[125,512]{1,0:T(8,128)} %source_ref.3) | copy-start | bytes 768004
  0.7 23.1 %copy-start.3 = (s32[2,960]{1,0:T(2,128)S(1)}, s32[2,960]{1,0:T(2,128)}, u32[]{:S(2)}) copy-start(s32[2,960]{1,0:T(2,128)} %pairs_ref.3) | copy-start | bytes 23044
  4.2 20.5 %collective-permute-start = (f32[128,128]{1,0:T(8,128)}, f32[128,128]{1,0:T(8,128)S(1)}, u32[]{:S(2)}, u32[]{:S(2)}) collective-permute-start(f32[128,128]{1,0:T(8,128)} %get-tuple-element.27), channel_id=1, source_target_pairs={{1,2},{3,4},{5,6},{7,8},{9,10},{11,12},{13,14},{15,16},{17,18},{19... | collective-permute-start | bytes 196616 | tf_op jit(solution)/shard_map/ppermute | solution.py:520
  8.8 15.9 %collective-permute-start.1 = (f32[32,512]{1,0:T(8,128)}, f32[32,512]{1,0:T(8,128)S(1)}, u32[]{:S(2)}, u32[]{:S(2)}) collective-permute-start(f32[32,512]{1,0:T(8,128)} %get-tuple-element.28), channel_id=1, source_target_pairs={{8,16},{24,32},{40,48},{56,64},{72,80},{88,96},{104,112},{120,128}... | collective-permute-start | bytes 196616 | tf_op jit(solution)/shard_map/ppermute | solution.py:520
  9.5 15.2 %collective-permute-start.2 = (f32[32,512]{1,0:T(8,128)}, f32[32,512]{1,0:T(8,128)S(1)}, u32[]{:S(2)}, u32[]{:S(2)}) collective-permute-start(f32[32,512]{1,0:T(8,128)} %get-tuple-element.29), channel_id=1, source_target_pairs={{0,8},{16,24},{32,40},{48,56},{64,72},{80,88},{96,104},{112,120},{... | collective-permute-start | bytes 196616 | tf_op jit(solution)/shard_map/ppermute | solution.py:520
  15.1 9.7 %copy-start.2 = (f32[16,1024]{1,0:T(8,128)S(1)}, f32[16,1024]{1,0:T(8,128)}, u32[]{:S(2)}) copy-start(f32[16,1024]{1,0:T(8,128)} %get-tuple-element.22.refs_0_.codes) | copy-start | bytes 196612
  15.1 9.7 %collective-permute-start.3 = (f32[128,128]{1,0:T(8,128)}, f32[128,128]{1,0:T(8,128)S(1)}, u32[]{:S(2)}, u32[]{:S(2)}) collective-permute-start(f32[128,128]{1,0:T(8,128)} %get-tuple-element.30), channel_id=1, source_target_pairs={{0,1},{2,3},{4,5},{6,7},{8,9},{10,11},{12,13},{14,15},{16,17},{18,... | collective-permute-start | bytes 196616 | tf_op jit(solution)/shard_map/ppermute | solution.py:520
  28.3 11.5 %collective-permute-start.4 = (f32[128,128]{1,0:T(8,128)S(1)}, f32[128,128]{1,0:T(8,128)S(1)}, u32[]{:S(2)}, u32[]{:S(2)}) collective-permute-start(f32[128,128]{1,0:T(8,128)S(1)} %get-tuple-element.36._sent_chip_ref), channel_id=1, source_target_pairs={{1,2},{3,4},{5,6},{7,8},{9,10},{11,12},{13,14},{15,16},{17,18},{19... | collective-permute-start | bytes 196616 | tf_op jit(solution)/shard_map/ppermute | solution.py:520
  30.2 9.6 %collective-permute-start.5 = (f32[32,512]{1,0:T(8,128)S(1)}, f32[32,512]{1,0:T(8,128)S(1)}, u32[]{:S(2)}, u32[]{:S(2)}) collective-permute-start(f32[32,512]{1,0:T(8,128)S(1)} %get-tuple-element.37.sent_odd_ref), channel_id=1, source_target_pairs={{8,16},{24,32},{40,48},{56,64},{72,80},{88,96},{104,112},{120,128}... | collective-permute-start | bytes 196616 | tf_op jit(solution)/shard_map/ppermute | solution.py:520
  30.9 8.9 %collective-permute-start.6 = (f32[32,512]{1,0:T(8,128)S(1)}, f32[32,512]{1,0:T(8,128)S(1)}, u32[]{:S(2)}, u32[]{:S(2)}) collective-permute-start(f32[32,512]{1,0:T(8,128)S(1)} %get-tuple-element.38.sent_even_ref), channel_id=1, source_target_pairs={{0,8},{16,24},{32,40},{48,56},{64,72},{80,88},{96,104},{112,120},{... | collective-permute-start | bytes 196616 | tf_op jit(solution)/shard_map/ppermute | solution.py:520
  35.8 4.0 %collective-permute-start.7 = (f32[128,128]{1,0:T(8,128)S(1)}, f32[128,128]{1,0:T(8,128)S(1)}, u32[]{:S(2)}, u32[]{:S(2)}) collective-permute-start(f32[128,128]{1,0:T(8,128)S(1)} %get-tuple-element.39._sent_core_ref), channel_id=1, source_target_pairs={{0,1},{2,3},{4,5},{6,7},{8,9},{10,11},{12,13},{14,15},{16,17},{18,... | collective-permute-start | bytes 196616 | tf_op jit(solution)/shard_map/ppermute | solution.py:520
  52.9 17.7 %collective-permute-start.8 = (f32[1,1,128]{2,1,0:T(1,128)S(1)}, f32[1,1,128]{2,1,0:T(1,128)S(1)}, u32[]{:S(2)}, u32[]{:S(2)}) collective-permute-start(f32[1,1,128]{2,1,0:T(1,128)S(1)} %bitcast.9), channel_id=1, source_target_pairs={{0,0},{1,33},{2,66},{3,99},{4,132},{5,165},{6,198},{7,231},{8,264}... | collective-permute-start | bytes 1544 | tf_op jit(solution)/shard_map/ppermute | solution.py:539
  71.2 22.2 %all-to-all-start.1 = ((f32[32,1,128]{2,1,0:T(1,128)}), f32[32,1,128]{2,1,0:T(1,128)S(1)}, u32[]{:S(2)}, u32[]{:S(2)}) async-start(f32[32,1,128]{2,1,0:T(1,128)} %broadcast_in_dim.12), calls=%async_computation.1 | async-start | bytes 32768 | tf_op jit(solution)/shard_map/all_to_all | solution.py:540

commit v6 on v5

--- a/solution.py
+++ b/solution.py
@@ -255,7 +255,7 @@
     return joined(*face_traces(trace_ref, field))
 
 
-def swaps(low, high, send_coarse, send_fine, rim_chip_ref, dom_odd_ref, dom_even_ref, rim_core_ref):
+def swaps(low, high, send_coarse, send_fine, dom_odd_ref, rim_chip_ref, dom_even_ref, rim_core_ref):
     first_core = lax.axis_index("core") == 0
     even_dom = lax.axis_index("x") % 2 == 0
     rim_core_ref[...] = jnp.where(first_core, high, low)
@@ -364,8 +364,8 @@
     trace_in_ref,
     coarse_in_ref,
     partner_ref,
+    dom_odd_ref,
     rim_chip_ref,
-    dom_odd_ref,
     dom_even_ref,
     rim_core_ref,
     hot,
@@ -445,12 +445,12 @@
     trace_ref,
     coarse_ref,
     partner_ref,
+    dom_odd_ref,
     rim_chip_ref,
-    dom_odd_ref,
     dom_even_ref,
     rim_core_ref,
+    sent_odd_ref,
     _sent_chip_ref,
-    sent_odd_ref,
     sent_even_ref,
     _sent_core_ref,
     first_ref,
@@ -520,12 +520,12 @@
     return lax.ppermute(value, axes, pairs + [(above, below) for below, above in pairs])
 
 
-def exchange(rim_chip, dom_odd, dom_even, rim_core):
+def exchange(dom_odd, rim_chip, dom_even, rim_core):
     rim_chip = swapped(rim_chip, BLOCK, 1)
     dom_odd = swapped(dom_odd, DOM, 1)
     dom_even = swapped(dom_even, DOM, 0)
     rim_core = swapped(rim_core, BLOCK, 0)
-    return rim_chip, dom_odd, dom_even, rim_core
+    return dom_odd, rim_chip, dom_even, rim_core
 
 
 def summed_over_blocks(sums):
@@ -543,7 +543,7 @@
 def on_device(source, levels, ids, values, pairs, coarse, fine):
     levels, ids, values, coarse = (a.reshape(1, -1) for a in (levels, ids, values, coarse))
     table = jnp.asarray(packed_table())
-    sends = [(128, SIDE), (FACE, CELLS), (FACE, CELLS), (128, SIDE)]
+    sends = [(FACE, CELLS), (128, SIDE), (FACE, CELLS), (128, SIDE)]
     params = (source, levels, ids, values, pairs, coarse, fine)
     *swapping, codes = call(
         first_kernel,

time: 94.9 us -> 94.1 us (level)
  waiting for transfers between devices: 20.5 us -> 17.8 us
  starting transfers between devices: 46.8 us -> 48.3 us
    ppermute x1, waiting for transfers between devices: 15.7 us -> 13 us  [summed_over_blocks(): other = lax.ppermute(jnp.sum(sums, axis=0, keepdims=True), BLOCK, diagonal)]
    all_to_all x1, starting transfers between devices: 15.4 us -> 16.7 us  [summed_over_blocks(): lax.all_to_all(jnp.broadcast_to(other, sums.shape), PLANE, 0, 0, tiled=True)]
where the time goes in v6:
time: 94.1 us; the launch traced here: 93.6 us
  starting transfers between devices  48.3 us (51%)
  waiting for transfers between devices  17.8 us (19%)
  Pallas kernels  13.3 us (14%)
  blocking collectives  12.7 us (13%)
    ppermute x8, starting transfers between devices, swapped(): lax.ppermute(value, axes, pairs + [(above, below) for below, above in pai...  29.4 us
    all_to_all x1, starting transfers between devices, summed_over_blocks(): lax.all_to_all(jnp.broadcast_to(other, sums.shape), PLANE, 0, 0, tiled=True)  16.7 us
    pallas_call x7, Pallas kernels, call(): pl.pallas_call(kernel, out_shape=[jax.ShapeDtypeStruct(shape, F32) for sh...  13.3 us
    ppermute x1, waiting for transfers between devices, summed_over_blocks(): other = lax.ppermute(jnp.sum(sums, axis=0, keepdims=True), BLOCK, diagonal)  13 us
    all_to_all x1, blocking collectives, summed_over_blocks(): sums = lax.all_to_all(sums, PLANE, 0, 0, tiled=True)  12.7 us
    all_to_all x1, waiting for transfers between devices, summed_over_blocks(): lax.all_to_all(jnp.broadcast_to(other, sums.shape), PLANE, 0, 0, tiled=True)  4.7 us
    ppermute x1, starting transfers between devices, summed_over_blocks(): other = lax.ppermute(jnp.sum(sums, axis=0, keepdims=True), BLOCK, diagonal)  2.11 us
  transfers between devices with their start and end apart: 10, of which 3 were waited for; matrix products, arithmetic and copies ran while one was open for 0% of the time, Pallas kernels for 5%

profile of v6, /device:TPU:1, one launch (start us, length us, event | category | flops | bytes accessed | tf_op | source)
XLA Modules:
  0.0 93.6 jit_solution(13254470627612370657)
XLA Ops:
  0.6 0.0 copy-start
  0.7 3.6 %first.1 = (f32[32,512]{1,0:T(8,128)}, f32[128,128]{1,0:T(8,128)}, f32[32,512]{1,0:T(8,128)}, f32[128,128]{1,0:T(8,128)}, f32[16,1024]{1,0:T(8,128)}) custom-call(f32[125,512]{1,0:T(8,128)} %source_ref.3, s32[1,512]{1,0:T(1,128)} %bitcast.6, s32[1,512]{1,0:T(1,128)} %bitcast.7, f32[1,64]{1,0:T(1,128)} %bitcast.11, s32[2,960]{1,0:T(2,128)} %pairs_ref.3, ...), custom_call_target="tpu_custom_call" | custom-call | tf_op jit(solution)/shard_map/first/pallas_call | solution.py:500
  4.2 0.7 collective-permute-start
  4.9 4.6 %collective-permute-start.1 = (f32[128,128]{1,0:T(8,128)}, f32[128,128]{1,0:T(8,128)S(1)}, u32[]{:S(2)}, u32[]{:S(2)}) collective-permute-start(f32[128,128]{1,0:T(8,128)} %get-tuple-element.28), channel_id=1, source_target_pairs={{1,2},{3,4},{5,6},{7,8},{9,10},{11,12},{13,14},{15,16},{17,18},{19... | collective-permute-start | bytes 196616 | tf_op jit(solution)/shard_map/ppermute | solution.py:520
  9.5 5.9 %collective-permute-start.2 = (f32[32,512]{1,0:T(8,128)}, f32[32,512]{1,0:T(8,128)S(1)}, u32[]{:S(2)}, u32[]{:S(2)}) collective-permute-start(f32[32,512]{1,0:T(8,128)} %get-tuple-element.29), channel_id=1, source_target_pairs={{0,8},{16,24},{32,40},{48,56},{64,72},{80,88},{96,104},{112,120},{... | collective-permute-start | bytes 196616 | tf_op jit(solution)/shard_map/ppermute | solution.py:520
  15.4 8.3 %collective-permute-start.3 = (f32[128,128]{1,0:T(8,128)}, f32[128,128]{1,0:T(8,128)S(1)}, u32[]{:S(2)}, u32[]{:S(2)}) collective-permute-start(f32[128,128]{1,0:T(8,128)} %get-tuple-element.30), channel_id=1, source_target_pairs={{0,1},{2,3},{4,5},{6,7},{8,9},{10,11},{12,13},{14,15},{16,17},{18,... | collective-permute-start | bytes 196616 | tf_op jit(solution)/shard_map/ppermute | solution.py:520
  23.8 1.0 %middle.2 = (f32[128,512]{1,0:T(8,128)S(1)}, f32[160,512]{1,0:T(8,128)S(1)}, f32[160,512]{1,0:T(8,128)S(1)}, f32[32,1024]{1,0:T(8,128)S(1)}) custom-call(f32[125,512]{1,0:T(8,128)S(1)} %copy-done.1, s32[2,960]{1,0:T(2,128)S(1)} %copy-done.3, bf16[1024,256]{1,0:T(8,128)(2,1)S(1)} %copy-done), custom_call_target="tpu_custom_call" | custom-call | tf_op jit(solution)/shard_map/middle/pallas_call | solution.py:500
  24.7 0.1 collective-permute-done.3.refs_10_
  24.8 3.5 %image.1 = (f32[128,512]{1,0:T(8,128)S(1)}, f32[32,512]{1,0:T(8,128)S(1)}, f32[128,128]{1,0:T(8,128)S(1)}, f32[32,512]{1,0:T(8,128)S(1)}, f32[128,128]{1,0:T(8,128)S(1)}, /*index=5*/f32[16,512]{1,0:T(8,128)S(1)}) custom-call(f32[16,1024]{1,0:T(8,128)S(1)} %copy-done.2, bf16[1024,256]{1,0:T(8,128)(2,1)S(1)} %copy-done, f32[125,512]{1,0:T(8,128)S(1)} %copy-done.1, ...), custom_call_target="tpu_custom_call" | custom-call | tf_op jit(solution)/shard_map/image/pallas_call | solution.py:500
  28.3 0.7 collective-permute-start.4
  29.0 1.9 %collective-permute-start.5 = (f32[128,128]{1,0:T(8,128)S(1)}, f32[128,128]{1,0:T(8,128)S(1)}, u32[]{:S(2)}, u32[]{:S(2)}) collective-permute-start(f32[128,128]{1,0:T(8,128)S(1)} %get-tuple-element.37._sent_chip_ref), channel_id=1, source_target_pairs={{1,2},{3,4},{5,6},{7,8},{9,10},{11,12},{13,14},{15,16},{17,18},{19... | collective-permute-start | bytes 196616 | tf_op jit(solution)/shard_map/ppermute | solution.py:520
  30.9 4.9 %collective-permute-start.6 = (f32[32,512]{1,0:T(8,128)S(1)}, f32[32,512]{1,0:T(8,128)S(1)}, u32[]{:S(2)}, u32[]{:S(2)}) collective-permute-start(f32[32,512]{1,0:T(8,128)S(1)} %get-tuple-element.38.sent_even_ref), channel_id=1, source_target_pairs={{0,8},{16,24},{32,40},{48,56},{64,72},{80,88},{96,104},{112,120},{... | collective-permute-start | bytes 196616 | tf_op jit(solution)/shard_map/ppermute | solution.py:520
  35.8 2.5 %collective-permute-start.7 = (f32[128,128]{1,0:T(8,128)S(1)}, f32[128,128]{1,0:T(8,128)S(1)}, u32[]{:S(2)}, u32[]{:S(2)}) collective-permute-start(f32[128,128]{1,0:T(8,128)S(1)} %get-tuple-element.39._sent_core_ref), channel_id=1, source_target_pairs={{0,1},{2,3},{4,5},{6,7},{8,9},{10,11},{12,13},{14,15},{16,17},{18,... | collective-permute-start | bytes 196616 | tf_op jit(solution)/shard_map/ppermute | solution.py:520
  38.3 1.4 %middle.3 = (f32[128,512]{1,0:T(8,128)S(1)}, f32[160,512]{1,0:T(8,128)S(1)}, f32[160,512]{1,0:T(8,128)S(1)}, f32[32,1024]{1,0:T(8,128)S(1)}, f32[32,1024]{1,0:T(8,128)S(1)}) custom-call(f32[128,512]{1,0:T(8,128)S(1)} %get-tuple-element.31.field_ref.image_ref.refs_2_, s32[2,960]{1,0:T(2,128)S(1)} %copy-done.3, bf16[1024,256]{1,0:T(8,128)(2,1)S(1)} %copy-done), custom_call_target="tpu_custom_call" | custom-call | tf_op jit(solution)/shard_map/middle/pallas_call | solution.py:500
  39.8 0.7 moments.1
  40.5 12.7 %all_to_all.10 = f32[32,1,128]{2,1,0:T(1,128)S(1)} all-to-all(f32[32,1,128]{2,1,0:T(1,128)S(1)} %moments.1), channel_id=1, replica_groups=mesh['z'=32,'x'=4,'y'=4,'core'=2] {'x','y','core'}, dimensions={0} | all-to-all | bytes 32768 | tf_op jit(solution)/shard_map/all_to_all | solution.py:533
  53.2 0.1 reduce_sum.9
  53.3 2.1 %collective-permute-start.8 = (f32[1,1,128]{2,1,0:T(1,128)S(1)}, f32[1,1,128]{2,1,0:T(1,128)S(1)}, u32[]{:S(2)}, u32[]{:S(2)}) collective-permute-start(f32[1,1,128]{2,1,0:T(1,128)S(1)} %bitcast.9), channel_id=1, source_target_pairs={{0,0},{1,33},{2,66},{3,99},{4,132},{5,165},{6,198},{7,231},{8,264}... | collective-permute-start | bytes 1544 | tf_op jit(solution)/shard_map/ppermute | solution.py:539
  55.4 13.0 %collective-permute-done.8 = f32[1,1,128]{2,1,0:T(1,128)S(1)} collective-permute-done((f32[1,1,128]{2,1,0:T(1,128)S(1)}, f32[1,1,128]{2,1,0:T(1,128)S(1)}, u32[]{:S(2)}, u32[]{:S(2)}) %collective-permute-start.8) | collective-permute-done | bytes 544 | tf_op jit(solution)/shard_map/ppermute | solution.py:539
  68.4 0.6 broadcast_in_dim.12
  69.1 16.7 %all-to-all-start.1 = ((f32[32,1,128]{2,1,0:T(1,128)}), f32[32,1,128]{2,1,0:T(1,128)S(1)}, u32[]{:S(2)}, u32[]{:S(2)}) async-start(f32[32,1,128]{2,1,0:T(1,128)} %broadcast_in_dim.12), calls=%async_computation.1 | async-start | bytes 32768 | tf_op jit(solution)/shard_map/all_to_all | solution.py:540
  85.8 2.2 %second.1.second_ref = f32[128,512]{1,0:T(8,128)S(1)} custom-call(f32[16,1024]{1,0:T(8,128)S(1)} %copy-done.2, bf16[1024,256]{1,0:T(8,128)(2,1)S(1)} %copy-done, f32[128,512]{1,0:T(8,128)S(1)} %get-tuple-element.31.field_ref.image_ref.refs_2_, f32[128,512]{1,0:T(8,128)S(1)} %get-tuple-element.32.stiff_ref.refs_3_, ...), custom_call_target="tpu_custom_call" | custom-call | tf_op jit(solution)/shard_map/second/pallas_call | solution.py:500
  87.9 4.7 %all-to-all-done.1.sums_ref = f32[32,1,128]{2,1,0:T(1,128)S(1)} async-done(((f32[32,1,128]{2,1,0:T(1,128)}), f32[32,1,128]{2,1,0:T(1,128)S(1)}, u32[]{:S(2)}, u32[]{:S(2)}) %all-to-all-start.1) | async-done | bytes 16416 | tf_op jit(solution)/shard_map/all_to_all | solution.py:540
  92.6 1.0 %last.1 = (f32[125,512]{1,0:T(8,128)}, f32[125,512]{1,0:T(8,128)}) custom-call(f32[32,1,128]{2,1,0:T(1,128)S(1)} %all-to-all-done.1.sums_ref, f32[125,512]{1,0:T(8,128)S(1)} %copy-done.1, f32[128,512]{1,0:T(8,128)S(1)} %get-tuple-element.31.field_ref.image_ref.refs_2_, f32[128,512]{1,0:T(8,128)S(1)} %second.1.second_ref), custom_call_target="tpu_custom_call" | custom-call | tf_op jit(solution)/shard_map/last/pallas_call | solution.py:500
  (14 shorter events, 0.0 us)
Async XLA Ops:
  0.6 23.1 %copy-start = (bf16[1024,256]{1,0:T(8,128)(2,1)S(1)}, bf16[1024,256]{1,0:T(8,128)(2,1)}, u32[]{:S(2)}) copy-start(bf16[1024,256]{1,0:T(8,128)(2,1)} %constant.4.clone.refs_7_.table_ref.refs_1_) | copy-start | bytes 1572868
  0.6 23.1 %copy-start.1 = (f32[125,512]{1,0:T(8,128)S(1)}, f32[125,512]{1,0:T(8,128)}, u32[]{:S(2)}) copy-start(f32[125,512]{1,0:T(8,128)} %source_ref.3) | copy-start | bytes 768004
  0.7 23.1 %copy-start.3 = (s32[2,960]{1,0:T(2,128)S(1)}, s32[2,960]{1,0:T(2,128)}, u32[]{:S(2)}) copy-start(s32[2,960]{1,0:T(2,128)} %pairs_ref.3) | copy-start | bytes 23044
  4.2 20.5 %collective-permute-start = (f32[32,512]{1,0:T(8,128)}, f32[32,512]{1,0:T(8,128)S(1)}, u32[]{:S(2)}, u32[]{:S(2)}) collective-permute-start(f32[32,512]{1,0:T(8,128)} %get-tuple-element.27), channel_id=1, source_target_pairs={{8,16},{24,32},{40,48},{56,64},{72,80},{88,96},{104,112},{120,128}... | collective-permute-start | bytes 196616 | tf_op jit(solution)/shard_map/ppermute | solution.py:520
  4.9 19.8 %collective-permute-start.1 = (f32[128,128]{1,0:T(8,128)}, f32[128,128]{1,0:T(8,128)S(1)}, u32[]{:S(2)}, u32[]{:S(2)}) collective-permute-start(f32[128,128]{1,0:T(8,128)} %get-tuple-element.28), channel_id=1, source_target_pairs={{1,2},{3,4},{5,6},{7,8},{9,10},{11,12},{13,14},{15,16},{17,18},{19... | collective-permute-start | bytes 196616 | tf_op jit(solution)/shard_map/ppermute | solution.py:520
  9.5 15.2 %collective-permute-start.2 = (f32[32,512]{1,0:T(8,128)}, f32[32,512]{1,0:T(8,128)S(1)}, u32[]{:S(2)}, u32[]{:S(2)}) collective-permute-start(f32[32,512]{1,0:T(8,128)} %get-tuple-element.29), channel_id=1, source_target_pairs={{0,8},{16,24},{32,40},{48,56},{64,72},{80,88},{96,104},{112,120},{... | collective-permute-start | bytes 196616 | tf_op jit(solution)/shard_map/ppermute | solution.py:520
  15.4 9.4 %copy-start.2 = (f32[16,1024]{1,0:T(8,128)S(1)}, f32[16,1024]{1,0:T(8,128)}, u32[]{:S(2)}) copy-start(f32[16,1024]{1,0:T(8,128)} %get-tuple-element.22.refs_0_.codes) | copy-start | bytes 196612
  15.4 9.4 %collective-permute-start.3 = (f32[128,128]{1,0:T(8,128)}, f32[128,128]{1,0:T(8,128)S(1)}, u32[]{:S(2)}, u32[]{:S(2)}) collective-permute-start(f32[128,128]{1,0:T(8,128)} %get-tuple-element.30), channel_id=1, source_target_pairs={{0,1},{2,3},{4,5},{6,7},{8,9},{10,11},{12,13},{14,15},{16,17},{18,... | collective-permute-start | bytes 196616 | tf_op jit(solution)/shard_map/ppermute | solution.py:520
  28.3 11.5 %collective-permute-start.4 = (f32[32,512]{1,0:T(8,128)S(1)}, f32[32,512]{1,0:T(8,128)S(1)}, u32[]{:S(2)}, u32[]{:S(2)}) collective-permute-start(f32[32,512]{1,0:T(8,128)S(1)} %get-tuple-element.36.sent_odd_ref), channel_id=1, source_target_pairs={{8,16},{24,32},{40,48},{56,64},{72,80},{88,96},{104,112},{120,128}... | collective-permute-start | bytes 196616 | tf_op jit(solution)/shard_map/ppermute | solution.py:520
  29.0 10.8 %collective-permute-start.5 = (f32[128,128]{1,0:T(8,128)S(1)}, f32[128,128]{1,0:T(8,128)S(1)}, u32[]{:S(2)}, u32[]{:S(2)}) collective-permute-start(f32[128,128]{1,0:T(8,128)S(1)} %get-tuple-element.37._sent_chip_ref), channel_id=1, source_target_pairs={{1,2},{3,4},{5,6},{7,8},{9,10},{11,12},{13,14},{15,16},{17,18},{19... | collective-permute-start | bytes 196616 | tf_op jit(solution)/shard_map/ppermute | solution.py:520
  30.9 8.9 %collective-permute-start.6 = (f32[32,512]{1,0:T(8,128)S(1)}, f32[32,512]{1,0:T(8,128)S(1)}, u32[]{:S(2)}, u32[]{:S(2)}) collective-permute-start(f32[32,512]{1,0:T(8,128)S(1)} %get-tuple-element.38.sent_even_ref), channel_id=1, source_target_pairs={{0,8},{16,24},{32,40},{48,56},{64,72},{80,88},{96,104},{112,120},{... | collective-permute-start | bytes 196616 | tf_op jit(solution)/shard_map/ppermute | solution.py:520
  35.8 4.0 %collective-permute-start.7 = (f32[128,128]{1,0:T(8,128)S(1)}, f32[128,128]{1,0:T(8,128)S(1)}, u32[]{:S(2)}, u32[]{:S(2)}) collective-permute-start(f32[128,128]{1,0:T(8,128)S(1)} %get-tuple-element.39._sent_core_ref), channel_id=1, source_target_pairs={{0,1},{2,3},{4,5},{6,7},{8,9},{10,11},{12,13},{14,15},{16,17},{18,... | collective-permute-start | bytes 196616 | tf_op jit(solution)/shard_map/ppermute | solution.py:520
  53.3 15.2 %collective-permute-start.8 = (f32[1,1,128]{2,1,0:T(1,128)S(1)}, f32[1,1,128]{2,1,0:T(1,128)S(1)}, u32[]{:S(2)}, u32[]{:S(2)}) collective-permute-start(f32[1,1,128]{2,1,0:T(1,128)S(1)} %bitcast.9), channel_id=1, source_target_pairs={{0,0},{1,33},{2,66},{3,99},{4,132},{5,165},{6,198},{7,231},{8,264}... | collective-permute-start | bytes 1544 | tf_op jit(solution)/shard_map/ppermute | solution.py:539
  69.1 23.6 %all-to-all-start.1 = ((f32[32,1,128]{2,1,0:T(1,128)}), f32[32,1,128]{2,1,0:T(1,128)S(1)}, u32[]{:S(2)}, u32[]{:S(2)}) async-start(f32[32,1,128]{2,1,0:T(1,128)} %broadcast_in_dim.12), calls=%async_computation.1 | async-start | bytes 32768 | tf_op jit(solution)/shard_map/all_to_all | solution.py:540

commit v7 on v6

--- a/solution.py
+++ b/solution.py
@@ -255,19 +255,18 @@
     return joined(*face_traces(trace_ref, field))
 
 
-def swaps(low, high, send_coarse, send_fine, dom_odd_ref, rim_chip_ref, dom_even_ref, rim_core_ref):
-    first_core = lax.axis_index("core") == 0
+def swaps(low, high, send_coarse, send_fine, dom_odd_ref, rim_ref, dom_even_ref):
     even_dom = lax.axis_index("x") % 2 == 0
-    rim_core_ref[...] = jnp.where(first_core, high, low)
-    rim_chip_ref[...] = jnp.where(first_core, low, high)
+    lane = lax.broadcasted_iota(jnp.int32, low.shape, 1)
+    rim_ref[...] = jnp.where(lane < RIM, low, high)
     dom_even_ref[...] = jnp.where(even_dom, send_coarse, send_fine)
     dom_odd_ref[...] = jnp.where(even_dom, send_fine, send_coarse)
 
 
 def first_kernel(*refs):
     field_in, level_in, id_in, values_in, pairs_in, coarse_in, fine_in, table_in = refs[:8]
-    outs, codes = refs[8:12], refs[12]
-    source, levels, ids, values, pairs, coarse, fine, table, field, hot, sems = refs[13:]
+    outs, codes = refs[8:11], refs[11]
+    source, levels, ids, values, pairs, coarse, fine, table, field, hot, sems = refs[12:]
     moves = [
         (coarse_in, coarse),
         (fine_in, fine),
@@ -421,12 +420,12 @@
 
 def image_kernel(*refs):
     codes, table = refs[0], views(refs[1])
-    image, counts = add_faces(*refs[:11], *refs[17:])
+    image, counts = add_faces(*refs[:11], *refs[16:])
     refs[11][...] = image
     traces = stacked_traces(table["trace"], image)
-    send_coarse, send_fine = gather_hanging(traces, refs[17], codes, table["up"])
-    swaps(image[:, 0:SIDE], image[:, CELLS - SIDE :], send_coarse, send_fine, *refs[12:16])
-    refs[16][...] = counts
+    send_coarse, send_fine = gather_hanging(traces, refs[16], codes, table["up"])
+    swaps(image[:, 0:SIDE], image[:, CELLS - SIDE :], send_coarse, send_fine, *refs[12:15])
+    refs[15][...] = counts
 
 
 def second_kernel(*refs):
@@ -450,9 +449,8 @@
     dom_even_ref,
     rim_core_ref,
     sent_odd_ref,
-    _sent_chip_ref,
+    _sent_rim_ref,
     sent_even_ref,
-    _sent_core_ref,
     first_ref,
     counts_ref,
     source_ref,
@@ -520,11 +518,11 @@
     return lax.ppermute(value, axes, pairs + [(above, below) for below, above in pairs])
 
 
-def exchange(dom_odd, rim_chip, dom_even, rim_core):
-    rim_chip = swapped(rim_chip, BLOCK, 1)
+def exchange(dom_odd, rim, dom_even):
+    rim_chip = swapped(rim, BLOCK, 1)
     dom_odd = swapped(dom_odd, DOM, 1)
     dom_even = swapped(dom_even, DOM, 0)
-    rim_core = swapped(rim_core, BLOCK, 0)
+    rim_core = swapped(rim, BLOCK, 0)
     return dom_odd, rim_chip, dom_even, rim_core
 
 
@@ -543,7 +541,7 @@
 def on_device(source, levels, ids, values, pairs, coarse, fine):
     levels, ids, values, coarse = (a.reshape(1, -1) for a in (levels, ids, values, coarse))
     table = jnp.asarray(packed_table())
-    sends = [(FACE, CELLS), (128, SIDE), (FACE, CELLS), (128, SIDE)]
+    sends = [(FACE, CELLS), (128, SIDE), (FACE, CELLS)]
     params = (source, levels, ids, values, pairs, coarse, fine)
     *swapping, codes = call(
         first_kernel,

time: 94.1 us -> 101 us (1.073)
  waiting for transfers between devices: 17.8 us -> 21.7 us
  starting transfers between devices: 48.3 us -> 50.9 us
    ppermute x8, waiting for transfers between devices: 0.08 us -> 5.02 us  [swapped(): lax.ppermute(value, axes, pairs + [(above, below) for below, above in pai...]
    ppermute x8, starting transfers between devices: 29.4 us -> 32.5 us  [swapped(): lax.ppermute(value, axes, pairs + [(above, below) for below, above in pai...]
    ppermute x1, waiting for transfers between devices: 13 us -> 12 us  [summed_over_blocks(): other = lax.ppermute(jnp.sum(sums, axis=0, keepdims=True), BLOCK, diagonal)]
  transfers between devices with their start and end apart: 10 -> 10, of which waited for: 3 -> 4; matrix products, arithmetic and copies ran while one was open for 0% -> 0% of each run, Pallas kernels for 5% -> 5%
where the time goes in v7:
time: 101 us; the launch traced here: 100 us
  starting transfers between devices  50.9 us (50%)
  waiting for transfers between devices  21.7 us (21%)
  Pallas kernels  13.3 us (13%)
  blocking collectives  12.9 us (13%)
    ppermute x8, starting transfers between devices, swapped(): lax.ppermute(value, axes, pairs + [(above, below) for below, above in pai...  32.5 us
    all_to_all x1, starting transfers between devices, summed_over_blocks(): lax.all_to_all(jnp.broadcast_to(other, sums.shape), PLANE, 0, 0, tiled=True)  16.5 us
    pallas_call x7, Pallas kernels, call(): pl.pallas_call(kernel, out_shape=[jax.ShapeDtypeStruct(shape, F32) for sh...  13.3 us
    all_to_all x1, blocking collectives, summed_over_blocks(): sums = lax.all_to_all(sums, PLANE, 0, 0, tiled=True)  12.9 us
    ppermute x1, waiting for transfers between devices, summed_over_blocks(): other = lax.ppermute(jnp.sum(sums, axis=0, keepdims=True), BLOCK, diagonal)  12 us
    ppermute x8, waiting for transfers between devices, swapped(): lax.ppermute(value, axes, pairs + [(above, below) for below, above in pai...  5.02 us
    all_to_all x1, waiting for transfers between devices, summed_over_blocks(): lax.all_to_all(jnp.broadcast_to(other, sums.shape), PLANE, 0, 0, tiled=True)  4.7 us
  transfers between devices with their start and end apart: 10, of which 4 were waited for; matrix products, arithmetic and copies ran while one was open for 0% of the time, Pallas kernels for 5%

profile of v7, /device:TPU:1, one launch (start us, length us, event | category | flops | bytes accessed | tf_op | source)
XLA Modules:
  0.0 100.4 jit_solution(17278856353151426858)
XLA Ops:
  0.7 3.5 %first.1 = (f32[32,512]{1,0:T(8,128)}, f32[128,128]{1,0:T(8,128)}, f32[32,512]{1,0:T(8,128)}, f32[16,1024]{1,0:T(8,128)}) custom-call(f32[125,512]{1,0:T(8,128)} %source_ref.3, s32[1,512]{1,0:T(1,128)} %bitcast.6, s32[1,512]{1,0:T(1,128)} %bitcast.7, f32[1,64]{1,0:T(1,128)} %bitcast.11, s32[2,960]{1,0:T(2,128)} %pairs_ref.3, s32[1,512]{1,0:T(1,128)} %bitcast.8, ...), custom_call_target="tpu_custom_call" | custom-call | tf_op jit(solution)/shard_map/first/pallas_call | solution.py:498
  4.2 0.7 collective-permute-start
  4.9 6.4 %collective-permute-start.2 = (f32[32,512]{1,0:T(8,128)}, f32[32,512]{1,0:T(8,128)S(1)}, u32[]{:S(2)}, u32[]{:S(2)}) collective-permute-start(f32[32,512]{1,0:T(8,128)} %get-tuple-element.27), channel_id=1, source_target_pairs={{0,8},{16,24},{32,40},{48,56},{64,72},{80,88},{96,104},{112,120},{... | collective-permute-start | bytes 196616 | tf_op jit(solution)/shard_map/ppermute | solution.py:518
  11.3 11.7 %collective-permute-start.3 = (f32[128,128]{1,0:T(8,128)}, f32[128,128]{1,0:T(8,128)S(1)}, u32[]{:S(2)}, u32[]{:S(2)}) collective-permute-start(f32[128,128]{1,0:T(8,128)} %get-tuple-element.26), channel_id=1, source_target_pairs={{0,1},{2,3},{4,5},{6,7},{8,9},{10,11},{12,13},{14,15},{16,17},{18,... | collective-permute-start | bytes 196616 | tf_op jit(solution)/shard_map/ppermute | solution.py:518
  23.0 1.9 %collective-permute-start.1 = (f32[128,128]{1,0:T(8,128)}, f32[128,128]{1,0:T(8,128)S(1)}, u32[]{:S(2)}, u32[]{:S(2)}) collective-permute-start(f32[128,128]{1,0:T(8,128)} %get-tuple-element.26), channel_id=1, source_target_pairs={{1,2},{3,4},{5,6},{7,8},{9,10},{11,12},{13,14},{15,16},{17,18},{19... | collective-permute-start | bytes 196616 | tf_op jit(solution)/shard_map/ppermute | solution.py:518
  25.0 1.0 middle.2
  26.0 2.8 %collective-permute-done.1.refs_8_ = f32[128,128]{1,0:T(8,128)S(1)} collective-permute-done((f32[128,128]{1,0:T(8,128)}, f32[128,128]{1,0:T(8,128)S(1)}, u32[]{:S(2)}, u32[]{:S(2)}) %collective-permute-start.1) | collective-permute-done | bytes 65568 | tf_op jit(solution)/shard_map/ppermute | solution.py:518
  28.8 3.5 %image.1 = (f32[128,512]{1,0:T(8,128)S(1)}, f32[32,512]{1,0:T(8,128)S(1)}, f32[128,128]{1,0:T(8,128)S(1)}, f32[32,512]{1,0:T(8,128)S(1)}, f32[16,512]{1,0:T(8,128)S(1)}) custom-call(f32[16,1024]{1,0:T(8,128)S(1)} %copy-done.2, bf16[1024,256]{1,0:T(8,128)(2,1)S(1)} %copy-done, f32[125,512]{1,0:T(8,128)S(1)} %copy-done.1, ...), custom_call_target="tpu_custom_call" | custom-call | tf_op jit(solution)/shard_map/image/pallas_call | solution.py:498
  32.3 0.7 collective-permute-start.4
  33.0 4.9 %collective-permute-start.6 = (f32[32,512]{1,0:T(8,128)S(1)}, f32[32,512]{1,0:T(8,128)S(1)}, u32[]{:S(2)}, u32[]{:S(2)}) collective-permute-start(f32[32,512]{1,0:T(8,128)S(1)} %get-tuple-element.35.sent_even_ref), channel_id=1, source_target_pairs={{0,8},{16,24},{32,40},{48,56},{64,72},{80,88},{96,104},{112,120},{... | collective-permute-start | bytes 196616 | tf_op jit(solution)/shard_map/ppermute | solution.py:518
  37.9 4.3 %collective-permute-start.7 = (f32[128,128]{1,0:T(8,128)S(1)}, f32[128,128]{1,0:T(8,128)S(1)}, u32[]{:S(2)}, u32[]{:S(2)}) collective-permute-start(f32[128,128]{1,0:T(8,128)S(1)} %get-tuple-element.34._sent_rim_ref), channel_id=1, source_target_pairs={{0,1},{2,3},{4,5},{6,7},{8,9},{10,11},{12,13},{14,15},{16,17},{18,... | collective-permute-start | bytes 196616 | tf_op jit(solution)/shard_map/ppermute | solution.py:518
  42.2 1.9 %collective-permute-start.5 = (f32[128,128]{1,0:T(8,128)S(1)}, f32[128,128]{1,0:T(8,128)S(1)}, u32[]{:S(2)}, u32[]{:S(2)}) collective-permute-start(f32[128,128]{1,0:T(8,128)S(1)} %get-tuple-element.34._sent_rim_ref), channel_id=1, source_target_pairs={{1,2},{3,4},{5,6},{7,8},{9,10},{11,12},{13,14},{15,16},{17,18},{19... | collective-permute-start | bytes 196616 | tf_op jit(solution)/shard_map/ppermute | solution.py:518
  44.1 1.5 %middle.3 = (f32[128,512]{1,0:T(8,128)S(1)}, f32[160,512]{1,0:T(8,128)S(1)}, f32[160,512]{1,0:T(8,128)S(1)}, f32[32,1024]{1,0:T(8,128)S(1)}, f32[32,1024]{1,0:T(8,128)S(1)}) custom-call(f32[128,512]{1,0:T(8,128)S(1)} %get-tuple-element.28.field_ref.image_ref.refs_2_, s32[2,960]{1,0:T(2,128)S(1)} %copy-done.3, bf16[1024,256]{1,0:T(8,128)(2,1)S(1)} %copy-done), custom_call_target="tpu_custom_call" | custom-call | tf_op jit(solution)/shard_map/middle/pallas_call | solution.py:498
  45.6 2.2 %collective-permute-done.5.rim_chip_ref.refs_8_ = f32[128,128]{1,0:T(8,128)S(1)} collective-permute-done((f32[128,128]{1,0:T(8,128)S(1)}, f32[128,128]{1,0:T(8,128)S(1)}, u32[]{:S(2)}, u32[]{:S(2)}) %collective-permute-start.5) | collective-permute-done | bytes 65568 | tf_op jit(solution)/shard_map/ppermute | solution.py:518
  47.8 0.7 moments.1
  48.5 12.9 %all_to_all.10 = f32[32,1,128]{2,1,0:T(1,128)S(1)} all-to-all(f32[32,1,128]{2,1,0:T(1,128)S(1)} %moments.1), channel_id=1, replica_groups=mesh['z'=32,'x'=4,'y'=4,'core'=2] {'x','y','core'}, dimensions={0} | all-to-all | bytes 32768 | tf_op jit(solution)/shard_map/all_to_all | solution.py:531
  61.4 0.1 reduce_sum.9
  61.5 1.9 %collective-permute-start.8 = (f32[1,1,128]{2,1,0:T(1,128)S(1)}, f32[1,1,128]{2,1,0:T(1,128)S(1)}, u32[]{:S(2)}, u32[]{:S(2)}) collective-permute-start(f32[1,1,128]{2,1,0:T(1,128)S(1)} %bitcast.9), channel_id=1, source_target_pairs={{0,0},{1,33},{2,66},{3,99},{4,132},{5,165},{6,198},{7,231},{8,264}... | collective-permute-start | bytes 1544 | tf_op jit(solution)/shard_map/ppermute | solution.py:537
  63.4 12.0 %collective-permute-done.8 = f32[1,1,128]{2,1,0:T(1,128)S(1)} collective-permute-done((f32[1,1,128]{2,1,0:T(1,128)S(1)}, f32[1,1,128]{2,1,0:T(1,128)S(1)}, u32[]{:S(2)}, u32[]{:S(2)}) %collective-permute-start.8) | collective-permute-done | bytes 544 | tf_op jit(solution)/shard_map/ppermute | solution.py:537
  75.4 0.6 broadcast_in_dim.12
  76.0 16.5 %all-to-all-start.1 = ((f32[32,1,128]{2,1,0:T(1,128)}), f32[32,1,128]{2,1,0:T(1,128)S(1)}, u32[]{:S(2)}, u32[]{:S(2)}) async-start(f32[32,1,128]{2,1,0:T(1,128)} %broadcast_in_dim.12), calls=%async_computation.1 | async-start | bytes 32768 | tf_op jit(solution)/shard_map/all_to_all | solution.py:538
  92.5 2.2 %second.1.second_ref = f32[128,512]{1,0:T(8,128)S(1)} custom-call(f32[16,1024]{1,0:T(8,128)S(1)} %copy-done.2, bf16[1024,256]{1,0:T(8,128)(2,1)S(1)} %copy-done, f32[128,512]{1,0:T(8,128)S(1)} %get-tuple-element.28.field_ref.image_ref.refs_2_, f32[128,512]{1,0:T(8,128)S(1)} %get-tuple-element.29.stiff_ref.refs_3_, ...), custom_call_target="tpu_custom_call" | custom-call | tf_op jit(solution)/shard_map/second/pallas_call | solution.py:498
  94.7 4.7 %all-to-all-done.1.sums_ref = f32[32,1,128]{2,1,0:T(1,128)S(1)} async-done(((f32[32,1,128]{2,1,0:T(1,128)}), f32[32,1,128]{2,1,0:T(1,128)S(1)}, u32[]{:S(2)}, u32[]{:S(2)}) %all-to-all-start.1) | async-done | bytes 16416 | tf_op jit(solution)/shard_map/all_to_all | solution.py:538
  99.4 1.0 %last.1 = (f32[125,512]{1,0:T(8,128)}, f32[125,512]{1,0:T(8,128)}) custom-call(f32[32,1,128]{2,1,0:T(1,128)S(1)} %all-to-all-done.1.sums_ref, f32[125,512]{1,0:T(8,128)S(1)} %copy-done.1, f32[128,512]{1,0:T(8,128)S(1)} %get-tuple-element.28.field_ref.image_ref.refs_2_, f32[128,512]{1,0:T(8,128)S(1)} %second.1.second_ref), custom_call_target="tpu_custom_call" | custom-call | tf_op jit(solution)/shard_map/last/pallas_call | solution.py:498
  (14 shorter events, 0.0 us)
Async XLA Ops:
  0.6 24.3 %copy-start = (bf16[1024,256]{1,0:T(8,128)(2,1)S(1)}, bf16[1024,256]{1,0:T(8,128)(2,1)}, u32[]{:S(2)}) copy-start(bf16[1024,256]{1,0:T(8,128)(2,1)} %constant.4.clone.refs_7_.table_ref.refs_1_) | copy-start | bytes 1572868
  0.6 24.3 %copy-start.1 = (f32[125,512]{1,0:T(8,128)S(1)}, f32[125,512]{1,0:T(8,128)}, u32[]{:S(2)}) copy-start(f32[125,512]{1,0:T(8,128)} %source_ref.3) | copy-start | bytes 768004
  0.7 24.3 %copy-start.3 = (s32[2,960]{1,0:T(2,128)S(1)}, s32[2,960]{1,0:T(2,128)}, u32[]{:S(2)}) copy-start(s32[2,960]{1,0:T(2,128)} %pairs_ref.3) | copy-start | bytes 23044
  4.2 21.7 %collective-permute-start = (f32[32,512]{1,0:T(8,128)}, f32[32,512]{1,0:T(8,128)S(1)}, u32[]{:S(2)}, u32[]{:S(2)}) collective-permute-start(f32[32,512]{1,0:T(8,128)} %get-tuple-element.25), channel_id=1, source_target_pairs={{8,16},{24,32},{40,48},{56,64},{72,80},{88,96},{104,112},{120,128}... | collective-permute-start | bytes 196616 | tf_op jit(solution)/shard_map/ppermute | solution.py:518
  4.9 21.1 %collective-permute-start.2 = (f32[32,512]{1,0:T(8,128)}, f32[32,512]{1,0:T(8,128)S(1)}, u32[]{:S(2)}, u32[]{:S(2)}) collective-permute-start(f32[32,512]{1,0:T(8,128)} %get-tuple-element.27), channel_id=1, source_target_pairs={{0,8},{16,24},{32,40},{48,56},{64,72},{80,88},{96,104},{112,120},{... | collective-permute-start | bytes 196616 | tf_op jit(solution)/shard_map/ppermute | solution.py:518
  11.3 17.5 %copy-start.2 = (f32[16,1024]{1,0:T(8,128)S(1)}, f32[16,1024]{1,0:T(8,128)}, u32[]{:S(2)}) copy-start(f32[16,1024]{1,0:T(8,128)} %get-tuple-element.20.refs_0_.codes) | copy-start | bytes 196612
  11.3 14.7 %collective-permute-start.3 = (f32[128,128]{1,0:T(8,128)}, f32[128,128]{1,0:T(8,128)S(1)}, u32[]{:S(2)}, u32[]{:S(2)}) collective-permute-start(f32[128,128]{1,0:T(8,128)} %get-tuple-element.26), channel_id=1, source_target_pairs={{0,1},{2,3},{4,5},{6,7},{8,9},{10,11},{12,13},{14,15},{16,17},{18,... | collective-permute-start | bytes 196616 | tf_op jit(solution)/shard_map/ppermute | solution.py:518
  23.0 5.8 %collective-permute-start.1 = (f32[128,128]{1,0:T(8,128)}, f32[128,128]{1,0:T(8,128)S(1)}, u32[]{:S(2)}, u32[]{:S(2)}) collective-permute-start(f32[128,128]{1,0:T(8,128)} %get-tuple-element.26), channel_id=1, source_target_pairs={{1,2},{3,4},{5,6},{7,8},{9,10},{11,12},{13,14},{15,16},{17,18},{19... | collective-permute-start | bytes 196616 | tf_op jit(solution)/shard_map/ppermute | solution.py:518
  32.3 13.3 %collective-permute-start.4 = (f32[32,512]{1,0:T(8,128)S(1)}, f32[32,512]{1,0:T(8,128)S(1)}, u32[]{:S(2)}, u32[]{:S(2)}) collective-permute-start(f32[32,512]{1,0:T(8,128)S(1)} %get-tuple-element.33.sent_odd_ref), channel_id=1, source_target_pairs={{8,16},{24,32},{40,48},{56,64},{72,80},{88,96},{104,112},{120,128}... | collective-permute-start | bytes 196616 | tf_op jit(solution)/shard_map/ppermute | solution.py:518
  33.0 12.6 %collective-permute-start.6 = (f32[32,512]{1,0:T(8,128)S(1)}, f32[32,512]{1,0:T(8,128)S(1)}, u32[]{:S(2)}, u32[]{:S(2)}) collective-permute-start(f32[32,512]{1,0:T(8,128)S(1)} %get-tuple-element.35.sent_even_ref), channel_id=1, source_target_pairs={{0,8},{16,24},{32,40},{48,56},{64,72},{80,88},{96,104},{112,120},{... | collective-permute-start | bytes 196616 | tf_op jit(solution)/shard_map/ppermute | solution.py:518
  37.9 7.7 %collective-permute-start.7 = (f32[128,128]{1,0:T(8,128)S(1)}, f32[128,128]{1,0:T(8,128)S(1)}, u32[]{:S(2)}, u32[]{:S(2)}) collective-permute-start(f32[128,128]{1,0:T(8,128)S(1)} %get-tuple-element.34._sent_rim_ref), channel_id=1, source_target_pairs={{0,1},{2,3},{4,5},{6,7},{8,9},{10,11},{12,13},{14,15},{16,17},{18,... | collective-permute-start | bytes 196616 | tf_op jit(solution)/shard_map/ppermute | solution.py:518
  42.2 5.6 %collective-permute-start.5 = (f32[128,128]{1,0:T(8,128)S(1)}, f32[128,128]{1,0:T(8,128)S(1)}, u32[]{:S(2)}, u32[]{:S(2)}) collective-permute-start(f32[128,128]{1,0:T(8,128)S(1)} %get-tuple-element.34._sent_rim_ref), channel_id=1, source_target_pairs={{1,2},{3,4},{5,6},{7,8},{9,10},{11,12},{13,14},{15,16},{17,18},{19... | collective-permute-start | bytes 196616 | tf_op jit(solution)/shard_map/ppermute | solution.py:518
  61.5 13.9 %collective-permute-start.8 = (f32[1,1,128]{2,1,0:T(1,128)S(1)}, f32[1,1,128]{2,1,0:T(1,128)S(1)}, u32[]{:S(2)}, u32[]{:S(2)}) collective-permute-start(f32[1,1,128]{2,1,0:T(1,128)S(1)} %bitcast.9), channel_id=1, source_target_pairs={{0,0},{1,33},{2,66},{3,99},{4,132},{5,165},{6,198},{7,231},{8,264}... | collective-permute-start | bytes 1544 | tf_op jit(solution)/shard_map/ppermute | solution.py:537
  76.0 23.4 %all-to-all-start.1 = ((f32[32,1,128]{2,1,0:T(1,128)}), f32[32,1,128]{2,1,0:T(1,128)S(1)}, u32[]{:S(2)}, u32[]{:S(2)}) async-start(f32[32,1,128]{2,1,0:T(1,128)} %broadcast_in_dim.12), calls=%async_computation.1 | async-start | bytes 32768 | tf_op jit(solution)/shard_map/all_to_all | solution.py:538
